TPU v7x, 32 devices: a whole 2x2x4 slice. The times are simulated.
32 devices in a mesh: seq: 16 (over z, y, core), tp: 2 (over x).
Axes of the slice: x: 2, y: 2, z: 4, core: 2. Of those that a mesh axis runs over, the one named last changes fastest.
Arguments:
- grad_out: bfloat16 [4096, 14336], P('seq', 'tp'), may hold values from -6 to 6
- weight: bfloat16 [4096, 14336], P('seq', 'tp'), may hold values from -0.046875 to 0.046875
- saved: bfloat16 [4096, 512], P('seq'), may hold values from -0.125 to 0.125
- first_moment: float32 [512, 14336], P('seq', 'tp'), may hold values from -6 to 6
- second_moment: float32 [512, 14336], P('seq', 'tp'), may hold values from 0.05 to 2
- basis: bfloat16 [4096, 512], P('seq'), may hold values from -0.0625 to 0.0625
- new_basis: bfloat16 [4096, 512], P('seq'), may hold values from -0.09375 to 0.09375
Outputs:
- grad_input: float32 [4096, 4096], P('seq', 'tp')
- first_new: float32 [512, 14336], P('seq', 'tp')
- second_new: float32 [512, 14336], P('seq', 'tp')
- update: float32 [512, 14336], P('seq', 'tp')
All inputs are finite; a program needn't handle non-finite values.
Results may differ from a plain program's by a relative error of at most 0.0003.
Values may be sent and summed in bfloat16 or wider, within the bound.
No kernel may reach another device: no remote copies, remote signals or barrier semaphores. Data moves between devices by JAX's collectives and lax.ppermute only.
A program may use at most 192 MiB of HBM per device.

v0:
```python
import jax
import jax.numpy as jnp
from jax import lax
from jax.sharding import PartitionSpec as P


def contract_rows(left, right):
    return lax.dot_general(
        left, right, (((0,), (0,)), ((), ())), preferred_element_type=jnp.float32
    )


def exact_dot(left, right):
    return jnp.dot(left, right, precision=lax.Precision.HIGHEST, preferred_element_type=jnp.float32)


def per_device(grad_out, weight, saved, first_moment, second_moment, basis, new_basis):
    partial_input = lax.dot_general(
        grad_out,
        lax.all_gather(weight, "seq", axis=0, tiled=True),
        (((1,), (1,)), ((), ())),
        preferred_element_type=jnp.float32,
    )
    grad_input = lax.psum_scatter(partial_input, "tp", scatter_dimension=1, tiled=True)
    local_intersection = contract_rows(new_basis, basis)
    gradient = lax.psum_scatter(
        contract_rows(saved, grad_out), "seq", scatter_dimension=0, tiled=True
    )
    full_first, full_second = (
        lax.all_gather(first_moment, "seq", axis=0, tiled=True),
        lax.all_gather(second_moment, "seq", axis=0, tiled=True),
    )
    own_rows = lax.psum_scatter(local_intersection, "seq", scatter_dimension=0, tiled=True)
    first_rot = exact_dot(own_rows, full_first)
    second_rot = exact_dot(own_rows * own_rows, full_second)
    first_new = 0.9 * first_rot + 0.1 * gradient
    second_new = 0.95 * second_rot + 0.05 * gradient * gradient
    update = first_new / (jnp.sqrt(second_new) + 1e-08)
    return (grad_input, first_new, second_new, update)


def solution(mesh):
    return jax.shard_map(
        per_device,
        mesh=mesh,
        in_specs=(
            P("seq", "tp"),
            P("seq", "tp"),
            P("seq", None),
            P("seq", "tp"),
            P("seq", "tp"),
            P("seq", None),
            P("seq", None),
        ),
        out_specs=(P("seq", "tp"), P("seq", "tp"), P("seq", "tp"), P("seq", "tp")),
        check_vma=False,
    )
```

profile of v0, /device:TPU:0, one launch (start us, length us, event | category | flops | bytes accessed | tf_op | source)
XLA Modules:
  0.0 805.3 jit_solution(60620895233310129)
XLA Ops:
  7.2 0.0 copy-start
  7.2 0.0 all-gather.4.cloned.1.call-start
  7.2 0.7 all-gather.4.cloned.1.call-update
  7.9 0.0 reduce-scatter.6.cloned.1.call-start
  8.0 2.3 fusion.4
  10.3 0.0 reduce-scatter.6.cloned.1.call-update
  10.3 0.0 reduce-scatter.8.cloned.1.call-start
  10.4 0.0 copy-done
  10.4 10.3 %fusion.5 = f32[512,7168]{1,0:T(8,128)} fusion(bf16[256,512]{1,0:T(8,128)(2,1)S(1)} %copy-done, bf16[256,7168]{1,0:T(8,128)(2,1)} %param.7), kind=kOutput, calls=%fused_computation.9 | convolution fusion | flops 1879048192 | bytes 18612224 | tf_op jit(solution)/shard_map/dot_general | solution.py:8
  20.7 0.0 reduce-scatter.8.cloned.1.call-update
  20.7 0.0 all-gather.8.cloned.1.call-start
  20.8 0.5 all-gather.8.cloned.1.call-update
  21.3 0.0 all-gather.6.cloned.1.call-start
  21.4 0.5 all-gather.6.cloned.1.call-update
  21.9 0.2 reduce-scatter.4.cloned.1.call-start
  22.1 276.8 %all-gather.4.cloned.1.call-done = bf16[4096,7168]{1,0:T(8,128)(2,1)} async-done(((bf16[256,7168]{1,0:T(8,128)(2,1)}), bf16[4096,7168]{1,0:T(8,128)(2,1)}) %all-gather.4.cloned.1.call-update) | async-done | bytes 58720272 | tf_op jit(solution)/shard_map/all_gather | solution.py:20
  298.9 26.5 %fusion.3 = f32[256,4096]{1,0:T(8,128)} fusion(bf16[256,7168]{1,0:T(8,128)(2,1)} %param.7, bf16[4096,7168]{1,0:T(8,128)(2,1)} %all-gather.4.cloned.1.call-done), kind=kOutput, calls=%fused_computation.7 | convolution fusion | flops 15032385536 | bytes 66584576 | tf_op jit(solution)/shard_map/dot_general | solution.py:18
  325.5 0.0 reduce-scatter.4.cloned.1.call-update
  325.5 0.0 copy-start.1
  325.5 34.5 %reduce-scatter.6.cloned.1.call-done = f32[32,512]{1,0:T(8,128)} async-done(((f32[512,512]{1,0:T(8,128)}), f32[32,512]{1,0:T(8,128)}) %reduce-scatter.6.cloned.1.call-update) | async-done | bytes 65552 | tf_op jit(solution)/shard_map/reduce_scatter | solution.py:33
  360.0 0.0 copy-start.4
  360.0 153.2 %reduce-scatter.8.cloned.1.call-done = f32[32,7168]{1,0:T(8,128)} async-done(((f32[512,7168]{1,0:T(8,128)}), f32[32,7168]{1,0:T(8,128)}) %reduce-scatter.8.cloned.1.call-update) | async-done | bytes 917520 | tf_op jit(solution)/shard_map/reduce_scatter | solution.py:26
  513.2 0.0 copy-start.2
  513.2 115.4 %all-gather.8.cloned.1.call-done = f32[512,7168]{1,0:T(8,128)} async-done(((f32[32,7168]{1,0:T(8,128)}), f32[512,7168]{1,0:T(8,128)}) %all-gather.8.cloned.1.call-update) | async-done | bytes 14680080 | tf_op jit(solution)/shard_map/all_gather | solution.py:31
  628.6 11.7 %fusion.1 = f32[32,7168]{1,0:T(8,128)S(1)} fusion(f32[512,7168]{1,0:T(8,128)} %all-gather.8.cloned.1.call-done, f32[32,7168]{1,0:T(8,128)} %reduce-scatter.8.cloned.1.call-done, f32[32,512]{1,0:T(8,128)} %reduce-scatter.6.cloned.1.call-done), kind=kOutput, calls=%fused_computation.3 | convolution fusion | flops 1410220032 | bytes 16580608 | tf_op jit(solution)/shard_map/dot_general | solution.py:14
  640.4 0.0 copy-start.3
  640.4 102.7 %all-gather.6.cloned.1.call-done = f32[512,7168]{1,0:T(8,128)} async-done(((f32[32,7168]{1,0:T(8,128)}), f32[512,7168]{1,0:T(8,128)}) %all-gather.6.cloned.1.call-update) | async-done | bytes 14680080 | tf_op jit(solution)/shard_map/all_gather | solution.py:30
  743.1 0.0 copy-done.4
  743.1 0.0 copy-done.2
  743.1 13.2 %add_divide_fusion = (f32[32,7168]{1,0:T(8,128)}, f32[32,7168]{1,0:T(8,128)}) fusion(f32[32,7168]{1,0:T(8,128)S(1)} %fusion.1, f32[32,7168]{1,0:T(8,128)S(1)} %copy-done.2, f32[32,512]{1,0:T(8,128)S(1)} %copy-done.4, f32[512,7168]{1,0:T(8,128)} %all-gather.6.cloned.1.call-done), kind=kOutput, calls=%fused_computation.5 | convolution fusion | flops 1410433024 | bytes 18415616 | tf_op jit(solution)/shard_map/dot_general | solution.py:14
  756.3 42.1 %reduce-scatter.4.cloned.1.call-done = f32[256,2048]{1,0:T(8,128)} async-done(((f32[256,4096]{1,0:T(8,128)}), f32[256,2048]{1,0:T(8,128)}) %reduce-scatter.4.cloned.1.call-update) | async-done | bytes 2097168 | tf_op jit(solution)/shard_map/reduce_scatter | solution.py:24
  798.4 0.0 copy-done.3
  798.4 0.0 copy-done.1
Async XLA Ops:
  7.2 3.2 copy-start
  7.2 291.8 %all-gather.4.cloned.1.call-start = ((), (), s32[]{:S(2)}) async-start(), calls=%async_computation.3 | async-start | bytes 62390272 | tf_op jit(solution)/shard_map/all_gather | solution.py:20
  7.9 352.1 %reduce-scatter.6.cloned.1.call-start = ((), (), s32[]{:S(2)}) async-start(), calls=%async_computation.5 | async-start | bytes 1114112 | tf_op jit(solution)/shard_map/reduce_scatter | solution.py:33
  10.3 502.9 %reduce-scatter.8.cloned.1.call-start = ((), (), s32[]{:S(2)}) async-start(), calls=%async_computation.7 | async-start | bytes 15597568 | tf_op jit(solution)/shard_map/reduce_scatter | solution.py:26
  20.7 607.9 %all-gather.8.cloned.1.call-start = ((), (), s32[]{:S(2)}) async-start(), calls=%async_computation.8 | async-start | bytes 15597568 | tf_op jit(solution)/shard_map/all_gather | solution.py:31
  21.3 721.8 %all-gather.6.cloned.1.call-start = ((), (), s32[]{:S(2)}) async-start(), calls=%async_computation.6 | async-start | bytes 15597568 | tf_op jit(solution)/shard_map/all_gather | solution.py:30
  21.9 776.5 %reduce-scatter.4.cloned.1.call-start = ((), (), s32[]{:S(2)}) async-start(), calls=%async_computation.4 | async-start | bytes 6291456 | tf_op jit(solution)/shard_map/reduce_scatter | solution.py:24
  325.5 472.9 %copy-start.1 = (bf16[256,512]{1,0:T(8,128)(2,1)S(1)}, bf16[256,512]{1,0:T(8,128)(2,1)}, u32[]{:S(2)}) copy-start(bf16[256,512]{1,0:T(8,128)(2,1)} %param.9) | copy-start | bytes 786436
  360.0 383.1 %copy-start.4 = (f32[32,512]{1,0:T(8,128)S(1)}, f32[32,512]{1,0:T(8,128)}, u32[]{:S(2)}) copy-start(f32[32,512]{1,0:T(8,128)} %reduce-scatter.6.cloned.1.call-done) | copy-start | bytes 196612
  513.2 229.9 %copy-start.2 = (f32[32,7168]{1,0:T(8,128)S(1)}, f32[32,7168]{1,0:T(8,128)}, u32[]{:S(2)}) copy-start(f32[32,7168]{1,0:T(8,128)} %reduce-scatter.8.cloned.1.call-done) | copy-start | bytes 2752516
  640.4 158.0 %copy-start.3 = (f32[32,7168]{1,0:T(8,128)}, f32[32,7168]{1,0:T(8,128)S(1)}, u32[]{:S(2)}) copy-start(f32[32,7168]{1,0:T(8,128)S(1)} %fusion.1) | copy-start | bytes 2752516
Sparse Core Ops, SparseCore 0:
  9.6 289.2 all-gather.3
  302.6 57.3 reduce-scatter.5
  364.6 148.5 reduce-scatter.7
  515.6 112.9 all-gather.7
  631.0 112.0 all-gather.5
  745.9 52.4 reduce-scatter.3
where the time goes:
time: 805 us
  waiting for transfers between devices  726 us (90%)
  matrix products  64.2 us (8%)
  between operations  14.2 us (2%)
    all_gather x1, waiting for transfers between devices, per_device(): lax.all_gather(weight, 'seq', axis=0, tiled=True)  277 us
    reduce_scatter x1, waiting for transfers between devices, per_device(): lax.psum_scatter(contract_rows(saved, grad_out), 'seq', scatter_dimension...  153 us
    all_gather x1, waiting for transfers between devices, per_device(): lax.all_gather(second_moment, 'seq', axis=0, tiled=True)  115 us
    all_gather x1, waiting for transfers between devices, per_device(): lax.all_gather(first_moment, 'seq', axis=0, tiled=True)  103 us
    reduce_scatter x1, waiting for transfers between devices, per_device(): lax.psum_scatter(partial_input, 'tp', scatter_dimension=1, tiled=True)  42.1 us
    reduce_scatter x1, waiting for transfers between devices, per_device(): lax.psum_scatter(local_intersection, 'seq', scatter_dimension=0, tiled=True)  34.5 us
    dot_general x1, matrix products, per_device(): lax.dot_general(grad_out, lax.all_gather(weight, 'seq', axis=0, tiled=Tru...  26.5 us
    dot_general x2, matrix products, exact_dot(): jnp.dot(left, right, precision=lax.Precision.HIGHEST, preferred_element_t...  25 us
  transfers between devices with their start and end apart: 6, of which 6 were waited for; matrix products, arithmetic and copies ran while one was open for 8% of the time, Pallas kernels for 0%

commit v1 on v0

v1 whole, which is shorter than its diff:
```python
import jax
import jax.numpy as jnp
from jax import lax
from jax.sharding import PartitionSpec as P


def contract_rows(left, right):
    return lax.dot_general(
        left, right, (((0,), (0,)), ((), ())), preferred_element_type=jnp.float32
    )


def contract_columns(left, right):
    return lax.dot_general(
        left, right, (((1,), (1,)), ((), ())), preferred_element_type=jnp.float32
    )


def exact_dot(left, right):
    return jnp.dot(left, right, precision=lax.Precision.HIGHEST, preferred_element_type=jnp.float32)


def xor_order(items, index):
    bit = 1
    while bit < len(items):
        odd = (index & bit) != 0
        items = [jnp.where(odd, items[k ^ bit], items[k]) for k in range(len(items))]
        bit *= 2
    return items


def make_step(n, t):
    na = n // (2 * t)
    top_unit = 2 * na

    def swap(value, mask):
        return lax.ppermute(value, "seq", [(s, s ^ mask) for s in range(n)])

    def swap_tp(value, mask):
        return lax.ppermute(value, "tp", [(s, s ^ mask) for s in range(t)])

    def scatter(items, index, unit):
        items = xor_order(items, index)
        total = items[0]
        for k in range(1, len(items)):
            total = total + swap(items[k], k * unit)
        return total

    def exchange(items, index, unit):
        items = xor_order(items, index)
        return xor_order([items[0]] + [swap(items[k], k * unit) for k in range(1, len(items))], index)

    def per_device(grad_out, weight, saved, first_moment, second_moment, basis, new_basis):
        s, x = lax.axis_index("seq"), lax.axis_index("tp")
        core, group, top = s & 1, (s // 2) & (na - 1), s // top_unit
        tokens, width = grad_out.shape
        rows = first_moment.shape[0]
        half = width // 2
        part = half // na
        rank = saved.shape[1]

        w = {}
        w[0, 0] = weight
        for dz in range(1, t):
            w[dz, 0] = swap(weight, dz * top_unit)
        for dz in range(t):
            w[dz, 1] = swap(w[dz, 0], 1)

        a = [{0: grad_out[:, :half]}, {0: grad_out[:, half:]}]
        bit = na // 2
        while bit:
            for h in range(2):
                for j in list(a[h]):
                    a[h][j ^ bit] = swap(a[h][j], 2 * bit)
            bit //= 2
        saved_all = jnp.concatenate([saved if j == 0 else swap(saved, 2 * j) for j in range(na)], axis=0)

        gradient = []
        for h in range(2):
            mine = jnp.concatenate(
                [lax.dynamic_slice(a[h][j], (0, group * part), (tokens, part)) for j in range(na)], axis=0
            )
            g = contract_rows(saved_all, mine).reshape(t, na, 2, rows, part)
            g = scatter([g[:, :, 0], g[:, :, 1]], core, 1)
            g = scatter([g[k] for k in range(t)], top, top_unit)
            gradient.append(g.reshape(na * rows, part))
        gradient = jnp.concatenate(gradient, axis=1)

        local = contract_rows(new_basis, basis).reshape(t, na, 2, rows, rank)
        local = scatter([local[:, :, 0], local[:, :, 1]], core, 1)
        local = scatter([local[:, k] for k in range(na)], group, 2)
        own = scatter([local[k] for k in range(t)], top, top_unit)
        inter = jnp.stack(
            xor_order([own] + [swap(own, 2 * j) for j in range(1, na)], group), axis=0
        ).reshape(na * rows, t, na, 2, rows)
        inter = jnp.stack(xor_order([inter[:, k] for k in range(t)], top), axis=1)
        inter = jnp.stack(xor_order([inter[:, :, :, k] for k in range(2)], core), axis=2)
        inter = inter.reshape(na * rows, rank)

        def all_rows(moment):
            columns = moment.reshape(rows, 2, na, part)
            pieces = exchange([columns[:, :, k].reshape(rows, 2 * part) for k in range(na)], group, 2)
            near = jnp.concatenate(pieces, axis=0)
            found = []
            for dz in range(t):
                far = near if dz == 0 else swap(near, dz * top_unit)
                found += [far, swap(far, 1)]
            return jnp.concatenate(found, axis=0)

        first_rot = exact_dot(inter, all_rows(first_moment))
        second_rot = exact_dot(inter * inter, all_rows(second_moment))
        first = 0.9 * first_rot + 0.1 * gradient
        second = 0.95 * second_rot + 0.05 * gradient * gradient

        def own_rows(value):
            blocks = value.reshape(na, rows, 2 * part)
            pieces = exchange([blocks[k] for k in range(na)], group, 2)
            return jnp.stack([p.reshape(rows, 2, part) for p in pieces], axis=2).reshape(rows, width)

        first_new, second_new = own_rows(first), own_rows(second)
        update = first_new / (jnp.sqrt(second_new) + 1e-08)

        pieces = []
        for j in range(na):
            by_top = []
            for dz in range(t):
                c = [
                    contract_columns(a[0][j], w[dz, dc][:, :half]) + contract_columns(a[1][j], w[dz, dc][:, half:])
                    for dc in range(2)
                ]
                by_top.append(jnp.concatenate(xor_order(c, core), axis=1))
            by_top = xor_order(by_top, top ^ x)
            total = by_top[0]
            for e in range(1, t):
                total = total + swap_tp(by_top[e], e)
            pieces.append(total if j == 0 else swap(total, 2 * j))
        grad_input = jnp.concatenate(xor_order(pieces, group), axis=1)
        return (grad_input, first_new, second_new, update)

    return per_device


def solution(mesh):
    return jax.shard_map(
        make_step(mesh.shape["seq"], mesh.shape["tp"]),
        mesh=mesh,
        in_specs=(
            P("seq", "tp"),
            P("seq", "tp"),
            P("seq", None),
            P("seq", "tp"),
            P("seq", "tp"),
            P("seq", None),
            P("seq", None),
        ),
        out_specs=(P("seq", "tp"), P("seq", "tp"), P("seq", "tp"), P("seq", "tp")),
        check_vma=False,
    )
```

time: 805 us -> 550 us (0.68)
  waiting for transfers between devices: 726 us -> 354 us
  starting transfers between devices: 0.42 us -> 51.7 us
  local copies, waits for them, and re-layouts: 0.03 us -> 35.6 us
  matrix products: 64.2 us -> 86.6 us
  other arithmetic: 0 us -> 16.1 us
  between operations: 14.2 us -> 2.09 us
    all_gather x3 -> x0, waiting for transfers between devices: 495 us -> none  [the longest x1 277 us: per_device(): lax.all_gather(weight, 'seq', axis=0, tiled=True)]
    ppermute x0 -> x49, waiting for transfers between devices: none -> 354 us  [the longest x45 335 us: swap(): return lax.ppermute(value, 'seq', [(s, s ^ mask) for s in range(n)])]
    reduce_scatter x3 -> x0, waiting for transfers between devices: 230 us -> none  [the longest x1 153 us: per_device(): lax.psum_scatter(contract_rows(saved, grad_out), 'seq', scatter_dimension...]
    ppermute x0 -> x49, starting transfers between devices: none -> 51.7 us  [the longest x45 47.4 us: swap(): return lax.ppermute(value, 'seq', [(s, s ^ mask) for s in range(n)])]
    dot_general x1 -> x32, matrix products: 26.5 us -> 69.5 us  [contract_columns(): lax.dot_general(left, right, (((1,), (1,)), ((), ())), preferred_element_...]
    unnamed x10 -> x94, local copies, waits for them, and re-layouts: 0.03 us -> 14.7 us
    dot_general x2, matrix products: 25 us -> 14.2 us  [exact_dot(): jnp.dot(left, right, precision=lax.Precision.HIGHEST, preferred_element_t...]
    dot_general x2 -> x3, matrix products: 12.7 us -> 2.86 us  [contract_rows(): lax.dot_general(left, right, (((0,), (0,)), ((), ())), preferred_element_...]
  transfers between devices with their start and end apart: 6 -> 49, of which waited for: 6 -> 23; matrix products, arithmetic and copies ran while one was open for 8% -> 23% of each run, Pallas kernels for 0% -> 0%
where the time goes in v1:
time: 550 us; the launch traced here: 546 us
  waiting for transfers between devices  354 us (64%)
  matrix products  86.6 us (16%)
  starting transfers between devices  51.7 us (9%)
  local copies, waits for them, and re-layouts  35.6 us (6%)
  other arithmetic  16.1 us (3%)
    ppermute x45, waiting for transfers between devices, swap(): return lax.ppermute(value, 'seq', [(s, s ^ mask) for s in range(n)])  335 us
    dot_general x32, matrix products, contract_columns(): lax.dot_general(left, right, (((1,), (1,)), ((), ())), preferred_element_...  69.5 us
    ppermute x45, starting transfers between devices, swap(): return lax.ppermute(value, 'seq', [(s, s ^ mask) for s in range(n)])  47.4 us
    ppermute x4, waiting for transfers between devices, swap_tp(): return lax.ppermute(value, 'tp', [(s, s ^ mask) for s in range(t)])  18.3 us
    unnamed x94, local copies, waits for them, and re-layouts  14.7 us
    dot_general x2, matrix products, exact_dot(): jnp.dot(left, right, precision=lax.Precision.HIGHEST, preferred_element_t...  14.2 us
  transfers between devices with their start and end apart: 49, of which 23 were waited for; matrix products, arithmetic and copies ran while one was open for 23% of the time, Pallas kernels for 0%

profile of v1, /device:TPU:0, one launch (start us, length us, event | category | flops | bytes accessed | tf_op | source)
XLA Modules:
  0.0 545.7 jit_solution(6576269300622148948)
XLA Ops:
  0.6 3.1 collective-permute-start.31
  5.3 1.6 reshape.178
  12.1 1.6 collective-permute-start.41
  14.4 4.3 fusion.148
  25.6 2.2 constant_dynamic-slice_fusion.3
  28.1 1.9 collective-permute-start.26
  30.0 1.6 collective-permute-start.25
  34.5 2.9 collective-permute-done.24
  37.4 1.6 collective-permute-done.26
  44.3 1.6 collective-permute-start.19
  50.3 2.6 collective-permute-start.44
  52.9 7.0 %collective-permute-done.19 = f32[2,32,512]{2,1,0:T(8,128)S(1)} collective-permute-done((f32[2,32,512]{2,1,0:T(8,128)S(1)}, f32[2,32,512]{2,1,0:T(8,128)S(1)}, u32[]{:S(2)}, u32[]{:S(2)}) %collective-permute-start.19) | collective-permute-done | bytes 131104 | tf_op jit(solution)/shard_map/ppermute | solution.py:37
  61.0 31.9 %collective-permute-done.20 = f32[32,512]{1,0:T(8,128)S(1)} collective-permute-done((f32[32,512]{1,0:T(8,128)S(1)}, f32[32,512]{1,0:T(8,128)S(1)}, u32[]{:S(2)}, u32[]{:S(2)}) %collective-permute-start.20) | collective-permute-done | bytes 65568 | tf_op jit(solution)/shard_map/ppermute | solution.py:37
  94.5 3.0 collective-permute-done.23
  99.5 3.3 collective-permute-done.21
  104.3 2.0 collective-permute-start.4
  111.1 2.1 collective-permute-start.28
  113.2 2.3 constant_dynamic-update-slice_fusion.13
  117.9 83.7 %collective-permute-done.28 = f32[128,1792]{1,0:T(8,128)S(1)} collective-permute-done((f32[128,1792]{1,0:T(8,128)}, f32[128,1792]{1,0:T(8,128)S(1)}, u32[]{:S(2)}, u32[]{:S(2)}) %collective-permute-start.28) | collective-permute-done | bytes 917536 | tf_op jit(solution)/shard_map/ppermute | solution.py:37
  202.3 2.2 fusion.68
  206.6 2.2 fusion.88
  208.8 2.4 fusion.70
  215.5 2.3 fusion.85
  217.9 3.4 collective-permute-start.2
  221.4 26.2 %collective-permute-done.1 = bf16[256,3584]{1,0:T(8,128)(2,1)S(1)} collective-permute-done((bf16[256,3584]{1,0:T(8,128)(2,1)}, bf16[256,3584]{1,0:T(8,128)(2,1)S(1)}, u32[]{:S(2)}, u32[]{:S(2)}) %collective-permute-start.1) | collective-permute-done | bytes 1835040 | tf_op jit(solution)/shard_map/ppermute | solution.py:37
  249.1 37.3 %collective-permute-done.5 = bf16[256,3584]{1,0:T(8,128)(2,1)S(1)} collective-permute-done((bf16[256,3584]{1,0:T(8,128)(2,1)}, bf16[256,3584]{1,0:T(8,128)(2,1)S(1)}, u32[]{:S(2)}, u32[]{:S(2)}) %collective-permute-start.5) | collective-permute-done | bytes 1835040 | tf_op jit(solution)/shard_map/ppermute | solution.py:37
  288.7 2.2 fusion.22
  290.9 2.2 fusion.20
  295.8 83.6 %collective-permute-done.2 = bf16[256,7168]{1,0:T(8,128)(2,1)} collective-permute-done((bf16[256,7168]{1,0:T(8,128)(2,1)S(1)}, bf16[256,7168]{1,0:T(8,128)(2,1)}, u32[]{:S(2)}, u32[]{:S(2)}) %collective-permute-start.2) | collective-permute-done | bytes 3670048 | tf_op jit(solution)/shard_map/ppermute | solution.py:37
  379.4 2.7 fusion.38
  382.1 2.7 fusion.36
  384.8 2.2 fusion.34
  387.7 3.4 fusion.109
  391.2 2.9 fusion.115
  394.1 3.0 broadcast_select_fusion.35
  397.0 3.0 broadcast_select_fusion.31
  401.5 3.4 fusion.112
  404.9 2.2 fusion.40
  408.4 3.0 collective-permute-start.36
  411.3 2.9 fusion.106
  414.2 27.3 %collective-permute-done.34 = f32[4,32,896]{2,1,0:T(8,128)S(1)} collective-permute-done((f32[4,32,896]{2,1,0:T(8,128)S(1)}, f32[4,32,896]{2,1,0:T(8,128)S(1)}, u32[]{:S(2)}, u32[]{:S(2)}) %collective-permute-start.34) | collective-permute-done | bytes 458784 | tf_op jit(solution)/shard_map/ppermute | solution.py:37
  441.7 9.7 %collective-permute-done.36 = f32[4,32,896]{2,1,0:T(8,128)S(1)} collective-permute-done((f32[4,32,896]{2,1,0:T(8,128)S(1)}, f32[4,32,896]{2,1,0:T(8,128)S(1)}, u32[]{:S(2)}, u32[]{:S(2)}) %collective-permute-start.36) | collective-permute-done | bytes 458784 | tf_op jit(solution)/shard_map/ppermute | solution.py:37
  451.4 12.2 %fusion.1 = f32[128,1792]{1,0:T(8,128)S(1)} fusion(f32[512,1792]{1,0:T(8,128)S(1)} %constant_dynamic-update-slice_fusion.11, f32[128,896]{1,0:T(8,128)S(1)} %bitcast.160, f32[128,896]{1,0:T(8,128)S(1)} %bitcast.158, f32[128,512]{0,1:T(8,128)S(1)} %bitcast.162), kind=kOutput, calls=%fused_computation.3 | convolution fusion | flops 1410498560 | bytes 5767168 | tf_op jit(solution)/shard_map/dot_general | solution.py:20
  464.5 2.7 collective-permute-start.47
  467.2 2.1 fusion
  471.0 6.1 %collective-permute-done.48 = f32[32,1792]{1,0:T(8,128)S(1)} collective-permute-done((f32[32,1792]{1,0:T(8,128)S(1)}, f32[32,1792]{1,0:T(8,128)S(1)}, u32[]{:S(2)}, u32[]{:S(2)}) %collective-permute-start.48) | collective-permute-done | bytes 229408 | tf_op jit(solution)/shard_map/ppermute | solution.py:37
  477.1 2.3 collective-permute-start.38
  481.5 4.0 collective-permute-done.39
  491.0 3.1 fusion.56
  494.1 2.2 broadcast_select_fusion.41
  496.4 1.5 collective-permute-start.7
  498.0 2.7 fusion.52
  500.7 2.8 broadcast_select_fusion.33
  504.2 2.7 fusion.54
  507.0 2.9 broadcast_select_fusion.37
  510.0 1.5 collective-permute-start.9
  511.5 2.2 fusion.50
  513.7 2.2 broadcast_select_fusion.29
  517.8 4.7 collective-permute-done.13
  522.6 2.2 collective-permute-start.14
  524.8 9.0 %collective-permute-done.9 = f32[256,512]{0,1:T(8,128)S(1)} collective-permute-done((f32[256,512]{0,1:T(8,128)S(1)}, f32[256,512]{0,1:T(8,128)S(1)}, u32[]{:S(2)}, u32[]{:S(2)}) %collective-permute-start.9) | collective-permute-done | bytes 524320 | tf_op jit(solution)/shard_map/ppermute | solution.py:40
  536.1 4.6 collective-permute-done.15
  540.7 2.4 collective-permute-done.10
  543.7 1.8 copy.85
  (244 shorter events, 73.2 us)
Async XLA Ops:
  0.6 24.5 %copy-start = (bf16[256,512]{1,0:T(8,128)(2,1)S(1)}, bf16[256,512]{1,0:T(8,128)(2,1)}, u32[]{:S(2)}) copy-start(bf16[256,512]{1,0:T(8,128)(2,1)} %param.13) | copy-start | bytes 786436
  0.6 92.3 %collective-permute-start.31 = (bf16[256,512]{1,0:T(8,128)(2,1)}, bf16[256,512]{1,0:T(8,128)(2,1)S(1)}, u32[]{:S(2)}, u32[]{:S(2)}) collective-permute-start(bf16[256,512]{1,0:T(8,128)(2,1)} %param.9), channel_id=1, source_target_pairs={{0,8},{2,10},{4,12},{6,14},{8,0},{10,2},{12,4},{14,6},{16,24},{18,... | collective-permute-start | bytes 786440 | tf_op jit(solution)/shard_map/ppermute | solution.py:37
  3.7 56.2 %collective-permute-start.30 = (bf16[256,512]{1,0:T(8,128)(2,1)}, bf16[256,512]{1,0:T(8,128)(2,1)}, u32[]{:S(2)}, u32[]{:S(2)}) collective-permute-start(bf16[256,512]{1,0:T(8,128)(2,1)} %param.9), channel_id=1, source_target_pairs={{0,4},{2,6},{4,0},{6,2},{8,12},{10,14},{12,8},{14,10},{16,20},{18,... | collective-permute-start | bytes 786440 | tf_op jit(solution)/shard_map/ppermute | solution.py:37
  7.6 6.1 %copy-start.22 = (bf16[256,512]{1,0:T(8,128)(2,1)S(1)}, bf16[256,512]{1,0:T(8,128)(2,1)}, u32[]{:S(2)}) copy-start(bf16[256,512]{1,0:T(8,128)(2,1)} %param.9) | copy-start | bytes 786436
  8.8 19.2 %collective-permute-start.42 = (f32[32,1792]{1,0:T(8,128)}, f32[32,1792]{1,0:T(8,128)S(1)}, u32[]{:S(2)}, u32[]{:S(2)}) collective-permute-start(f32[32,1792]{1,0:T(8,128)} %bitcast.63), channel_id=1, source_target_pairs={{0,4},{2,6},{4,0},{6,2},{8,12},{10,14},{12,8},{14,10},{16,20},{18,... | collective-permute-start | bytes 688136 | tf_op jit(solution)/shard_map/ppermute | solution.py:37
  10.0 18.1 %collective-permute-start.40 = (f32[32,1792]{1,0:T(8,128)}, f32[32,1792]{1,0:T(8,128)S(1)}, u32[]{:S(2)}, u32[]{:S(2)}) collective-permute-start(f32[32,1792]{1,0:T(8,128)} %bitcast.55), channel_id=1, source_target_pairs={{0,12},{2,14},{4,8},{6,10},{8,4},{10,6},{12,0},{14,2},{16,28},{18,... | collective-permute-start | bytes 688136 | tf_op jit(solution)/shard_map/ppermute | solution.py:37
  12.1 17.9 %collective-permute-start.41 = (f32[32,1792]{1,0:T(8,128)}, f32[32,1792]{1,0:T(8,128)S(1)}, u32[]{:S(2)}, u32[]{:S(2)}) collective-permute-start(f32[32,1792]{1,0:T(8,128)} %bitcast.59), channel_id=1, source_target_pairs={{0,8},{2,10},{4,12},{6,14},{8,0},{10,2},{12,4},{14,6},{16,24},{18,... | collective-permute-start | bytes 688136 | tf_op jit(solution)/shard_map/ppermute | solution.py:37
  28.0 9.4 %collective-permute-start.24 = (f32[32,1792]{1,0:T(8,128)S(1)}, f32[32,1792]{1,0:T(8,128)S(1)}, u32[]{:S(2)}, u32[]{:S(2)}) collective-permute-start(f32[32,1792]{1,0:T(8,128)S(1)} %bitcast.174), channel_id=1, source_target_pairs={{0,12},{2,14},{4,8},{6,10},{8,4},{10,6},{12,0},{14,2},{16,28},{18,... | collective-permute-start | bytes 688136 | tf_op jit(solution)/shard_map/ppermute | solution.py:37
  28.1 10.9 %collective-permute-start.26 = (f32[32,1792]{1,0:T(8,128)S(1)}, f32[32,1792]{1,0:T(8,128)S(1)}, u32[]{:S(2)}, u32[]{:S(2)}) collective-permute-start(f32[32,1792]{1,0:T(8,128)S(1)} %bitcast.173), channel_id=1, source_target_pairs={{0,4},{2,6},{4,0},{6,2},{8,12},{10,14},{12,8},{14,10},{16,20},{18,... | collective-permute-start | bytes 688136 | tf_op jit(solution)/shard_map/ppermute | solution.py:37
  30.0 9.0 %collective-permute-start.25 = (f32[32,1792]{1,0:T(8,128)S(1)}, f32[32,1792]{1,0:T(8,128)S(1)}, u32[]{:S(2)}, u32[]{:S(2)}) collective-permute-start(f32[32,1792]{1,0:T(8,128)S(1)} %bitcast.172), channel_id=1, source_target_pairs={{0,8},{2,10},{4,12},{6,14},{8,0},{10,2},{12,4},{14,6},{16,24},{18,... | collective-permute-start | bytes 688136 | tf_op jit(solution)/shard_map/ppermute | solution.py:37
  37.4 4.7 collective-permute-start.16
  42.3 17.8 %copy-start.29 = (bf16[1024,512]{1,0:T(8,128)(2,1)S(1)}, bf16[1024,512]{1,0:T(8,128)(2,1)}, u32[]{:S(2)}) copy-start(bf16[1024,512]{1,0:T(8,128)(2,1)} %constant_dynamic-update-slice_fusion.10) | copy-start | bytes 3145732
  42.4 6.1 %collective-permute-start.17 = (f32[2,32,512]{2,1,0:T(8,128)S(1)}, f32[2,32,512]{2,1,0:T(8,128)S(1)}, u32[]{:S(2)}, u32[]{:S(2)}) collective-permute-start(f32[2,32,512]{2,1,0:T(8,128)S(1)} %get-tuple-element.83), channel_id=1, source_target_pairs={{0,4},{2,6},{4,0},{6,2},{8,12},{10,14},{12,8},{14,10},{16,20},{18,... | collective-permute-start | bytes 393224 | tf_op jit(solution)/shard_map/ppermute | solution.py:37
  43.8 6.4 %collective-permute-start.18 = (f32[2,32,512]{2,1,0:T(8,128)S(1)}, f32[2,32,512]{2,1,0:T(8,128)S(1)}, u32[]{:S(2)}, u32[]{:S(2)}) collective-permute-start(f32[2,32,512]{2,1,0:T(8,128)S(1)} %get-tuple-element.84), channel_id=1, source_target_pairs={{0,8},{2,10},{4,12},{6,14},{8,0},{10,2},{12,4},{14,6},{16,24},{18,... | collective-permute-start | bytes 393224 | tf_op jit(solution)/shard_map/ppermute | solution.py:37
  44.3 15.6 %collective-permute-start.19 = (f32[2,32,512]{2,1,0:T(8,128)S(1)}, f32[2,32,512]{2,1,0:T(8,128)S(1)}, u32[]{:S(2)}, u32[]{:S(2)}) collective-permute-start(f32[2,32,512]{2,1,0:T(8,128)S(1)} %get-tuple-element.85), channel_id=1, source_target_pairs={{0,12},{2,14},{4,8},{6,10},{8,4},{10,6},{12,0},{14,2},{16,28},{18,... | collective-permute-start | bytes 393224 | tf_op jit(solution)/shard_map/ppermute | solution.py:37
  46.9 55.9 %copy-start.9 = (bf16[256,3584]{1,0:T(8,128)(2,1)S(1)}, bf16[256,3584]{1,0:T(8,128)(2,1)}, u32[]{:S(2)}) copy-start(bf16[256,3584]{1,0:T(8,128)(2,1)} %get-tuple-element.41) | copy-start | bytes 5505028
  48.4 46.0 %collective-permute-start.32 = (bf16[256,512]{1,0:T(8,128)(2,1)S(1)}, bf16[256,512]{1,0:T(8,128)(2,1)S(1)}, u32[]{:S(2)}, u32[]{:S(2)}) collective-permute-start(bf16[256,512]{1,0:T(8,128)(2,1)S(1)} %copy-done.22), channel_id=1, source_target_pairs={{0,12},{2,14},{4,8},{6,10},{8,4},{10,6},{12,0},{14,2},{16,28},{18,... | collective-permute-start | bytes 786440 | tf_op jit(solution)/shard_map/ppermute | solution.py:37
  50.3 53.9 %collective-permute-start.44 = (f32[128,1792]{1,0:T(8,128)S(1)}, f32[128,1792]{1,0:T(8,128)S(1)}, u32[]{:S(2)}, u32[]{:S(2)}) collective-permute-start(f32[128,1792]{1,0:T(8,128)S(1)} %pad_maximum_fusion.4), channel_id=1, source_target_pairs={{0,16},{2,18},{4,20},{6,22},{8,24},{10,26},{12,28},{14,30},{16,0},... | collective-permute-start | bytes 2752520 | tf_op jit(solution)/shard_map/ppermute | solution.py:37
  59.9 44.4 %collective-permute-start.43 = (f32[128,1792]{1,0:T(8,128)S(1)}, f32[128,1792]{1,0:T(8,128)S(1)}, u32[]{:S(2)}, u32[]{:S(2)}) collective-permute-start(f32[128,1792]{1,0:T(8,128)S(1)} %pad_maximum_fusion.4), channel_id=1, source_target_pairs={{0,2},{2,0},{4,6},{6,4},{8,10},{10,8},{12,14},{14,12},{16,18},{18,... | collective-permute-start | bytes 2752520 | tf_op jit(solution)/shard_map/ppermute | solution.py:37
  60.0 33.0 %collective-permute-start.20 = (f32[32,512]{1,0:T(8,128)S(1)}, f32[32,512]{1,0:T(8,128)S(1)}, u32[]{:S(2)}, u32[]{:S(2)}) collective-permute-start(f32[32,512]{1,0:T(8,128)S(1)} %select_bitcast_fusion.14), channel_id=1, source_target_pairs={{0,16},{2,18},{4,20},{6,22},{8,24},{10,26},{12,28},{14,30},{16,0},... | collective-permute-start | bytes 196616 | tf_op jit(solution)/shard_map/ppermute | solution.py:37
  92.9 18.1 %collective-permute-start.27 = (f32[128,1792]{1,0:T(8,128)}, f32[128,1792]{1,0:T(8,128)}, u32[]{:S(2)}, u32[]{:S(2)}) collective-permute-start(f32[128,1792]{1,0:T(8,128)} %pad_maximum_fusion.1), channel_id=1, source_target_pairs={{0,2},{2,0},{4,6},{6,4},{8,10},{10,8},{12,14},{14,12},{16,18},{18,... | collective-permute-start | bytes 2752520 | tf_op jit(solution)/shard_map/ppermute | solution.py:37
  93.0 4.6 collective-permute-start.23
  94.4 4.3 collective-permute-start.22
  97.5 5.2 collective-permute-start.21
  98.1 8.2 %copy-start.30 = (bf16[1024,512]{1,0:T(8,128)(2,1)}, bf16[1024,512]{1,0:T(8,128)(2,1)S(1)}, u32[]{:S(2)}) copy-start(bf16[1024,512]{1,0:T(8,128)(2,1)S(1)} %constant_dynamic-update-slice_fusion.7) | copy-start | bytes 3145732
  98.7 105.7 %collective-permute-start.11 = (bf16[256,3584]{1,0:T(8,128)(2,1)}, bf16[256,3584]{1,0:T(8,128)(2,1)}, u32[]{:S(2)}, u32[]{:S(2)}) collective-permute-start(bf16[256,3584]{1,0:T(8,128)(2,1)} %get-tuple-element.40), channel_id=1, source_target_pairs={{0,4},{2,6},{4,0},{6,2},{8,12},{10,14},{12,8},{14,10},{16,20},{18,... | collective-permute-start | bytes 5505032 | tf_op jit(solution)/shard_map/ppermute | solution.py:37
  102.8 98.9 %collective-permute-start.12 = (bf16[256,3584]{1,0:T(8,128)(2,1)S(1)}, bf16[256,3584]{1,0:T(8,128)(2,1)}, u32[]{:S(2)}, u32[]{:S(2)}) collective-permute-start(bf16[256,3584]{1,0:T(8,128)(2,1)S(1)} %copy-done.9), channel_id=1, source_target_pairs={{0,4},{2,6},{4,0},{6,2},{8,12},{10,14},{12,8},{14,10},{16,20},{18,... | collective-permute-start | bytes 5505032 | tf_op jit(solution)/shard_map/ppermute | solution.py:37
  104.2 100.4 %collective-permute-start = (bf16[256,3584]{1,0:T(8,128)(2,1)}, bf16[256,3584]{1,0:T(8,128)(2,1)}, u32[]{:S(2)}, u32[]{:S(2)}) collective-permute-start(bf16[256,3584]{1,0:T(8,128)(2,1)} %get-tuple-element.40), channel_id=1, source_target_pairs={{0,8},{2,10},{4,12},{6,14},{8,0},{10,2},{12,4},{14,6},{16,24},{18,... | collective-permute-start | bytes 5505032 | tf_op jit(solution)/shard_map/ppermute | solution.py:37
  104.3 101.0 %collective-permute-start.4 = (bf16[256,3584]{1,0:T(8,128)(2,1)S(1)}, bf16[256,3584]{1,0:T(8,128)(2,1)}, u32[]{:S(2)}, u32[]{:S(2)}) collective-permute-start(bf16[256,3584]{1,0:T(8,128)(2,1)S(1)} %copy-done.9), channel_id=1, source_target_pairs={{0,8},{2,10},{4,12},{6,14},{8,0},{10,2},{12,4},{14,6},{16,24},{18,... | collective-permute-start | bytes 5505032 | tf_op jit(solution)/shard_map/ppermute | solution.py:37
  109.7 5.8 %copy-start.18 = (f32[128,1792]{1,0:T(8,128)S(1)}, f32[128,1792]{1,0:T(8,128)}, u32[]{:S(2)}) copy-start(f32[128,1792]{1,0:T(8,128)} %copy-done.17) | copy-start | bytes 2752516
  111.1 90.5 %collective-permute-start.28 = (f32[128,1792]{1,0:T(8,128)}, f32[128,1792]{1,0:T(8,128)S(1)}, u32[]{:S(2)}, u32[]{:S(2)}) collective-permute-start(f32[128,1792]{1,0:T(8,128)} %pad_maximum_fusion.1), channel_id=1, source_target_pairs={{0,16},{2,18},{4,20},{6,22},{8,24},{10,26},{12,28},{14,30},{16,0},... | collective-permute-start | bytes 2752520 | tf_op jit(solution)/shard_map/ppermute | solution.py:37
  116.5 85.7 %copy-start.33 = (bf16[256,7168]{1,0:T(8,128)(2,1)S(1)}, bf16[256,7168]{1,0:T(8,128)(2,1)}, u32[]{:S(2)}) copy-start(bf16[256,7168]{1,0:T(8,128)(2,1)} %param.8) | copy-start | bytes 11010052
  201.6 87.1 %collective-permute-start.6 = (bf16[256,7168]{1,0:T(8,128)(2,1)}, bf16[256,7168]{1,0:T(8,128)(2,1)S(1)}, u32[]{:S(2)}, u32[]{:S(2)}) collective-permute-start(bf16[256,7168]{1,0:T(8,128)(2,1)} %param.8), channel_id=1, source_target_pairs={{0,2},{2,0},{4,6},{6,4},{8,10},{10,8},{12,14},{14,12},{16,18},{18,... | collective-permute-start | bytes 11010056 | tf_op jit(solution)/shard_map/ppermute | solution.py:37
  201.7 16.2 %collective-permute-start.45 = (f32[128,1792]{1,0:T(8,128)S(1)}, f32[128,1792]{1,0:T(8,128)S(1)}, u32[]{:S(2)}, u32[]{:S(2)}) collective-permute-start(f32[128,1792]{1,0:T(8,128)S(1)} %copy-done.18), channel_id=1, source_target_pairs={{0,2},{2,0},{4,6},{6,4},{8,10},{10,8},{12,14},{14,12},{16,18},{18,... | collective-permute-start | bytes 2752520 | tf_op jit(solution)/shard_map/ppermute | solution.py:37
  204.4 16.9 %collective-permute-start.29 = (f32[128,1792]{1,0:T(8,128)S(1)}, f32[128,1792]{1,0:T(8,128)S(1)}, u32[]{:S(2)}, u32[]{:S(2)}) collective-permute-start(f32[128,1792]{1,0:T(8,128)S(1)} %collective-permute-done.28), channel_id=1, source_target_pairs={{0,2},{2,0},{4,6},{6,4},{8,10},{10,8},{12,14},{14,12},{16,18},{18,... | collective-permute-start | bytes 2752520 | tf_op jit(solution)/shard_map/ppermute | solution.py:37
  204.5 43.1 %collective-permute-start.1 = (bf16[256,3584]{1,0:T(8,128)(2,1)}, bf16[256,3584]{1,0:T(8,128)(2,1)S(1)}, u32[]{:S(2)}, u32[]{:S(2)}) collective-permute-start(bf16[256,3584]{1,0:T(8,128)(2,1)} %collective-permute-done), channel_id=1, source_target_pairs={{0,4},{2,6},{4,0},{6,2},{8,12},{10,14},{12,8},{14,10},{16,20},{18,... | collective-permute-start | bytes 5505032 | tf_op jit(solution)/shard_map/ppermute | solution.py:37
  205.3 81.2 %collective-permute-start.5 = (bf16[256,3584]{1,0:T(8,128)(2,1)}, bf16[256,3584]{1,0:T(8,128)(2,1)S(1)}, u32[]{:S(2)}, u32[]{:S(2)}) collective-permute-start(bf16[256,3584]{1,0:T(8,128)(2,1)} %collective-permute-done.4), channel_id=1, source_target_pairs={{0,4},{2,6},{4,0},{6,2},{8,12},{10,14},{12,8},{14,10},{16,20},{18,... | collective-permute-start | bytes 5505032 | tf_op jit(solution)/shard_map/ppermute | solution.py:37
  215.5 5.7 %copy-start.2 = (f32[512,1792]{1,0:T(8,128)S(1)}, f32[512,1792]{1,0:T(8,128)}, u32[]{:S(2)}) copy-start(f32[512,1792]{1,0:T(8,128)} %constant_dynamic-update-slice_fusion.12) | copy-start | bytes 11010052
  217.9 161.5 %collective-permute-start.2 = (bf16[256,7168]{1,0:T(8,128)(2,1)S(1)}, bf16[256,7168]{1,0:T(8,128)(2,1)}, u32[]{:S(2)}, u32[]{:S(2)}) collective-permute-start(bf16[256,7168]{1,0:T(8,128)(2,1)S(1)} %copy-done.33), channel_id=1, source_target_pairs={{0,16},{2,18},{4,20},{6,22},{8,24},{10,26},{12,28},{14,30},{16,0},... | collective-permute-start | bytes 11010056 | tf_op jit(solution)/shard_map/ppermute | solution.py:37
  221.3 26.4 %copy-start.21 = (bf16[256,896]{1,0:T(8,128)(2,1)S(1)}, bf16[256,896]{1,0:T(8,128)(2,1)}, u32[]{:S(2)}) copy-start(bf16[256,896]{1,0:T(8,128)(2,1)} %get-tuple-element.109) | copy-start | bytes 1376260
  221.3 26.4 %copy-start.31 = (bf16[1024,512]{1,0:T(8,128)(2,1)S(1)}, bf16[1024,512]{1,0:T(8,128)(2,1)}, u32[]{:S(2)}) copy-start(bf16[1024,512]{1,0:T(8,128)(2,1)} %copy-done.30) | copy-start | bytes 3145732
  247.6 163.7 %copy-start.26 = (bf16[256,3584]{1,0:T(8,128)(2,1)}, bf16[256,3584]{1,0:T(8,128)(2,1)S(1)}, u32[]{:S(2)}) copy-start(bf16[256,3584]{1,0:T(8,128)(2,1)S(1)} %collective-permute-done.1) | copy-start | bytes 5505028
  249.0 37.6 %copy-start.20 = (bf16[256,896]{1,0:T(8,128)(2,1)S(1)}, bf16[256,896]{1,0:T(8,128)(2,1)}, u32[]{:S(2)}) copy-start(bf16[256,896]{1,0:T(8,128)(2,1)} %get-tuple-element.108) | copy-start | bytes 1376260
  249.1 158.8 %collective-permute-start.33 = (f32[2,4,32,896]{3,2,1,0:T(8,128)S(1)}, f32[2,4,32,896]{3,2,1,0:T(8,128)S(1)}, u32[]{:S(2)}, u32[]{:S(2)}) collective-permute-start(f32[2,4,32,896]{3,2,1,0:T(8,128)S(1)} %select_bitcast_fusion.1), channel_id=1, source_target_pairs={{0,2},{2,0},{4,6},{6,4},{8,10},{10,8},{12,14},{14,12},{16,18},{18,... | collective-permute-start | bytes 2752520 | tf_op jit(solution)/shard_map/ppermute | solution.py:37
  286.5 118.5 %copy-start.28 = (bf16[256,3584]{1,0:T(8,128)(2,1)}, bf16[256,3584]{1,0:T(8,128)(2,1)S(1)}, u32[]{:S(2)}) copy-start(bf16[256,3584]{1,0:T(8,128)(2,1)S(1)} %collective-permute-done.5) | copy-start | bytes 5505028
  287.9 120.2 %collective-permute-start.35 = (f32[2,4,32,896]{3,2,1,0:T(8,128)S(1)}, f32[2,4,32,896]{3,2,1,0:T(8,128)S(1)}, u32[]{:S(2)}, u32[]{:S(2)}) collective-permute-start(f32[2,4,32,896]{3,2,1,0:T(8,128)S(1)} %select_bitcast_fusion), channel_id=1, source_target_pairs={{0,2},{2,0},{4,6},{6,4},{8,10},{10,8},{12,14},{14,12},{16,18},{18,... | collective-permute-start | bytes 2752520 | tf_op jit(solution)/shard_map/ppermute | solution.py:37
  387.0 104.0 %collective-permute-start.3 = (bf16[256,7168]{1,0:T(8,128)(2,1)}, bf16[256,7168]{1,0:T(8,128)(2,1)}, u32[]{:S(2)}, u32[]{:S(2)}) collective-permute-start(bf16[256,7168]{1,0:T(8,128)(2,1)} %collective-permute-done.2), channel_id=1, source_target_pairs={{0,2},{2,0},{4,6},{6,4},{8,10},{10,8},{12,14},{14,12},{16,18},{18,... | collective-permute-start | bytes 11010056 | tf_op jit(solution)/shard_map/ppermute | solution.py:37
  408.1 33.5 %collective-permute-start.34 = (f32[4,32,896]{2,1,0:T(8,128)S(1)}, f32[4,32,896]{2,1,0:T(8,128)S(1)}, u32[]{:S(2)}, u32[]{:S(2)}) collective-permute-start(f32[4,32,896]{2,1,0:T(8,128)S(1)} %select_bitcast_fusion.4), channel_id=1, source_target_pairs={{0,16},{2,18},{4,20},{6,22},{8,24},{10,26},{12,28},{14,30},{16,0},... | collective-permute-start | bytes 1376264 | tf_op jit(solution)/shard_map/ppermute | solution.py:37
  408.4 43.0 %collective-permute-start.36 = (f32[4,32,896]{2,1,0:T(8,128)S(1)}, f32[4,32,896]{2,1,0:T(8,128)S(1)}, u32[]{:S(2)}, u32[]{:S(2)}) collective-permute-start(f32[4,32,896]{2,1,0:T(8,128)S(1)} %select_bitcast_fusion.3), channel_id=1, source_target_pairs={{0,16},{2,18},{4,20},{6,22},{8,24},{10,26},{12,28},{14,30},{16,0},... | collective-permute-start | bytes 1376264 | tf_op jit(solution)/shard_map/ppermute | solution.py:37
  463.7 13.4 %collective-permute-start.48 = (f32[32,1792]{1,0:T(8,128)S(1)}, f32[32,1792]{1,0:T(8,128)S(1)}, u32[]{:S(2)}, u32[]{:S(2)}) collective-permute-start(f32[32,1792]{1,0:T(8,128)S(1)} %get-tuple-element.57), channel_id=1, source_target_pairs={{0,4},{2,6},{4,0},{6,2},{8,12},{10,14},{12,8},{14,10},{16,20},{18,... | collective-permute-start | bytes 688136 | tf_op jit(solution)/shard_map/ppermute | solution.py:37
  464.5 12.6 %collective-permute-start.46 = (f32[32,1792]{1,0:T(8,128)S(1)}, f32[32,1792]{1,0:T(8,128)S(1)}, u32[]{:S(2)}, u32[]{:S(2)}) collective-permute-start(f32[32,1792]{1,0:T(8,128)S(1)} %get-tuple-element.58), channel_id=1, source_target_pairs={{0,12},{2,14},{4,8},{6,10},{8,4},{10,6},{12,0},{14,2},{16,28},{18,... | collective-permute-start | bytes 688136 | tf_op jit(solution)/shard_map/ppermute | solution.py:37
  464.5 14.9 %collective-permute-start.47 = (f32[32,1792]{1,0:T(8,128)S(1)}, f32[32,1792]{1,0:T(8,128)S(1)}, u32[]{:S(2)}, u32[]{:S(2)}) collective-permute-start(f32[32,1792]{1,0:T(8,128)S(1)} %get-tuple-element.59), channel_id=1, source_target_pairs={{0,8},{2,10},{4,12},{6,14},{8,0},{10,2},{12,4},{14,6},{16,24},{18,... | collective-permute-start | bytes 688136 | tf_op jit(solution)/shard_map/ppermute | solution.py:37
  470.3 15.2 %collective-permute-start.39 = (f32[32,1792]{1,0:T(8,128)}, f32[32,1792]{1,0:T(8,128)}, u32[]{:S(2)}, u32[]{:S(2)}) collective-permute-start(f32[32,1792]{1,0:T(8,128)} %get-tuple-element.70), channel_id=1, source_target_pairs={{0,4},{2,6},{4,0},{6,2},{8,12},{10,14},{12,8},{14,10},{16,20},{18,... | collective-permute-start | bytes 688136 | tf_op jit(solution)/shard_map/ppermute | solution.py:37
  477.1 9.6 %collective-permute-start.37 = (f32[32,1792]{1,0:T(8,128)}, f32[32,1792]{1,0:T(8,128)}, u32[]{:S(2)}, u32[]{:S(2)}) collective-permute-start(f32[32,1792]{1,0:T(8,128)} %get-tuple-element.71), channel_id=1, source_target_pairs={{0,12},{2,14},{4,8},{6,10},{8,4},{10,6},{12,0},{14,2},{16,28},{18,... | collective-permute-start | bytes 688136 | tf_op jit(solution)/shard_map/ppermute | solution.py:37
  477.1 10.6 %collective-permute-start.38 = (f32[32,1792]{1,0:T(8,128)}, f32[32,1792]{1,0:T(8,128)}, u32[]{:S(2)}, u32[]{:S(2)}) collective-permute-start(f32[32,1792]{1,0:T(8,128)} %get-tuple-element.72), channel_id=1, source_target_pairs={{0,8},{2,10},{4,12},{6,14},{8,0},{10,2},{12,4},{14,6},{16,24},{18,... | collective-permute-start | bytes 688136 | tf_op jit(solution)/shard_map/ppermute | solution.py:37
  481.5 53.4 %copy-start.7 = (f32[32,7168]{1,0:T(8,128)}, f32[32,7168]{1,0:T(8,128)S(1)}, u32[]{:S(2)}) copy-start(f32[32,7168]{1,0:T(8,128)S(1)} %reshape.179) | copy-start | bytes 2752516
  490.9 43.9 %copy-start.8 = (f32[32,7168]{1,0:T(8,128)}, f32[32,7168]{1,0:T(8,128)S(1)}, u32[]{:S(2)}) copy-start(f32[32,7168]{1,0:T(8,128)S(1)} %reshape.177) | copy-start | bytes 2752516
  496.4 20.2 %collective-permute-start.7 = (f32[256,512]{0,1:T(8,128)S(1)}, f32[256,512]{0,1:T(8,128)S(1)}, u32[]{:S(2)}, u32[]{:S(2)}) collective-permute-start(f32[256,512]{0,1:T(8,128)S(1)} %fusion.133), channel_id=1, source_target_pairs={{0,1},{1,0},{2,3},{3,2},{4,5},{5,4},{6,7},{7,6},{8,9},{9,8},{10,11... | collective-permute-start | bytes 1572872 | tf_op jit(solution)/shard_map/ppermute | solution.py:40
  503.6 18.9 %collective-permute-start.13 = (f32[256,512]{0,1:T(8,128)S(1)}, f32[256,512]{0,1:T(8,128)S(1)}, u32[]{:S(2)}, u32[]{:S(2)}) collective-permute-start(f32[256,512]{0,1:T(8,128)S(1)} %fusion.131), channel_id=1, source_target_pairs={{0,1},{1,0},{2,3},{3,2},{4,5},{5,4},{6,7},{7,6},{8,9},{9,8},{10,11... | collective-permute-start | bytes 1572872 | tf_op jit(solution)/shard_map/ppermute | solution.py:40
  510.0 23.8 %collective-permute-start.9 = (f32[256,512]{0,1:T(8,128)S(1)}, f32[256,512]{0,1:T(8,128)S(1)}, u32[]{:S(2)}, u32[]{:S(2)}) collective-permute-start(f32[256,512]{0,1:T(8,128)S(1)} %fusion.132), channel_id=1, source_target_pairs={{0,1},{1,0},{2,3},{3,2},{4,5},{5,4},{6,7},{7,6},{8,9},{9,8},{10,11... | collective-permute-start | bytes 1572872 | tf_op jit(solution)/shard_map/ppermute | solution.py:40
  516.0 24.7 %collective-permute-start.15 = (f32[256,512]{0,1:T(8,128)S(1)}, f32[256,512]{0,1:T(8,128)S(1)}, u32[]{:S(2)}, u32[]{:S(2)}) collective-permute-start(f32[256,512]{0,1:T(8,128)S(1)} %fusion.130), channel_id=1, source_target_pairs={{0,1},{1,0},{2,3},{3,2},{4,5},{5,4},{6,7},{7,6},{8,9},{9,8},{10,11... | collective-permute-start | bytes 1572872 | tf_op jit(solution)/shard_map/ppermute | solution.py:40
  516.7 24.0 %collective-permute-start.8 = (f32[256,512]{0,1:T(8,128)S(1)}, f32[256,512]{0,1:T(8,128)S(1)}, u32[]{:S(2)}, u32[]{:S(2)}) collective-permute-start(f32[256,512]{0,1:T(8,128)S(1)} %select_add_fusion.3), channel_id=1, source_target_pairs={{0,12},{2,14},{4,8},{6,10},{8,4},{10,6},{12,0},{14,2},{16,28},{18,... | collective-permute-start | bytes 1572872 | tf_op jit(solution)/shard_map/ppermute | solution.py:37
  522.6 18.1 %collective-permute-start.14 = (f32[256,512]{0,1:T(8,128)S(1)}, f32[256,512]{0,1:T(8,128)S(1)}, u32[]{:S(2)}, u32[]{:S(2)}) collective-permute-start(f32[256,512]{0,1:T(8,128)S(1)} %select_add_fusion.1), channel_id=1, source_target_pairs={{0,4},{2,6},{4,0},{6,2},{8,12},{10,14},{12,8},{14,10},{16,20},{18,... | collective-permute-start | bytes 1572872 | tf_op jit(solution)/shard_map/ppermute | solution.py:37
  533.9 9.2 %collective-permute-start.10 = (f32[256,512]{0,1:T(8,128)S(1)}, f32[256,512]{0,1:T(8,128)S(1)}, u32[]{:S(2)}, u32[]{:S(2)}) collective-permute-start(f32[256,512]{0,1:T(8,128)S(1)} %select_add_fusion.2), channel_id=1, source_target_pairs={{0,8},{2,10},{4,12},{6,14},{8,0},{10,2},{12,4},{14,6},{16,24},{18,... | collective-permute-start | bytes 1572872 | tf_op jit(solution)/shard_map/ppermute | solution.py:37
  (24 other events, 69.9 us)

commit v2 on v0

v2 whole, which is shorter than its diff:
```python
import functools

import jax
import jax.numpy as jnp
from jax import lax
from jax.experimental import pallas as pl
from jax.experimental.pallas import tpu as pltpu
from jax.sharding import PartitionSpec as P

SCALE = 1024.0
VMEM = 40 * 2**20


def contract_rows(left, right):
    return lax.dot_general(
        left, right, (((0,), (0,)), ((), ())), preferred_element_type=jnp.float32
    )


def exact_dot(left, right):
    return jnp.dot(left, right, precision=lax.Precision.HIGHEST, preferred_element_type=jnp.float32)


def squared(value):
    return (value * jnp.abs(value) * SCALE).astype(jnp.float16)


def rooted(code):
    code = code.astype(jnp.float32) * (1.0 / SCALE)
    root = jnp.sqrt(jnp.abs(code))
    return jnp.where(code < 0, -root, root)


def xor_order(items, index):
    bit = 1
    while bit < len(items):
        odd = (index & bit) != 0
        items = [jnp.where(odd, items[k ^ bit], items[k]) for k in range(len(items))]
        bit *= 2
    return items


def together(*values):
    return lax.optimization_barrier(values)


def long_op():
    return pl.CostEstimate(flops=10**12, bytes_accessed=2**20, transcendentals=0)


def short_op():
    return pl.CostEstimate(flops=2**10, bytes_accessed=2**10, transcendentals=0)


def anchor_kernel(source, out):
    out[...] = source[...]


def anchor(value):
    return pl.pallas_call(
        anchor_kernel, out_shape=jax.ShapeDtypeStruct(value.shape, value.dtype), cost_estimate=long_op()
    )(value)


def tile_of(extent):
    return next(size for size in (512, 896, 256, 128, extent) if extent % size == 0)


def multiply_kernel(n_tokens, *refs):
    out = refs[-1]

    @pl.when(pl.program_id(0) == 0)
    def _():
        out[...] = jnp.zeros_like(out)

    left = jnp.concatenate([r[...] for r in refs[:n_tokens]], axis=0)
    right = jnp.concatenate([r[...] for r in refs[n_tokens:-1]], axis=0)
    out[...] += lax.dot_general(left, right, (((1,), (1,)), ((), ())), preferred_element_type=jnp.float32)


def multiply(tokens, rows):
    width = tokens[0].shape[1]
    tile = tile_of(width)
    height = sum(value.shape[0] for value in tokens)
    extent = sum(value.shape[0] for value in rows)
    return pl.pallas_call(
        functools.partial(multiply_kernel, len(tokens)),
        grid=(width // tile,),
        in_specs=[pl.BlockSpec((value.shape[0], tile), lambda k: (0, k)) for value in tokens + rows],
        out_specs=pl.BlockSpec((height, extent), lambda k: (0, 0)),
        out_shape=jax.ShapeDtypeStruct((height, extent), jnp.float32),
        compiler_params=pltpu.CompilerParams(vmem_limit_bytes=VMEM),
        cost_estimate=short_op(),
    )(*tokens, *rows)


def gradient_kernel(counts, place, *refs):
    keep, send = refs[-2:]
    total, at = None, len(counts)
    for saved, count in zip(refs, counts):
        block = jnp.concatenate([r[...] for r in refs[at : at + count]], axis=0)
        at += count
        product = jnp.dot(saved[...], block, preferred_element_type=jnp.float32)
        total = product if total is None else total + product
    middle = keep.shape[0]
    keep[...] = total[:middle]
    send[...] = total[middle:]


def gradient_part(saved, tokens, place, part):
    rank, depth = saved[0].shape
    if part % 128:
        total = 0.0
        for value, pieces in zip(saved, tokens):
            block = jnp.concatenate(pieces, axis=0)
            block = lax.dynamic_slice(block, (0, place * part), (depth, part))
            total = total + jnp.dot(value, block, preferred_element_type=jnp.float32)
        return total[: rank // 2], total[rank // 2 :]
    tile = part // 2 if part % 256 == 0 else part
    steps = part // tile
    flat = [value for pieces in tokens for value in pieces]
    return pl.pallas_call(
        functools.partial(gradient_kernel, [len(pieces) for pieces in tokens]),
        grid_spec=pltpu.PrefetchScalarGridSpec(
            num_scalar_prefetch=1,
            grid=(steps,),
            in_specs=[pl.BlockSpec((rank, depth), lambda i, p: (0, 0))] * len(saved)
            + [pl.BlockSpec((value.shape[0], tile), lambda i, p: (0, p[0] * steps + i)) for value in flat],
            out_specs=[pl.BlockSpec((rank // 2, tile), lambda i, p: (0, i))] * 2,
        ),
        out_shape=[jax.ShapeDtypeStruct((rank // 2, part), jnp.float32)] * 2,
        compiler_params=pltpu.CompilerParams(vmem_limit_bytes=VMEM),
        cost_estimate=short_op(),
    )(place.reshape(1), *saved, *flat)


def blend_kernel(na, group, rot_first, rot_second, gradient, *outs):
    rows = outs[0].shape[1]
    for j in range(na):
        mine = pl.ds(pl.multiple_of((group[0] ^ j) * rows, rows), rows)
        g = gradient[mine, :]
        outs[j][0] = 0.9 * rot_first[mine, :] + 0.1 * g
        outs[j][1] = 0.95 * rot_second[mine, :] + 0.05 * g * g


def blend(rot_first, rot_second, gradient, group, na):
    height, part = gradient.shape
    rows = height // na
    if rows % 8 or part % 128:
        first = 0.9 * rot_first + 0.1 * gradient
        second = 0.95 * rot_second + 0.05 * gradient * gradient
        both = jnp.stack([first, second]).reshape(2, na, rows, part)
        return xor_order([both[:, k] for k in range(na)], group)
    whole = pl.BlockSpec((height, part), lambda i, g: (0, 0))
    return pl.pallas_call(
        functools.partial(blend_kernel, na),
        grid_spec=pltpu.PrefetchScalarGridSpec(
            num_scalar_prefetch=1,
            grid=(1,),
            in_specs=[whole] * 3,
            out_specs=[pl.BlockSpec((2, rows, part), lambda i, g: (0, 0, 0))] * na,
        ),
        out_shape=[jax.ShapeDtypeStruct((2, rows, part), jnp.float32)] * na,
        compiler_params=pltpu.CompilerParams(vmem_limit_bytes=VMEM),
        cost_estimate=short_op(),
    )(group.reshape(1), rot_first, rot_second, gradient)


def finish_kernel(na, group, *refs):
    first, second, update = refs[na:]
    part = refs[0].shape[2]
    for j in range(na):
        mine = pl.ds(pl.multiple_of((group[0] ^ j) * part, 128), part)
        f, v = refs[j][0], refs[j][1]
        first[:, mine] = f
        second[:, mine] = v
        update[:, mine] = f / (jnp.sqrt(v) + 1e-08)


def finish(pieces, group):
    na = len(pieces)
    _, rows, part = pieces[0].shape
    if part % 128:
        both = jnp.concatenate(xor_order(pieces, group), axis=2)
        return both[0], both[1], both[0] / (jnp.sqrt(both[1]) + 1e-08)
    return pl.pallas_call(
        functools.partial(finish_kernel, na),
        grid_spec=pltpu.PrefetchScalarGridSpec(
            num_scalar_prefetch=1,
            grid=(1,),
            in_specs=[pl.BlockSpec((2, rows, part), lambda i, g: (0, 0, 0))] * na,
            out_specs=[pl.BlockSpec((rows, na * part), lambda i, g: (0, 0))] * 3,
        ),
        out_shape=[jax.ShapeDtypeStruct((rows, na * part), jnp.float32)] * 3,
        compiler_params=pltpu.CompilerParams(vmem_limit_bytes=VMEM),
        cost_estimate=short_op(),
    )(group.reshape(1), *pieces)


def place_kernel(na, place, *refs):
    out = refs[na]
    extent = refs[0].shape[1] // 2
    for j in range(na):
        for core in range(2):
            mine = pl.ds(pl.multiple_of((place[0] ^ (2 * j + core)) * extent, 128), extent)
            out[:, mine] = refs[j][:, core * extent : (core + 1) * extent]


def place_columns(pieces, place):
    na = len(pieces)
    tokens, extent = pieces[0].shape
    if extent % 256:
        halves = [p[:, k * extent // 2 : (k + 1) * extent // 2] for p in pieces for k in range(2)]
        return jnp.concatenate(xor_order(halves, place), axis=1)
    return pl.pallas_call(
        functools.partial(place_kernel, na),
        grid_spec=pltpu.PrefetchScalarGridSpec(
            num_scalar_prefetch=1,
            grid=(1,),
            in_specs=[pl.BlockSpec((tokens, extent), lambda i, g: (0, 0))] * na,
            out_specs=pl.BlockSpec((tokens, na * extent), lambda i, g: (0, 0)),
        ),
        out_shape=jax.ShapeDtypeStruct((tokens, na * extent), jnp.float32),
        compiler_params=pltpu.CompilerParams(vmem_limit_bytes=VMEM),
        cost_estimate=short_op(),
    )(place.reshape(1), *pieces)


def make_step(n, t):
    na = n // (2 * t)
    top_unit = 2 * na
    strides = [2**b for b in reversed(range(na.bit_length() - 1))]

    def swap(value, mask):
        return lax.ppermute(value, "seq", [(s, s ^ mask) for s in range(n)])

    def swap_tp(value, mask):
        return lax.ppermute(value, "tp", [(s, s ^ mask) for s in range(t)])

    def scatter(items, index, unit):
        items = xor_order(items, index)
        total = items[0]
        for k in range(1, len(items)):
            total = total + swap(items[k], k * unit)
        return total

    def per_device(grad_out, weight, saved, first_moment, second_moment, basis, new_basis):
        s, x = lax.axis_index("seq"), lax.axis_index("tp")
        core, group, top = s & 1, (s // 2) & (na - 1), s // top_unit
        tokens, width = grad_out.shape
        rows = first_moment.shape[0]
        part = width // na
        rank = saved.shape[1]
        drows = weight.shape[0]
        tops = range(1, t)

        def pieces_of(value):
            cuts = [0, value.shape[0] // 2, value.shape[0] * 3 // 4, value.shape[0]]
            return [value[lo:hi] for lo, hi in zip(cuts[:-1], cuts[1:])]

        last, others = strides[0], strides[1:]
        token_cuts, weight_cuts = pieces_of(grad_out), pieces_of(weight)
        a = {(0, p): token_cuts[p] for p in range(3)}
        w = {}

        def send_weight(value, p):
            for dz in tops:
                w[dz, p] = swap(value, dz * top_unit)

        def settle(p, *values):
            keys_a = [k for k in a if k[1] == p and k[0] != 0]
            keys_w = [k for k in w if k[1] == p]
            held, values = together([a[k] for k in keys_a] + [w[k] for k in keys_w], values)
            for k, v in zip(keys_a, held):
                a[k] = v
            for k, v in zip(keys_w, held[len(keys_a) :]):
                w[k] = v
            return values

        a[last, 0] = swap(token_cuts[0], 2 * last)
        send_weight(weight_cuts[0], 0)
        for bit in others:
            a[bit, 0] = swap(grad_out, 2 * bit)
        w_core = swap(weight, 1)
        ticket = anchor(jnp.full((8, 128), group, jnp.int32))
        ticket, first_moment, second_moment, new_basis, saved = together(
            ticket, first_moment, second_moment, new_basis, saved
        )

        both = squared(jnp.stack([first_moment, second_moment])).reshape(2, rows, na, part)
        near = xor_order([both[:, :, k] for k in range(na)], group)

        local = contract_rows(new_basis, basis).reshape(t, na, 2, rows, rank)
        local = scatter([local[:, :, 0], local[:, :, 1]], core, 1)
        local = xor_order([local[:, k] for k in range(na)], group)

        saved = saved.reshape(tokens, t, na, 2, rows)
        saved = jnp.stack(xor_order([saved[:, :, :, k] for k in range(2)], core), axis=1)
        saved = jnp.stack(xor_order([saved[:, :, k] for k in range(t)], top), axis=2)
        saved_t = saved.reshape(tokens, rank).T

        ticket, near, local, saved_t, more_tokens, more_weight = settle(
            0, ticket, near, local, saved_t, token_cuts[1], weight_cuts[1]
        )
        near = [near[0]] + [swap(near[j], 2 * j) for j in range(1, na)]
        local = [local[0]] + [swap(local[j], 2 * j) for j in range(1, na)]

        def forward(p):
            for bit in others:
                for j in [k[0] for k in a if k[1] == p and k[0] & last and not k[0] & bit]:
                    a[j | bit, p] = swap(a[j, p], 2 * bit)

        forward(0)
        a[last, 1] = swap(more_tokens, 2 * last)
        send_weight(more_weight, 1)
        saved_all = [saved_t if j == 0 else swap(saved_t, 2 * j) for j in range(na)]
        ticket = anchor(ticket)
        group = ticket[0, 0]
        ticket, local, near, own_rows = together(ticket, local, near, [weight, w_core])
        local = functools.reduce(jnp.add, local)
        near = jnp.concatenate(near, axis=1)
        near_other = swap(near, 1)

        ticket, local, near, more_tokens, more_weight = settle(1, ticket, local, near, token_cuts[2], weight_cuts[2])
        forward(1)
        a[last, 2] = swap(more_tokens, 2 * last)
        send_weight(more_weight, 2)
        far = {dz: swap(near, dz * top_unit) for dz in tops}
        ticket = anchor(ticket)
        group_late = ticket[0, 0]
        ticket, local = together(ticket, local)

        (ticket,) = settle(2, ticket)
        forward(2)

        def blocks_of(j):
            if j == 0:
                return [grad_out]
            return [a[j, p] for p in range(3) if (j, p) in a]

        own = scatter([local[k] for k in range(t)], top, top_unit)

        moments = [rooted(jnp.concatenate([near, near_other], axis=1))]
        for dz in tops:
            moments.append(rooted(jnp.concatenate([far[dz], swap(far[dz], 1)], axis=1)))

        inter = jnp.stack(
            xor_order([own] + [swap(own, 2 * j) for j in range(1, na)], group), axis=0
        ).reshape(na * rows, t, na, 2, rows)
        inter = xor_order([inter[:, k] for k in range(t)], top)
        rot_first = rot_second = None
        for dz in range(t):
            part_of = jnp.stack(xor_order([inter[dz][:, :, k] for k in range(2)], core), axis=1)
            part_of = jnp.stack(xor_order([part_of[:, :, k] for k in range(na)], group), axis=2)
            part_of = part_of.reshape(na * rows, 2 * na * rows)
            f = exact_dot(part_of, moments[dz][0])
            v = exact_dot(part_of * part_of, moments[dz][1])
            rot_first = f if dz == 0 else rot_first + f
            rot_second = v if dz == 0 else rot_second + v

        keep, send = gradient_part(saved_all, [blocks_of(j) for j in range(na)], group, part)
        g = (keep + swap(send, 1)).reshape(t, na * rows, part)
        gradient = g[0]
        for dz in tops:
            gradient = gradient + swap(g[dz].astype(jnp.float16), dz * top_unit).astype(jnp.float32)

        pieces = blend(rot_first, rot_second, gradient, group_late, na)
        pieces = [pieces[0]] + [swap(pieces[j], 2 * j) for j in range(1, na)]
        first_new, second_new, update = finish(pieces, group)

        other_rows = {dz: [w[dz, p] for p in range(3)] + [swap(w[dz, p], 1) for p in range(3)] for dz in tops}
        sums = [None] * na
        near_tokens = [j for j in range(na) if not j & last]
        for some in [near_tokens] + [[j] for j in range(na) if j & last]:
            block = [value for j in some for value in blocks_of(j)]
            by_top = [multiply(block, own_rows)] + [multiply(block, other_rows[dz]) for dz in tops]
            for i, j in enumerate(some):
                rel = xor_order([c[i * tokens : (i + 1) * tokens] for c in by_top], top ^ x)
                total = rel[0]
                for e in tops:
                    total = total + swap_tp(rel[e], e)
                sums[j] = swap(total, 2 * j) if j else total
        grad_input = place_columns(sums, 2 * group + core)
        return (grad_input, first_new, second_new, update)

    return per_device


def solution(mesh):
    return jax.shard_map(
        make_step(mesh.shape["seq"], mesh.shape["tp"]),
        mesh=mesh,
        in_specs=(
            P("seq", "tp"),
            P("seq", "tp"),
            P("seq", None),
            P("seq", "tp"),
            P("seq", "tp"),
            P("seq", None),
            P("seq", None),
        ),
        out_specs=(P("seq", "tp"), P("seq", "tp"), P("seq", "tp"), P("seq", "tp")),
        check_vma=False,
    )
```

time: 805 us -> 412 us (0.51)
  waiting for transfers between devices: 726 us -> 206 us
  Pallas kernels: 0 us -> 84.1 us
  matrix products: 64.2 us -> 4.66 us
  starting transfers between devices: 0.42 us -> 43.6 us
  local copies, waits for them, and re-layouts: 0.03 us -> 37.2 us
  other arithmetic: 0 us -> 31.2 us
  between operations: 14.2 us -> 3.24 us
    all_gather x3 -> x0, waiting for transfers between devices: 495 us -> none  [the longest x1 277 us: per_device(): lax.all_gather(weight, 'seq', axis=0, tiled=True)]
    reduce_scatter x3 -> x0, waiting for transfers between devices: 230 us -> none  [the longest x1 153 us: per_device(): lax.psum_scatter(contract_rows(saved, grad_out), 'seq', scatter_dimension...]
    ppermute x0 -> x43, waiting for transfers between devices: none -> 206 us  [the longest x39 204 us: swap(): return lax.ppermute(value, 'seq', [(s, s ^ mask) for s in range(n)])]
    pallas_call x0 -> x13, Pallas kernels: none -> 84.1 us  [the longest x6 65.4 us: multiply(): pl.pallas_call(functools.partial(multiply_kernel, len(tokens)), grid=(wid...]
    ppermute x0 -> x43, starting transfers between devices: none -> 43.6 us  [the longest x39 39.1 us: swap(): return lax.ppermute(value, 'seq', [(s, s ^ mask) for s in range(n)])]
    dot_general x1 -> x0, matrix products: 26.5 us -> none  [per_device(): lax.dot_general(grad_out, lax.all_gather(weight, 'seq', axis=0, tiled=Tru...]
    dot_general x2 -> x4, matrix products: 25 us -> 4.34 us  [exact_dot(): jnp.dot(left, right, precision=lax.Precision.HIGHEST, preferred_element_t...]
    select_n x0 -> x20, other arithmetic: none -> 17.9 us  [the longest x18 14.6 us: xor_order(): jnp.where(odd, items[k ^ bit], items[k])]
  transfers between devices with their start and end apart: 6 -> 43, of which waited for: 6 -> 19; matrix products, arithmetic and copies ran while one was open for 8% -> 16% of each run, Pallas kernels for 0% -> 19%
where the time goes in v2:
time: 412 us; the launch traced here: 410 us
  waiting for transfers between devices  206 us (50%)
  Pallas kernels  84.1 us (20%)
  starting transfers between devices  43.6 us (11%)
  local copies, waits for them, and re-layouts  37.2 us (9%)
  other arithmetic  31.2 us (8%)
  matrix products  4.66 us (1%)
    ppermute x39, waiting for transfers between devices, swap(): return lax.ppermute(value, 'seq', [(s, s ^ mask) for s in range(n)])  204 us
    pallas_call x6, Pallas kernels, multiply(): pl.pallas_call(functools.partial(multiply_kernel, len(tokens)), grid=(wid...  65.4 us
    ppermute x39, starting transfers between devices, swap(): return lax.ppermute(value, 'seq', [(s, s ^ mask) for s in range(n)])  39.1 us
    select_n x18, other arithmetic, xor_order(): jnp.where(odd, items[k ^ bit], items[k])  14.6 us
    unnamed x72, local copies, waits for them, and re-layouts  13.1 us
    slice x3, local copies, waits for them, and re-layouts, pieces_of(): return [value[lo:hi] for lo, hi in zip(cuts[:-1], cuts[1:])]  9.75 us
  transfers between devices with their start and end apart: 43, of which 19 were waited for; matrix products, arithmetic and copies ran while one was open for 16% of the time, Pallas kernels for 19%

profile of v2, /device:TPU:0, one launch (start us, length us, event | category | flops | bytes accessed | tf_op | source)
XLA Modules:
  0.0 409.6 jit_solution(1865511592389238945)
XLA Ops:
  0.6 3.0 collective-permute-start.1
  3.7 2.9 slice.147
  6.6 1.6 collective-permute-start
  8.2 2.8 slice.148
  11.0 2.6 collective-permute-start.2
  14.2 1.3 shard_map.102.source
  20.6 2.2 fusion.3
  22.9 3.8 broadcast_select_fusion.4
  26.8 4.0 fusion.25
  35.4 48.1 %collective-permute-done.refs_0_.refs_6_ = bf16[128,7168]{1,0:T(8,128)(2,1)} collective-permute-done((bf16[128,7168]{1,0:T(8,128)(2,1)}, bf16[128,7168]{1,0:T(8,128)(2,1)}, u32[]{:S(2)}, u32[]{:S(2)}) %collective-permute-start) | collective-permute-done | bytes 1835040 | tf_op jit(solution)/shard_map/ppermute | solution.py:235
  83.5 10.5 %collective-permute-done.2.refs_2_.refs_3_ = bf16[128,7168]{1,0:T(8,128)(2,1)} collective-permute-done((bf16[128,7168]{1,0:T(8,128)(2,1)}, bf16[128,7168]{1,0:T(8,128)(2,1)}, u32[]{:S(2)}, u32[]{:S(2)}) %collective-permute-start.2) | collective-permute-done | bytes 1835040 | tf_op jit(solution)/shard_map/ppermute | solution.py:235
  94.5 3.0 collective-permute-start.8
  99.8 1.8 collective-permute-start.11
  101.7 1.4 shard_map.103.source
  103.3 1.8 collective-permute-done.8
  107.0 21.7 %collective-permute-done.10 = f16[2,32,1792]{2,1,0:T(8,128)(2,1)} collective-permute-done((f16[2,32,1792]{2,1,0:T(8,128)(2,1)}, f16[2,32,1792]{2,1,0:T(8,128)(2,1)}, u32[]{:S(2)}, u32[]{:S(2)}) %collective-permute-start.10) | collective-permute-done | bytes 229408 | tf_op jit(solution)/shard_map/ppermute | solution.py:235
  128.7 5.9 %collective-permute-done.11 = f16[2,32,1792]{2,1,0:T(8,128)(2,1)} collective-permute-done((f16[2,32,1792]{2,1,0:T(8,128)(2,1)}, f16[2,32,1792]{2,1,0:T(8,128)(2,1)}, u32[]{:S(2)}, u32[]{:S(2)}) %collective-permute-start.11) | collective-permute-done | bytes 229408 | tf_op jit(solution)/shard_map/ppermute | solution.py:235
  137.6 2.0 add_add_fusion
  139.6 12.1 %collective-permute-done.4.refs_1_.refs_7_ = bf16[64,7168]{1,0:T(8,128)(2,1)} collective-permute-done((bf16[64,7168]{1,0:T(8,128)(2,1)S(1)}, bf16[64,7168]{1,0:T(8,128)(2,1)}, u32[]{:S(2)}, u32[]{:S(2)}) %collective-permute-start.4) | collective-permute-done | bytes 917536 | tf_op jit(solution)/shard_map/ppermute | solution.py:235
  151.7 1.3 shard_map.111
  153.0 1.3 collective-permute-start.28
  154.3 4.0 collective-permute-done.28
  158.3 2.3 collective-permute-start.29
  161.8 1.2 slice.165
  163.1 1.5 collective-permute-start.35
  164.6 1.3 collective-permute-start.36
  167.2 2.0 copy-done.2
  169.3 12.2 %shard_map.105 = f32[512,512]{1,0:T(8,128)S(1)} custom-call(bf16[256,7168]{1,0:T(8,128)(2,1)S(1)} %copy-done.2, bf16[256,7168]{1,0:T(8,128)(2,1)} %collective-permute-done.1.refs_1_.refs_5_, bf16[256,7168]{1,0:T(8,128)(2,1)} %refs_3_.1, bf16[256,7168]{1,0:T(8,128)(2,1)} %collective-permute-done.12.refs_3_.refs_4_), custom_call_target="tpu_custom_call" | custom-call | flops 1024 | bytes 1024 | tf_op jit(solution)/shard_map/pallas_call | solution.py:86
  183.4 1.5 collective-permute-start.23
  184.9 1.3 collective-permute-start.13
  187.8 2.8 reshape.225
  190.6 1.6 fusion.7
  193.3 2.1 collective-permute-start.14
  198.6 2.5 broadcast_select_fusion.9
  201.1 1.7 copy.175
  202.8 1.7 copy.174
  204.5 1.3 collective-permute-done.37.refs_3_
  205.8 16.9 %collective-permute-done.13.refs_2_.refs_8_ = bf16[64,7168]{1,0:T(8,128)(2,1)} collective-permute-done((bf16[64,7168]{1,0:T(8,128)(2,1)}, bf16[64,7168]{1,0:T(8,128)(2,1)}, u32[]{:S(2)}, u32[]{:S(2)}) %collective-permute-start.13) | collective-permute-done | bytes 917536 | tf_op jit(solution)/shard_map/ppermute | solution.py:235
  222.7 2.9 collective-permute-start.24
  226.5 19.0 %collective-permute-done.14.refs_4_.refs_5_ = bf16[64,7168]{1,0:T(8,128)(2,1)} collective-permute-done((bf16[64,7168]{1,0:T(8,128)(2,1)}, bf16[64,7168]{1,0:T(8,128)(2,1)}, u32[]{:S(2)}, u32[]{:S(2)}) %collective-permute-start.14) | collective-permute-done | bytes 917536 | tf_op jit(solution)/shard_map/ppermute | solution.py:235
  247.5 1.7 negate_select_fusion.1
  250.2 20.9 %collective-permute-done.33 = f16[2,128,1792]{2,1,0:T(8,128)(2,1)S(1)} collective-permute-done((f16[2,128,1792]{2,1,0:T(8,128)(2,1)}, f16[2,128,1792]{2,1,0:T(8,128)(2,1)S(1)}, u32[]{:S(2)}, u32[]{:S(2)}) %collective-permute-start.33) | collective-permute-done | bytes 917536 | tf_op jit(solution)/shard_map/ppermute | solution.py:235
  272.2 11.3 %shard_map.107 = f32[256,512]{1,0:T(8,128)S(1)} custom-call(bf16[128,7168]{1,0:T(8,128)(2,1)} %collective-permute-done.refs_0_.refs_6_, bf16[64,7168]{1,0:T(8,128)(2,1)} %collective-permute-done.4.refs_1_.refs_7_, bf16[64,7168]{1,0:T(8,128)(2,1)} %collective-permute-done.13.refs_2_.refs_8_, bf16[256,7168]{1,0:T(8,128)(2,1)} %refs_3_.1, ...), custom_call_target="tpu_custom_call" | custom-call | flops 1024 | bytes 1024 | tf_op jit(solution)/shard_map/pallas_call | solution.py:86
  284.3 6.2 %shard_map.112 = (f32[256,1792]{1,0:T(8,128)S(1)}, f32[256,1792]{1,0:T(8,128)}) custom-call(s32[1]{0:T(128)} %bitcast.17.place.group, bf16[512,256]{1,0:T(8,128)(2,1)S(1)} %bitcast.104, bf16[512,256]{1,0:T(8,128)(2,1)S(1)} %collective-permute-done.35.refs_1_, bf16[512,256]{1,0:T(8,128)(2,1)} %collective-permute-done.36.refs_2_, ...), custom_call_target="tpu_custom_call" | custom-call | flops 1024 | bytes 1024 | tf_op jit(solution)/shard_map/pallas_call | solution.py:122
  290.5 1.3 copy-done.11
  294.4 11.4 %shard_map.104 = f32[512,512]{1,0:T(8,128)S(1)} custom-call(bf16[256,7168]{1,0:T(8,128)(2,1)S(1)} %copy-done.3, bf16[256,7168]{1,0:T(8,128)(2,1)} %collective-permute-done.1.refs_1_.refs_5_, bf16[128,7168]{1,0:T(8,128)(2,1)} %collective-permute-done.2.refs_2_.refs_3_, bf16[64,7168]{1,0:T(8,128)(2,1)} %collective-permute-done.5.refs_3_.refs_4_, ...), custom_call_target="tpu_custom_call" | custom-call | flops 1024 | bytes 1024 | tf_op jit(solution)/shard_map/pallas_call | solution.py:86
  306.7 1.5 collective-permute-start.19
  308.2 10.2 %shard_map.106 = f32[256,512]{1,0:T(8,128)S(1)} custom-call(bf16[128,7168]{1,0:T(8,128)(2,1)} %collective-permute-done.refs_0_.refs_6_, bf16[64,7168]{1,0:T(8,128)(2,1)} %collective-permute-done.4.refs_1_.refs_7_, bf16[64,7168]{1,0:T(8,128)(2,1)} %collective-permute-done.13.refs_2_.refs_8_, bf16[128,7168]{1,0:T(8,128)(2,1)} %collective-permute-done.2.refs_2_.refs_3_, ...), custom_call_target="tpu_custom_call" | custom-call | flops 1024 | bytes 1024 | tf_op jit(solution)/shard_map/pallas_call | solution.py:86
  320.2 10.4 %shard_map.109 = f32[256,512]{1,0:T(8,128)S(1)} custom-call(bf16[128,7168]{1,0:T(8,128)(2,1)S(1)} %collective-permute-done.23.refs_0_.refs_9_, bf16[64,7168]{1,0:T(8,128)(2,1)S(1)} %collective-permute-done.24.refs_1_.refs_10_, bf16[64,7168]{1,0:T(8,128)(2,1)S(1)} %collective-permute-done.25.refs_2_.refs_11_, bf16[256,7168]{1,0:T(8,128)(2,1)} %refs_3_.1, ...), custom_call_target="tpu_custom_call" | custom-call | flops 1024 | bytes 1024 | tf_op jit(solution)/shard_map/pallas_call | solution.py:86
  330.6 9.9 %shard_map.108 = f32[256,512]{1,0:T(8,128)S(1)} custom-call(bf16[128,7168]{1,0:T(8,128)(2,1)S(1)} %collective-permute-done.23.refs_0_.refs_9_, bf16[64,7168]{1,0:T(8,128)(2,1)S(1)} %collective-permute-done.24.refs_1_.refs_10_, bf16[64,7168]{1,0:T(8,128)(2,1)S(1)} %collective-permute-done.25.refs_2_.refs_11_, ...), custom_call_target="tpu_custom_call" | custom-call | flops 1024 | bytes 1024 | tf_op jit(solution)/shard_map/pallas_call | solution.py:86
  341.8 1.7 negate_select_fusion
  345.7 1.5 select_add_fusion.2
  348.8 2.0 select_add_fusion.1
  350.8 2.6 collective-permute-start.22
  353.4 2.1 collective-permute-done.26
  356.4 13.9 %collective-permute-done.39 = f16[128,1792]{1,0:T(8,128)(2,1)S(1)} collective-permute-done((f16[128,1792]{1,0:T(8,128)(2,1)S(1)}, f16[128,1792]{1,0:T(8,128)(2,1)S(1)}, u32[]{:S(2)}, u32[]{:S(2)}) %collective-permute-start.39) | collective-permute-done | bytes 458784 | tf_op jit(solution)/shard_map/ppermute | solution.py:235
  370.4 2.0 shard_map.113
  373.2 1.4 collective-permute-start.40
  374.6 2.1 collective-permute-start.42
  377.5 10.8 %collective-permute-done.27.refs_3_ = f32[256,512]{1,0:T(8,128)} collective-permute-done((f32[256,512]{1,0:T(8,128)}, f32[256,512]{1,0:T(8,128)}, u32[]{:S(2)}, u32[]{:S(2)}) %collective-permute-start.27) | collective-permute-done | bytes 524320 | tf_op jit(solution)/shard_map/ppermute | solution.py:235
  388.4 2.8 shard_map.110
  391.1 5.9 %collective-permute-done.40.refs_1_ = f32[2,32,1792]{2,1,0:T(8,128)} collective-permute-done((f32[2,32,1792]{2,1,0:T(8,128)}, f32[2,32,1792]{2,1,0:T(8,128)}, u32[]{:S(2)}, u32[]{:S(2)}) %collective-permute-start.40) | collective-permute-done | bytes 458784 | tf_op jit(solution)/shard_map/ppermute | solution.py:235
  397.4 8.5 %collective-permute-done.42.refs_3_ = f32[2,32,1792]{2,1,0:T(8,128)} collective-permute-done((f32[2,32,1792]{2,1,0:T(8,128)}, f32[2,32,1792]{2,1,0:T(8,128)}, u32[]{:S(2)}, u32[]{:S(2)}) %collective-permute-start.42) | collective-permute-done | bytes 458784 | tf_op jit(solution)/shard_map/ppermute | solution.py:235
  405.9 3.8 shard_map.114
  (165 shorter events, 46.0 us)
Async XLA Ops:
  0.6 14.9 %copy-start = (bf16[256,512]{1,0:T(8,128)(2,1)S(1)}, bf16[256,512]{1,0:T(8,128)(2,1)}, u32[]{:S(2)}) copy-start(bf16[256,512]{1,0:T(8,128)(2,1)} %param.13) | copy-start | bytes 786436
  0.6 93.4 %collective-permute-start.1 = (bf16[256,7168]{1,0:T(8,128)(2,1)}, bf16[256,7168]{1,0:T(8,128)(2,1)}, u32[]{:S(2)}, u32[]{:S(2)}) collective-permute-start(bf16[256,7168]{1,0:T(8,128)(2,1)} %refs_4_.1), channel_id=1, source_target_pairs={{0,4},{2,6},{4,0},{6,2},{8,12},{10,14},{12,8},{14,10},{16,20},{18,... | collective-permute-start | bytes 11010056 | tf_op jit(solution)/shard_map/ppermute | solution.py:235
  6.6 76.9 %collective-permute-start = (bf16[128,7168]{1,0:T(8,128)(2,1)}, bf16[128,7168]{1,0:T(8,128)(2,1)}, u32[]{:S(2)}, u32[]{:S(2)}) collective-permute-start(bf16[128,7168]{1,0:T(8,128)(2,1)} %slice.147), channel_id=1, source_target_pairs={{0,8},{2,10},{4,12},{6,14},{8,0},{10,2},{12,4},{14,6},{16,24},{18,... | collective-permute-start | bytes 5505032 | tf_op jit(solution)/shard_map/ppermute | solution.py:235
  8.2 89.9 %collective-permute-start.12 = (bf16[256,7168]{1,0:T(8,128)(2,1)}, bf16[256,7168]{1,0:T(8,128)(2,1)}, u32[]{:S(2)}, u32[]{:S(2)}) collective-permute-start(bf16[256,7168]{1,0:T(8,128)(2,1)} %refs_3_.1), channel_id=1, source_target_pairs={{0,2},{2,0},{4,6},{6,4},{8,10},{10,8},{12,14},{14,12},{16,18},{18,... | collective-permute-start | bytes 11010056 | tf_op jit(solution)/shard_map/ppermute | solution.py:235
  11.0 83.0 %collective-permute-start.2 = (bf16[128,7168]{1,0:T(8,128)(2,1)}, bf16[128,7168]{1,0:T(8,128)(2,1)}, u32[]{:S(2)}, u32[]{:S(2)}) collective-permute-start(bf16[128,7168]{1,0:T(8,128)(2,1)} %slice.148), channel_id=1, source_target_pairs={{0,16},{2,18},{4,20},{6,22},{8,24},{10,26},{12,28},{14,30},{16,0},... | collective-permute-start | bytes 5505032 | tf_op jit(solution)/shard_map/ppermute | solution.py:235
  16.9 16.5 %collective-permute-start.3 = (f32[2,4,32,512]{3,2,0,1:T(8,128)}, f32[2,4,32,512]{3,2,0,1:T(8,128)}, u32[]{:S(2)}, u32[]{:S(2)}) collective-permute-start(f32[2,4,32,512]{3,2,0,1:T(8,128)} %select_bitcast_fusion), channel_id=1, source_target_pairs={{0,2},{2,0},{4,6},{6,4},{8,10},{10,8},{12,14},{14,12},{16,18},{18,... | collective-permute-start | bytes 1572872 | tf_op jit(solution)/shard_map/ppermute | solution.py:235
  20.6 2.2 copy-start.29
  26.7 4.1 copy-start.17
  26.8 4.1 copy-start.18
  94.0 5.1 %collective-permute-start.6 = (f32[2,32,512]{2,1,0:T(8,128)S(1)}, f32[2,32,512]{2,1,0:T(8,128)S(1)}, u32[]{:S(2)}, u32[]{:S(2)}) collective-permute-start(f32[2,32,512]{2,1,0:T(8,128)S(1)} %get-tuple-element.65), channel_id=1, source_target_pairs={{0,4},{2,6},{4,0},{6,2},{8,12},{10,14},{12,8},{14,10},{16,20},{18,... | collective-permute-start | bytes 393224 | tf_op jit(solution)/shard_map/ppermute | solution.py:235
  94.5 8.5 %collective-permute-start.7 = (f32[2,32,512]{2,1,0:T(8,128)}, f32[2,32,512]{2,1,0:T(8,128)}, u32[]{:S(2)}, u32[]{:S(2)}) collective-permute-start(f32[2,32,512]{2,1,0:T(8,128)} %get-tuple-element.66), channel_id=1, source_target_pairs={{0,8},{2,10},{4,12},{6,14},{8,0},{10,2},{12,4},{14,6},{16,24},{18,... | collective-permute-start | bytes 393224 | tf_op jit(solution)/shard_map/ppermute | solution.py:235
  94.5 10.5 %collective-permute-start.8 = (f32[2,32,512]{2,1,0:T(8,128)}, f32[2,32,512]{2,1,0:T(8,128)}, u32[]{:S(2)}, u32[]{:S(2)}) collective-permute-start(f32[2,32,512]{2,1,0:T(8,128)} %get-tuple-element.67), channel_id=1, source_target_pairs={{0,12},{2,14},{4,8},{6,10},{8,4},{10,6},{12,0},{14,2},{16,28},{18,... | collective-permute-start | bytes 393224 | tf_op jit(solution)/shard_map/ppermute | solution.py:235
  97.5 9.5 %collective-permute-start.9 = (f16[2,32,1792]{2,1,0:T(8,128)(2,1)}, f16[2,32,1792]{2,1,0:T(8,128)(2,1)}, u32[]{:S(2)}, u32[]{:S(2)}) collective-permute-start(f16[2,32,1792]{2,1,0:T(8,128)(2,1)} %get-tuple-element.69), channel_id=1, source_target_pairs={{0,4},{2,6},{4,0},{6,2},{8,12},{10,14},{12,8},{14,10},{16,20},{18,... | collective-permute-start | bytes 688136 | tf_op jit(solution)/shard_map/ppermute | solution.py:235
  98.0 30.6 %collective-permute-start.10 = (f16[2,32,1792]{2,1,0:T(8,128)(2,1)}, f16[2,32,1792]{2,1,0:T(8,128)(2,1)}, u32[]{:S(2)}, u32[]{:S(2)}) collective-permute-start(f16[2,32,1792]{2,1,0:T(8,128)(2,1)} %get-tuple-element.70), channel_id=1, source_target_pairs={{0,8},{2,10},{4,12},{6,14},{8,0},{10,2},{12,4},{14,6},{16,24},{18,... | collective-permute-start | bytes 688136 | tf_op jit(solution)/shard_map/ppermute | solution.py:235
  99.8 34.7 %collective-permute-start.11 = (f16[2,32,1792]{2,1,0:T(8,128)(2,1)}, f16[2,32,1792]{2,1,0:T(8,128)(2,1)}, u32[]{:S(2)}, u32[]{:S(2)}) collective-permute-start(f16[2,32,1792]{2,1,0:T(8,128)(2,1)} %get-tuple-element.71), channel_id=1, source_target_pairs={{0,12},{2,14},{4,8},{6,10},{8,4},{10,6},{12,0},{14,2},{16,28},{18,... | collective-permute-start | bytes 688136 | tf_op jit(solution)/shard_map/ppermute | solution.py:235
  101.7 3.4 copy-start.22
  101.7 32.9 %copy-start.26 = (f16[2,32,1792]{2,1,0:T(8,128)(2,1)S(1)}, f16[2,32,1792]{2,1,0:T(8,128)(2,1)}, u32[]{:S(2)}) copy-start(f16[2,32,1792]{2,1,0:T(8,128)(2,1)} %get-tuple-element.77) | copy-start | bytes 688132
  103.1 34.5 %copy-start.27 = (f32[2,32,512]{2,1,0:T(8,128)S(1)}, f32[2,32,512]{2,1,0:T(8,128)}, u32[]{:S(2)}) copy-start(f32[2,32,512]{2,1,0:T(8,128)} %get-tuple-element.73) | copy-start | bytes 393220
  103.1 34.5 %copy-start.32 = (f32[2,32,512]{2,1,0:T(8,128)S(1)}, f32[2,32,512]{2,1,0:T(8,128)}, u32[]{:S(2)}) copy-start(f32[2,32,512]{2,1,0:T(8,128)} %copy-done.31) | copy-start | bytes 393220
  103.1 48.6 %collective-permute-start.4 = (bf16[64,7168]{1,0:T(8,128)(2,1)S(1)}, bf16[64,7168]{1,0:T(8,128)(2,1)}, u32[]{:S(2)}, u32[]{:S(2)}) collective-permute-start(bf16[64,7168]{1,0:T(8,128)(2,1)S(1)} %copy-done.23), channel_id=1, source_target_pairs={{0,8},{2,10},{4,12},{6,14},{8,0},{10,2},{12,4},{14,6},{16,24},{18,... | collective-permute-start | bytes 2752520 | tf_op jit(solution)/shard_map/ppermute | solution.py:235
  105.1 46.6 %collective-permute-start.5 = (bf16[64,7168]{1,0:T(8,128)(2,1)S(1)}, bf16[64,7168]{1,0:T(8,128)(2,1)}, u32[]{:S(2)}, u32[]{:S(2)}) collective-permute-start(bf16[64,7168]{1,0:T(8,128)(2,1)S(1)} %copy-done.22), channel_id=1, source_target_pairs={{0,16},{2,18},{4,20},{6,22},{8,24},{10,26},{12,28},{14,30},{16,0},... | collective-permute-start | bytes 2752520 | tf_op jit(solution)/shard_map/ppermute | solution.py:235
  137.6 14.1 %copy-start.19 = (f16[2,128,1792]{2,1,0:T(8,128)(2,1)}, f16[2,128,1792]{2,1,0:T(8,128)(2,1)S(1)}, u32[]{:S(2)}) copy-start(f16[2,128,1792]{2,1,0:T(8,128)(2,1)S(1)} %constant_dynamic-update-slice_fusion.2) | copy-start | bytes 2752516
  151.7 11.4 %copy-start.13 = (bf16[256,2,2,4,32]{0,4,3,2,1:T(8,128)(2,1)S(1)}, bf16[256,2,2,4,32]{0,4,3,2,1:T(8,128)(2,1)}, u32[]{:S(2)}) copy-start(bf16[256,2,2,4,32]{0,4,3,2,1:T(8,128)(2,1)} %pad_maximum_fusion) | copy-start | bytes 786436
  153.0 5.2 %collective-permute-start.28 = (f32[32,512]{1,0:T(8,128)S(1)}, f32[32,512]{1,0:T(8,128)S(1)}, u32[]{:S(2)}, u32[]{:S(2)}) collective-permute-start(f32[32,512]{1,0:T(8,128)S(1)} %select_bitcast_fusion.9), channel_id=1, source_target_pairs={{0,16},{2,18},{4,20},{6,22},{8,24},{10,26},{12,28},{14,30},{16,0},... | collective-permute-start | bytes 196616 | tf_op jit(solution)/shard_map/ppermute | solution.py:235
  158.3 24.4 %collective-permute-start.29 = (f32[32,512]{1,0:T(8,128)S(1)}, f32[32,512]{1,0:T(8,128)S(1)}, u32[]{:S(2)}, u32[]{:S(2)}) collective-permute-start(f32[32,512]{1,0:T(8,128)S(1)} %bitcast_add_fusion.1), channel_id=1, source_target_pairs={{0,12},{2,14},{4,8},{6,10},{8,4},{10,6},{12,0},{14,2},{16,28},{18,... | collective-permute-start | bytes 196616 | tf_op jit(solution)/shard_map/ppermute | solution.py:235
  160.6 22.8 %collective-permute-start.30 = (f32[32,512]{1,0:T(8,128)S(1)}, f32[32,512]{1,0:T(8,128)}, u32[]{:S(2)}, u32[]{:S(2)}) collective-permute-start(f32[32,512]{1,0:T(8,128)S(1)} %bitcast_add_fusion.1), channel_id=1, source_target_pairs={{0,8},{2,10},{4,12},{6,14},{8,0},{10,2},{12,4},{14,6},{16,24},{18,... | collective-permute-start | bytes 196616 | tf_op jit(solution)/shard_map/ppermute | solution.py:235
  161.3 23.6 %collective-permute-start.31 = (f32[32,512]{1,0:T(8,128)S(1)}, f32[32,512]{1,0:T(8,128)}, u32[]{:S(2)}, u32[]{:S(2)}) collective-permute-start(f32[32,512]{1,0:T(8,128)S(1)} %bitcast_add_fusion.1), channel_id=1, source_target_pairs={{0,4},{2,6},{4,0},{6,2},{8,12},{10,14},{12,8},{14,10},{16,20},{18,... | collective-permute-start | bytes 196616 | tf_op jit(solution)/shard_map/ppermute | solution.py:235
  163.1 30.2 %collective-permute-start.35 = (bf16[512,256]{1,0:T(8,128)(2,1)S(1)}, bf16[512,256]{1,0:T(8,128)(2,1)S(1)}, u32[]{:S(2)}, u32[]{:S(2)}) collective-permute-start(bf16[512,256]{1,0:T(8,128)(2,1)S(1)} %bitcast.101), channel_id=1, source_target_pairs={{0,4},{2,6},{4,0},{6,2},{8,12},{10,14},{12,8},{14,10},{16,20},{18,... | collective-permute-start | bytes 786440 | tf_op jit(solution)/shard_map/ppermute | solution.py:235
  164.6 39.9 %collective-permute-start.36 = (bf16[512,256]{1,0:T(8,128)(2,1)S(1)}, bf16[512,256]{1,0:T(8,128)(2,1)}, u32[]{:S(2)}, u32[]{:S(2)}) collective-permute-start(bf16[512,256]{1,0:T(8,128)(2,1)S(1)} %bitcast.102), channel_id=1, source_target_pairs={{0,8},{2,10},{4,12},{6,14},{8,0},{10,2},{12,4},{14,6},{16,24},{18,... | collective-permute-start | bytes 786440 | tf_op jit(solution)/shard_map/ppermute | solution.py:235
  167.2 2.0 copy-start.2
  182.7 23.1 %collective-permute-start.37 = (bf16[512,256]{1,0:T(8,128)(2,1)S(1)}, bf16[512,256]{1,0:T(8,128)(2,1)}, u32[]{:S(2)}, u32[]{:S(2)}) collective-permute-start(bf16[512,256]{1,0:T(8,128)(2,1)S(1)} %bitcast.103), channel_id=1, source_target_pairs={{0,12},{2,14},{4,8},{6,10},{8,4},{10,6},{12,0},{14,2},{16,28},{18,... | collective-permute-start | bytes 786440 | tf_op jit(solution)/shard_map/ppermute | solution.py:235
  183.4 62.8 %collective-permute-start.23 = (bf16[128,7168]{1,0:T(8,128)(2,1)}, bf16[128,7168]{1,0:T(8,128)(2,1)S(1)}, u32[]{:S(2)}, u32[]{:S(2)}) collective-permute-start(bf16[128,7168]{1,0:T(8,128)(2,1)} %collective-permute-done.refs_0_.refs_6_), channel_id=1, source_target_pairs={{0,4},{2,6},{4,0},{6,2},{8,12},{10,14},{12,8},{14,10},{16,20},{18,... | collective-permute-start | bytes 5505032 | tf_op jit(solution)/shard_map/ppermute | solution.py:235
  184.9 37.8 %collective-permute-start.13 = (bf16[64,7168]{1,0:T(8,128)(2,1)}, bf16[64,7168]{1,0:T(8,128)(2,1)}, u32[]{:S(2)}, u32[]{:S(2)}) collective-permute-start(bf16[64,7168]{1,0:T(8,128)(2,1)} %get-tuple-element.82), channel_id=1, source_target_pairs={{0,8},{2,10},{4,12},{6,14},{8,0},{10,2},{12,4},{14,6},{16,24},{18,... | collective-permute-start | bytes 2752520 | tf_op jit(solution)/shard_map/ppermute | solution.py:235
  193.3 52.2 %collective-permute-start.14 = (bf16[64,7168]{1,0:T(8,128)(2,1)}, bf16[64,7168]{1,0:T(8,128)(2,1)}, u32[]{:S(2)}, u32[]{:S(2)}) collective-permute-start(bf16[64,7168]{1,0:T(8,128)(2,1)} %get-tuple-element.83), channel_id=1, source_target_pairs={{0,16},{2,18},{4,20},{6,22},{8,24},{10,26},{12,28},{14,30},{16,0},... | collective-permute-start | bytes 2752520 | tf_op jit(solution)/shard_map/ppermute | solution.py:235
  204.5 43.0 %copy-start.20 = (f16[2,128,1792]{2,1,0:T(8,128)(2,1)S(1)}, f16[2,128,1792]{2,1,0:T(8,128)(2,1)}, u32[]{:S(2)}) copy-start(f16[2,128,1792]{2,1,0:T(8,128)(2,1)} %copy-done.19) | copy-start | bytes 2752516
  204.5 87.8 %collective-permute-start.15 = (bf16[128,7168]{1,0:T(8,128)(2,1)}, bf16[128,7168]{1,0:T(8,128)(2,1)S(1)}, u32[]{:S(2)}, u32[]{:S(2)}) collective-permute-start(bf16[128,7168]{1,0:T(8,128)(2,1)} %collective-permute-done.2.refs_2_.refs_3_), channel_id=1, source_target_pairs={{0,2},{2,0},{4,6},{6,4},{8,10},{10,8},{12,14},{14,12},{16,18},{18,... | collective-permute-start | bytes 5505032 | tf_op jit(solution)/shard_map/ppermute | solution.py:235
  205.8 40.4 %collective-permute-start.32 = (f16[2,128,1792]{2,1,0:T(8,128)(2,1)}, f16[2,128,1792]{2,1,0:T(8,128)(2,1)S(1)}, u32[]{:S(2)}, u32[]{:S(2)}) collective-permute-start(f16[2,128,1792]{2,1,0:T(8,128)(2,1)} %copy-done.19), channel_id=1, source_target_pairs={{0,2},{2,0},{4,6},{6,4},{8,10},{10,8},{12,14},{14,12},{16,18},{18,... | collective-permute-start | bytes 2752520 | tf_op jit(solution)/shard_map/ppermute | solution.py:235
  222.7 24.0 %collective-permute-start.24 = (bf16[64,7168]{1,0:T(8,128)(2,1)}, bf16[64,7168]{1,0:T(8,128)(2,1)S(1)}, u32[]{:S(2)}, u32[]{:S(2)}) collective-permute-start(bf16[64,7168]{1,0:T(8,128)(2,1)} %collective-permute-done.4.refs_1_.refs_7_), channel_id=1, source_target_pairs={{0,4},{2,6},{4,0},{6,2},{8,12},{10,14},{12,8},{14,10},{16,20},{18,... | collective-permute-start | bytes 2752520 | tf_op jit(solution)/shard_map/ppermute | solution.py:235
  245.5 25.6 %collective-permute-start.33 = (f16[2,128,1792]{2,1,0:T(8,128)(2,1)}, f16[2,128,1792]{2,1,0:T(8,128)(2,1)S(1)}, u32[]{:S(2)}, u32[]{:S(2)}) collective-permute-start(f16[2,128,1792]{2,1,0:T(8,128)(2,1)} %copy-done.19), channel_id=1, source_target_pairs={{0,16},{2,18},{4,20},{6,22},{8,24},{10,26},{12,28},{14,30},{16,0},... | collective-permute-start | bytes 2752520 | tf_op jit(solution)/shard_map/ppermute | solution.py:235
  246.2 46.1 %collective-permute-start.16 = (bf16[64,7168]{1,0:T(8,128)(2,1)}, bf16[64,7168]{1,0:T(8,128)(2,1)S(1)}, u32[]{:S(2)}, u32[]{:S(2)}) collective-permute-start(bf16[64,7168]{1,0:T(8,128)(2,1)} %collective-permute-done.5.refs_3_.refs_4_), channel_id=1, source_target_pairs={{0,2},{2,0},{4,6},{6,4},{8,10},{10,8},{12,14},{14,12},{16,18},{18,... | collective-permute-start | bytes 2752520 | tf_op jit(solution)/shard_map/ppermute | solution.py:235
  246.2 46.0 %collective-permute-start.17 = (bf16[64,7168]{1,0:T(8,128)(2,1)}, bf16[64,7168]{1,0:T(8,128)(2,1)S(1)}, u32[]{:S(2)}, u32[]{:S(2)}) collective-permute-start(bf16[64,7168]{1,0:T(8,128)(2,1)} %collective-permute-done.14.refs_4_.refs_5_), channel_id=1, source_target_pairs={{0,2},{2,0},{4,6},{6,4},{8,10},{10,8},{12,14},{14,12},{16,18},{18,... | collective-permute-start | bytes 2752520 | tf_op jit(solution)/shard_map/ppermute | solution.py:235
  246.7 37.6 %collective-permute-start.25 = (bf16[64,7168]{1,0:T(8,128)(2,1)}, bf16[64,7168]{1,0:T(8,128)(2,1)S(1)}, u32[]{:S(2)}, u32[]{:S(2)}) collective-permute-start(bf16[64,7168]{1,0:T(8,128)(2,1)} %collective-permute-done.13.refs_2_.refs_8_), channel_id=1, source_target_pairs={{0,4},{2,6},{4,0},{6,2},{8,12},{10,14},{12,8},{14,10},{16,20},{18,... | collective-permute-start | bytes 2752520 | tf_op jit(solution)/shard_map/ppermute | solution.py:235
  271.1 70.7 %collective-permute-start.34 = (f16[2,128,1792]{2,1,0:T(8,128)(2,1)S(1)}, f16[2,128,1792]{2,1,0:T(8,128)(2,1)S(1)}, u32[]{:S(2)}, u32[]{:S(2)}) collective-permute-start(f16[2,128,1792]{2,1,0:T(8,128)(2,1)S(1)} %collective-permute-done.33), channel_id=1, source_target_pairs={{0,2},{2,0},{4,6},{6,4},{8,10},{10,8},{12,14},{14,12},{16,18},{18,... | collective-permute-start | bytes 2752520 | tf_op jit(solution)/shard_map/ppermute | solution.py:235
  284.3 8.9 %copy-start.3 = (bf16[256,7168]{1,0:T(8,128)(2,1)S(1)}, bf16[256,7168]{1,0:T(8,128)(2,1)}, u32[]{:S(2)}) copy-start(bf16[256,7168]{1,0:T(8,128)(2,1)} %refs_4_.1) | copy-start | bytes 11010052
  291.7 56.8 %collective-permute-start.38 = (f32[256,1792]{1,0:T(8,128)}, f32[256,1792]{1,0:T(8,128)S(1)}, u32[]{:S(2)}, u32[]{:S(2)}) collective-permute-start(f32[256,1792]{1,0:T(8,128)} %get-tuple-element.96), channel_id=1, source_target_pairs={{0,2},{2,0},{4,6},{6,4},{8,10},{10,8},{12,14},{14,12},{16,18},{18,... | collective-permute-start | bytes 5505032 | tf_op jit(solution)/shard_map/ppermute | solution.py:235
  305.8 39.9 %copy-start.4 = (f32[512,512]{1,0:T(8,128)}, f32[512,512]{1,0:T(8,128)S(1)}, u32[]{:S(2)}) copy-start(f32[512,512]{1,0:T(8,128)S(1)} %shard_map.104) | copy-start | bytes 3145732
  305.8 2.4 copy-start.8
  306.7 11.7 %copy-start.10 = (f32[256,512]{1,0:T(8,128)S(1)}, f32[256,512]{1,0:T(8,128)}, u32[]{:S(2)}) copy-start(f32[256,512]{1,0:T(8,128)} %copy-done.9) | copy-start | bytes 1572868
  306.7 39.0 %collective-permute-start.19 = (f32[256,512]{1,0:T(8,128)}, f32[256,512]{1,0:T(8,128)}, u32[]{:S(2)}, u32[]{:S(2)}) collective-permute-start(f32[256,512]{1,0:T(8,128)} %slice_select_fusion), channel_id=1, source_target_pairs={{0,1},{1,0},{2,3},{3,2},{4,5},{5,4},{6,7},{7,6},{8,9},{9,8},{10,11... | collective-permute-start | bytes 1572872 | tf_op jit(solution)/shard_map/ppermute | solution.py:238
  319.3 29.5 %collective-permute-start.21 = (f32[256,512]{1,0:T(8,128)}, f32[256,512]{1,0:T(8,128)}, u32[]{:S(2)}, u32[]{:S(2)}) collective-permute-start(f32[256,512]{1,0:T(8,128)} %broadcast_select_fusion.13), channel_id=1, source_target_pairs={{0,1},{1,0},{2,3},{3,2},{4,5},{5,4},{6,7},{7,6},{8,9},{9,8},{10,11... | collective-permute-start | bytes 1572872 | tf_op jit(solution)/shard_map/ppermute | solution.py:238
  340.6 2.9 copy-start.28
  340.6 14.9 %collective-permute-start.26 = (f32[256,512]{1,0:T(8,128)S(1)}, f32[256,512]{1,0:T(8,128)S(1)}, u32[]{:S(2)}, u32[]{:S(2)}) collective-permute-start(f32[256,512]{1,0:T(8,128)S(1)} %broadcast_select_fusion.12), channel_id=1, source_target_pairs={{0,1},{1,0},{2,3},{3,2},{4,5},{5,4},{6,7},{7,6},{8,9},{9,8},{10,11... | collective-permute-start | bytes 1572872 | tf_op jit(solution)/shard_map/ppermute | solution.py:238
  345.7 2.8 copy-start.12
  347.2 27.4 %collective-permute-start.18 = (f32[256,512]{1,0:T(8,128)S(1)}, f32[256,512]{1,0:T(8,128)S(1)}, u32[]{:S(2)}, u32[]{:S(2)}) collective-permute-start(f32[256,512]{1,0:T(8,128)S(1)} %get-tuple-element.119), channel_id=1, source_target_pairs={{0,1},{1,0},{2,3},{3,2},{4,5},{5,4},{6,7},{7,6},{8,9},{9,8},{10,11... | collective-permute-start | bytes 1572872 | tf_op jit(solution)/shard_map/ppermute | solution.py:238
  348.1 26.5 %collective-permute-start.20 = (f32[256,512]{1,0:T(8,128)S(1)}, f32[256,512]{1,0:T(8,128)S(1)}, u32[]{:S(2)}, u32[]{:S(2)}) collective-permute-start(f32[256,512]{1,0:T(8,128)S(1)} %get-tuple-element.118), channel_id=1, source_target_pairs={{0,4},{2,6},{4,0},{6,2},{8,12},{10,14},{12,8},{14,10},{16,20},{18,... | collective-permute-start | bytes 1572872 | tf_op jit(solution)/shard_map/ppermute | solution.py:235
  348.8 21.6 %collective-permute-start.39 = (f16[128,1792]{1,0:T(8,128)(2,1)S(1)}, f16[128,1792]{1,0:T(8,128)(2,1)S(1)}, u32[]{:S(2)}, u32[]{:S(2)}) collective-permute-start(f16[128,1792]{1,0:T(8,128)(2,1)S(1)} %slice_convert_fusion), channel_id=1, source_target_pairs={{0,16},{2,18},{4,20},{6,22},{8,24},{10,26},{12,28},{14,30},{16,0},... | collective-permute-start | bytes 1376264 | tf_op jit(solution)/shard_map/ppermute | solution.py:235
  350.8 26.7 %collective-permute-start.22 = (f32[256,512]{1,0:T(8,128)}, f32[256,512]{1,0:T(8,128)}, u32[]{:S(2)}, u32[]{:S(2)}) collective-permute-start(f32[256,512]{1,0:T(8,128)} %select_add_fusion.1), channel_id=1, source_target_pairs={{0,8},{2,10},{4,12},{6,14},{8,0},{10,2},{12,4},{14,6},{16,24},{18,... | collective-permute-start | bytes 1572872 | tf_op jit(solution)/shard_map/ppermute | solution.py:235
  356.4 32.0 %collective-permute-start.27 = (f32[256,512]{1,0:T(8,128)}, f32[256,512]{1,0:T(8,128)}, u32[]{:S(2)}, u32[]{:S(2)}) collective-permute-start(f32[256,512]{1,0:T(8,128)} %select_add_fusion), channel_id=1, source_target_pairs={{0,12},{2,14},{4,8},{6,10},{8,4},{10,6},{12,0},{14,2},{16,28},{18,... | collective-permute-start | bytes 1572872 | tf_op jit(solution)/shard_map/ppermute | solution.py:235
  370.4 6.9 %copy-start.5 = (f32[512,512]{1,0:T(8,128)S(1)}, f32[512,512]{1,0:T(8,128)}, u32[]{:S(2)}) copy-start(f32[512,512]{1,0:T(8,128)} %copy-done.4) | copy-start | bytes 3145732
  373.2 23.9 %collective-permute-start.40 = (f32[2,32,1792]{2,1,0:T(8,128)}, f32[2,32,1792]{2,1,0:T(8,128)}, u32[]{:S(2)}, u32[]{:S(2)}) collective-permute-start(f32[2,32,1792]{2,1,0:T(8,128)} %get-tuple-element.98), channel_id=1, source_target_pairs={{0,4},{2,6},{4,0},{6,2},{8,12},{10,14},{12,8},{14,10},{16,20},{18,... | collective-permute-start | bytes 1376264 | tf_op jit(solution)/shard_map/ppermute | solution.py:235
  374.6 22.8 %collective-permute-start.41 = (f32[2,32,1792]{2,1,0:T(8,128)}, f32[2,32,1792]{2,1,0:T(8,128)}, u32[]{:S(2)}, u32[]{:S(2)}) collective-permute-start(f32[2,32,1792]{2,1,0:T(8,128)} %get-tuple-element.99), channel_id=1, source_target_pairs={{0,8},{2,10},{4,12},{6,14},{8,0},{10,2},{12,4},{14,6},{16,24},{18,... | collective-permute-start | bytes 1376264 | tf_op jit(solution)/shard_map/ppermute | solution.py:235
  374.6 31.3 %collective-permute-start.42 = (f32[2,32,1792]{2,1,0:T(8,128)}, f32[2,32,1792]{2,1,0:T(8,128)}, u32[]{:S(2)}, u32[]{:S(2)}) collective-permute-start(f32[2,32,1792]{2,1,0:T(8,128)} %get-tuple-element.100), channel_id=1, source_target_pairs={{0,12},{2,14},{4,8},{6,10},{8,4},{10,6},{12,0},{14,2},{16,28},{18,... | collective-permute-start | bytes 1376264 | tf_op jit(solution)/shard_map/ppermute | solution.py:235
  388.4 17.5 %copy-start.15 = (f32[2,32,1792]{2,1,0:T(8,128)S(1)}, f32[2,32,1792]{2,1,0:T(8,128)}, u32[]{:S(2)}) copy-start(f32[2,32,1792]{2,1,0:T(8,128)} %copy-done.14) | copy-start | bytes 1376260
  388.4 21.3 %copy-start.1 = (bf16[256,512]{1,0:T(8,128)(2,1)S(1)}, bf16[256,512]{1,0:T(8,128)(2,1)}, u32[]{:S(2)}) copy-start(bf16[256,512]{1,0:T(8,128)(2,1)} %param.13) | copy-start | bytes 786436
  (12 other events, 14.0 us)

commit v3 on v2

--- a/solution.py
+++ b/solution.py
@@ -7,7 +7,8 @@
 from jax.experimental.pallas import tpu as pltpu
 from jax.sharding import PartitionSpec as P
 
-SCALE = 1024.0
+SCALE = 40.0
+POWER = 16
 VMEM = 40 * 2**20
 
 
@@ -21,13 +22,20 @@
     return jnp.dot(left, right, precision=lax.Precision.HIGHEST, preferred_element_type=jnp.float32)
 
 
-def squared(value):
-    return (value * jnp.abs(value) * SCALE).astype(jnp.float16)
+def powered(value):
+    size = jnp.abs(value) * SCALE
+    power = 1
+    while power < POWER:
+        size = size * size
+        power *= 2
+    return jnp.where(value < 0, -size, size).astype(jnp.bfloat16)
 
 
 def rooted(code):
-    code = code.astype(jnp.float32) * (1.0 / SCALE)
-    root = jnp.sqrt(jnp.abs(code))
+    code = code.astype(jnp.float32)
+    size = jnp.abs(code)
+    root = jnp.exp(jnp.log(jnp.maximum(size, 1e-38)) * (1.0 / POWER)) * (1.0 / SCALE)
+    root = jnp.where(size < 1e-38, 0.0, root)
     return jnp.where(code < 0, -root, root)
 
 
@@ -63,7 +71,13 @@
 
 
 def tile_of(extent):
-    return next(size for size in (512, 896, 256, 128, extent) if extent % size == 0)
+    return next(size for size in (1792, 896, 512, 256, 128, extent) if extent % size == 0)
+
+
+def product_of(token_refs, row_refs):
+    left = jnp.concatenate([r[...] for r in token_refs], axis=0)
+    right = jnp.concatenate([r[...] for r in row_refs], axis=0)
+    return lax.dot_general(left, right, (((1,), (1,)), ((), ())), preferred_element_type=jnp.float32)
 
 
 def multiply_kernel(n_tokens, *refs):
@@ -73,9 +87,7 @@
     def _():
         out[...] = jnp.zeros_like(out)
 
-    left = jnp.concatenate([r[...] for r in refs[:n_tokens]], axis=0)
-    right = jnp.concatenate([r[...] for r in refs[n_tokens:-1]], axis=0)
-    out[...] += lax.dot_general(left, right, (((1,), (1,)), ((), ())), preferred_element_type=jnp.float32)
+    out[...] += product_of(refs[:n_tokens], refs[n_tokens:-1])
 
 
 def multiply(tokens, rows):
@@ -92,6 +104,63 @@
         compiler_params=pltpu.CompilerParams(vmem_limit_bytes=VMEM),
         cost_estimate=short_op(),
     )(*tokens, *rows)
+
+
+def parts_kernel(n_tokens, counts, given, blocks, flag, *refs):
+    t = len(counts) + given
+    token_refs, at = refs[:n_tokens], n_tokens
+    row_refs = []
+    for count in counts:
+        row_refs.append(refs[at : at + count])
+        at += count
+    ready = refs[at : at + given]
+    at += given
+    outs, sums = refs[at : at + t * blocks], refs[at + t * blocks :]
+    step = pl.program_id(0)
+
+    for total, rows in zip(sums, row_refs):
+        @pl.when(step == 0)
+        def _():
+            total[...] = jnp.zeros_like(total)
+
+        total[...] += product_of(token_refs, rows)
+
+    candidates = list(ready) + list(sums)
+    depth = outs[0].shape[0]
+
+    @pl.when(step == pl.num_programs(0) - 1)
+    def _():
+        for f in range(t):
+            @pl.when(flag[0] == f)
+            def _():
+                for e in range(t):
+                    for j in range(blocks):
+                        outs[e * blocks + j][...] = candidates[e ^ f][j * depth : (j + 1) * depth, :]
+
+
+def multiply_parts(tokens, rows, flag, depth, ready=()):
+    width = tokens[0].shape[1]
+    tile = tile_of(width)
+    height = sum(value.shape[0] for value in tokens)
+    extent = sum(value.shape[0] for value in rows[0])
+    blocks = height // depth
+    t = len(rows) + len(ready)
+    flat = [value for group in rows for value in group]
+    outs = pl.pallas_call(
+        functools.partial(parts_kernel, len(tokens), [len(group) for group in rows], len(ready), blocks),
+        grid_spec=pltpu.PrefetchScalarGridSpec(
+            num_scalar_prefetch=1,
+            grid=(width // tile,),
+            in_specs=[pl.BlockSpec((value.shape[0], tile), lambda k, f: (0, k)) for value in tokens + flat]
+            + [pl.BlockSpec((height, extent), lambda k, f: (0, 0))] * len(ready),
+            out_specs=[pl.BlockSpec((depth, extent), lambda k, f: (0, 0))] * (t * blocks),
+            scratch_shapes=[pltpu.VMEM((height, extent), jnp.float32)] * len(rows),
+        ),
+        out_shape=[jax.ShapeDtypeStruct((depth, extent), jnp.float32)] * (t * blocks),
+        compiler_params=pltpu.CompilerParams(vmem_limit_bytes=VMEM),
+        cost_estimate=short_op(),
+    )(flag.reshape(1), *tokens, *flat, *ready)
+    return [list(outs[e * blocks : (e + 1) * blocks]) for e in range(t)]
 
 
 def gradient_kernel(counts, place, *refs):
@@ -108,10 +177,12 @@
 
 
 def gradient_part(saved, tokens, place, part):
-    rank, depth = saved[0].shape
+    depth = saved[0][0].shape[1]
+    rank = saved[0][0].shape[0] // saved[0][2]
     if part % 128:
         total = 0.0
-        for value, pieces in zip(saved, tokens):
+        for (value, k, _), pieces in zip(saved, tokens):
+            value = value[k * rank : (k + 1) * rank]
             block = jnp.concatenate(pieces, axis=0)
             block = lax.dynamic_slice(block, (0, place * part), (depth, part))
             total = total + jnp.dot(value, block, preferred_element_type=jnp.float32)
@@ -124,14 +195,87 @@
         grid_spec=pltpu.PrefetchScalarGridSpec(
             num_scalar_prefetch=1,
             grid=(steps,),
-            in_specs=[pl.BlockSpec((rank, depth), lambda i, p: (0, 0))] * len(saved)
+            in_specs=[pl.BlockSpec((rank, depth), lambda i, p, k=k: (k, 0)) for _, k, _ in saved]
             + [pl.BlockSpec((value.shape[0], tile), lambda i, p: (0, p[0] * steps + i)) for value in flat],
             out_specs=[pl.BlockSpec((rank // 2, tile), lambda i, p: (0, i))] * 2,
         ),
         out_shape=[jax.ShapeDtypeStruct((rank // 2, part), jnp.float32)] * 2,
         compiler_params=pltpu.CompilerParams(vmem_limit_bytes=VMEM),
         cost_estimate=short_op(),
-    )(place.reshape(1), *saved, *flat)
+    )(place.reshape(1), *[value for value, _, _ in saved], *flat)
+
+
+def encode_kernel(na, group, first, second, *outs):
+    part = outs[0].shape[2]
+    for j in range(na):
+        mine = pl.ds(pl.multiple_of((group[0] ^ j) * part, 128), part)
+        outs[j][0] = powered(first[:, mine])
+        outs[j][1] = powered(second[:, mine])
+
+
+def encode(first, second, group, na):
+    rows, width = first.shape
+    part = width // na
+    if part % 128:
+        both = powered(jnp.stack([first, second])).reshape(2, rows, na, part)
+        return xor_order([both[:, :, k] for k in range(na)], group)
+    return list(
+        pl.pallas_call(
+            functools.partial(encode_kernel, na),
+            grid_spec=pltpu.PrefetchScalarGridSpec(
+                num_scalar_prefetch=1,
+                grid=(1,),
+                in_specs=[pl.BlockSpec((rows, width), lambda i, g: (0, 0))] * 2,
+                out_specs=[pl.BlockSpec((2, rows, part), lambda i, g: (0, 0, 0))] * na,
+            ),
+            out_shape=[jax.ShapeDtypeStruct((2, rows, part), jnp.bfloat16)] * na,
+            compiler_params=pltpu.CompilerParams(vmem_limit_bytes=VMEM),
+            cost_estimate=short_op(),
+        )(group.reshape(1), first, second)
+    )
+
+
+def stack_kernel(rows, *refs):
+    out = refs[-1]
+    for k, r in enumerate(refs[:-1]):
+        out[:, k * rows : (k + 1) * rows, :] = r[...]
+
+
+def stack_rows(blocks, rows):
+    two, _, part = blocks[0][0].shape
+    return pl.pallas_call(
+        functools.partial(stack_kernel, rows),
+        grid=(1,),
+        in_specs=[pl.BlockSpec((two, rows, part), lambda i, k=k: (0, k, 0)) for _, k in blocks],
+        out_specs=pl.BlockSpec((two, rows * len(blocks), part), lambda i: (0, 0, 0)),
+        out_shape=jax.ShapeDtypeStruct((two, rows * len(blocks), part), blocks[0][0].dtype),
+        compiler_params=pltpu.CompilerParams(vmem_limit_bytes=VMEM),
+        cost_estimate=short_op(),
+    )(*[value for value, _ in blocks])
+
+
+def rotate_kernel(n_codes, inter, *refs):
+    codes, (first, second) = refs[:n_codes], refs[n_codes:]
+    left = inter[...]
+    for k, out, matrix in ((0, first, left), (1, second, left * left)):
+        moment = jnp.concatenate([rooted(c[k]) for c in codes], axis=0)
+        out[...] = exact_dot(matrix, moment)
+
+
+def rotate(inter, codes):
+    height, rank = inter.shape
+    two, rows, part = codes[0].shape
+    tile = next((size for size in (896, 448, 256, 128) if part % size == 0 and size % 128 == 0), part)
+    return pl.pallas_call(
+        functools.partial(rotate_kernel, len(codes)),
+        grid=(part // tile,),
+        in_specs=[pl.BlockSpec((height, rank), lambda i: (0, 0))]
+        + [pl.BlockSpec((2, rows, tile), lambda i: (0, 0, i))] * len(codes),
+        out_specs=[pl.BlockSpec((height, tile), lambda i: (0, i))] * 2,
+        out_shape=[jax.ShapeDtypeStruct((height, part), jnp.float32)] * 2,
+        compiler_params=pltpu.CompilerParams(vmem_limit_bytes=VMEM),
+        cost_estimate=short_op(),
+    )(inter, *codes)
 
 
 def blend_kernel(na, group, rot_first, rot_second, gradient, *outs):
@@ -259,128 +403,230 @@
             return [value[lo:hi] for lo, hi in zip(cuts[:-1], cuts[1:])]
 
         last, others = strides[0], strides[1:]
-        token_cuts, weight_cuts = pieces_of(grad_out), pieces_of(weight)
-        a = {(0, p): token_cuts[p] for p in range(3)}
-        w = {}
-
-        def send_weight(value, p):
+
+        def chunks_of(value):
+            cuts = [0, value.shape[0] // 2, value.shape[0] * 3 // 4, value.shape[0]]
+            return [value[lo:hi] for lo, hi in zip(cuts[:-1], cuts[1:])]
+
+        token_cuts, weight_cuts = chunks_of(grad_out), chunks_of(weight)
+        a, w = {}, {}
+
+        def send(p, token_cut, weight_cut):
+            a[last, p] = swap(token_cut, 2 * last)
             for dz in tops:
-                w[dz, p] = swap(value, dz * top_unit)
-
-        def settle(p, *values):
-            keys_a = [k for k in a if k[1] == p and k[0] != 0]
-            keys_w = [k for k in w if k[1] == p]
-            held, values = together([a[k] for k in keys_a] + [w[k] for k in keys_w], values)
-            for k, v in zip(keys_a, held):
-                a[k] = v
-            for k, v in zip(keys_w, held[len(keys_a) :]):
-                w[k] = v
+                w[dz, p] = swap(weight_cut, dz * top_unit)
+
+        def forward(p):
+            for bit in others:
+                for j in [k[0] for k in list(a) if k[1] == p and k[0] & last and not k[0] & bit]:
+                    a[j | bit, p] = swap(a[j, p], 2 * bit)
+
+        def settle(keys_a, keys_w, *values):
+            held_a, held_w, values = together([a[k] for k in keys_a], [w[k] for k in keys_w], values)
+            a.update(zip(keys_a, held_a))
+            w.update(zip(keys_w, held_w))
             return values
 
-        a[last, 0] = swap(token_cuts[0], 2 * last)
-        send_weight(weight_cuts[0], 0)
+        def keys_of(p):
+            return [(last, p)], [(dz, p) for dz in tops]
+
+        def forwarded(p):
+            return [k for k in a if k[1] == p and k[0] & last and k[0] != last]
+
+        def blocks_of(j):
+            return [grad_out] if j == 0 else [a[j, p] for p in range(3) if (j, p) in a]
+
+        def hypercube(bits):
+            order = [0]
+            for bit in bits:
+                order += [k ^ bit for k in order]
+            return order
+
+        order = hypercube(strides)
+
         for bit in others:
             a[bit, 0] = swap(grad_out, 2 * bit)
+        send(0, token_cuts[0], weight_cuts[0])
         w_core = swap(weight, 1)
         ticket = anchor(jnp.full((8, 128), group, jnp.int32))
-        ticket, first_moment, second_moment, new_basis, saved = together(
-            ticket, first_moment, second_moment, new_basis, saved
+        ticket, first_moment, second_moment, saved, new_basis = together(
+            ticket, first_moment, second_moment, saved, new_basis
         )
-
-        both = squared(jnp.stack([first_moment, second_moment])).reshape(2, rows, na, part)
-        near = xor_order([both[:, :, k] for k in range(na)], group)
 
         local = contract_rows(new_basis, basis).reshape(t, na, 2, rows, rank)
         local = scatter([local[:, :, 0], local[:, :, 1]], core, 1)
-        local = xor_order([local[:, k] for k in range(na)], group)
+        local = jnp.stack(xor_order([local[:, k] for k in range(na)], group))
+
+        def halve(local, bit):
+            keep, give = local[: local.shape[0] // 2], local[local.shape[0] // 2 :]
+            return keep + swap(give, 2 * bit)
+
+        local = halve(local, strides[0])
+
+        ready = {k: [(code, 0)] for k, code in enumerate(encode(first_moment, second_moment, group, na))}
+
+        def exchange_codes(bit):
+            moving = [k for k in ready if k & bit]
+            buffer = swap(stack_rows([block for k in moving for block in ready[k]], rows), 2 * bit)
+            at = 0
+            for k in moving:
+                count = len(ready.pop(k))
+                ready[k ^ bit] += [(buffer, at + m) for m in range(count)]
+                at += count
+
+        def settle_codes(*values):
+            arrays = {id(block[0]): block[0] for blocks in ready.values() for block in blocks}
+            held, values = together(list(arrays.values()), values)
+            names = dict(zip(arrays, held))
+            for k in ready:
+                ready[k] = [(names[id(value)], m) for value, m in ready[k]]
+            return values
+
+        exchange_codes(strides[0])
 
         saved = saved.reshape(tokens, t, na, 2, rows)
         saved = jnp.stack(xor_order([saved[:, :, :, k] for k in range(2)], core), axis=1)
         saved = jnp.stack(xor_order([saved[:, :, k] for k in range(t)], top), axis=2)
-        saved_t = saved.reshape(tokens, rank).T
-
-        ticket, near, local, saved_t, more_tokens, more_weight = settle(
-            0, ticket, near, local, saved_t, token_cuts[1], weight_cuts[1]
+        saved_all = saved.reshape(tokens, rank).T
+        saved_list = [(saved_all, 0, 1)]
+
+        spot = lax.broadcasted_iota(jnp.int32, (rank, rank), 1)
+        block, within = spot // rows, spot % rows
+        place = sum((block % na == k) * order[k] for k in range(na))
+        source = ((block // (2 * na)) ^ top) * 2 * na + (place ^ group) * 2 + ((block // na % 2) ^ core)
+        arrival = (lax.broadcasted_iota(jnp.int32, (rank, rank), 0) == source * rows + within).astype(jnp.float32)
+
+        keys_a, keys_w = keys_of(0)
+        (ticket, local, saved_all, arrival, token_cut, weight_cut, w_core) = settle_codes(
+            *settle(
+                keys_a + [(bit, 0) for bit in others],
+                keys_w,
+                ticket,
+                local,
+                saved_all,
+                arrival,
+                token_cuts[1],
+                weight_cuts[1],
+                w_core,
+            )
         )
-        near = [near[0]] + [swap(near[j], 2 * j) for j in range(1, na)]
-        local = [local[0]] + [swap(local[j], 2 * j) for j in range(1, na)]
-
-        def forward(p):
-            for bit in others:
-                for j in [k[0] for k in a if k[1] == p and k[0] & last and not k[0] & bit]:
-                    a[j | bit, p] = swap(a[j, p], 2 * bit)
-
+        for bit in others:
+            exchange_codes(bit)
+            local = halve(local, bit)
         forward(0)
-        a[last, 1] = swap(more_tokens, 2 * last)
-        send_weight(more_weight, 1)
-        saved_all = [saved_t if j == 0 else swap(saved_t, 2 * j) for j in range(na)]
+        send(1, token_cut, weight_cut)
+        ticket = anchor(ticket)
+        ticket, w_core = together(ticket, w_core)
+        own_rows = [weight, w_core]
+        near_tokens = [j for j in range(na) if not j & last]
+        far_tokens = [j for j in range(na) if j & last]
+        own_products = multiply([value for j in near_tokens for value in blocks_of(j)], own_rows)
+        (ticket,) = settle_codes(ticket)
+        near = stack_rows(ready[0], rows)
+        near_other = swap(near, 1)
+        saved_list = [(saved_all, 0, 1), (swap(saved_all, 2 * last), 0, 1)]
+
+        keys_a, keys_w = keys_of(1)
+        ticket, local, near, near_other, saved_next, own_products, token_cut, weight_cut = settle(
+            keys_a + forwarded(0),
+            keys_w,
+            ticket,
+            local,
+            near,
+            near_other,
+            saved_list[1][0],
+            own_products,
+            token_cuts[2],
+            weight_cuts[2],
+        )
+        saved_list[1] = (saved_next, 0, 1)
+        own = scatter([local[0, k] for k in range(t)], top, top_unit)
+        forward(1)
+        send(2, token_cut, weight_cut)
+        for bit in others:
+            both = [value[k * rank : (k + 1) * rank] for value, k, _ in saved_list]
+            both = swap(jnp.concatenate(both, axis=0), 2 * bit)
+            saved_list += [(both, k, len(saved_list)) for k in range(len(saved_list))]
+        other_rows = {dz: [swap(w[dz, p], 1) for p in (0, 1)] for dz in tops}
+        ticket = anchor(ticket)
+
+        keys_a, keys_w = keys_of(2)
+        saved_arrays = {id(value): value for value, _, _ in saved_list}
+        ticket, own, near, held, other_rows = settle(
+            keys_a + forwarded(1), keys_w, ticket, own, near, list(saved_arrays.values()), other_rows
+        )
+        names = dict(zip(saved_arrays, held))
+        saved_list = [(names[id(value)], k, count) for value, k, count in saved_list]
+        forward(2)
+        far = {dz: swap(near, dz * top_unit) for dz in tops}
+        inter = [own] + [swap(own, 2 * bit) for bit in strides[:1]]
+        other_rows = [[w[dz, p] for p in range(3)] + other_rows[dz] + [swap(w[dz, 2], 1)] for dz in tops]
+        ticket = anchor(ticket)
+
+        def parts_of(js, rows_of, ready_products=()):
+            blocks = [value for j in js for value in blocks_of(j)]
+            flag = ticket[0, 0] ^ group ^ top ^ x
+            made = multiply_parts(blocks, rows_of, flag, tokens * len(js), ready_products)
+            return [m[0] for m in made]
+
+        def over_tp(parts):
+            return [swap_tp(parts[e].astype(jnp.float16), e) for e in tops]
+
+        def total_of(parts, arrived):
+            return functools.reduce(jnp.add, [parts[0]] + [value.astype(jnp.float32) for value in arrived])
+
+        near_parts = parts_of(near_tokens, other_rows, [own_products])
+        near_arrived = over_tp(near_parts)
+        ticket, near_parts, inter = together(ticket, near_parts, inter)
+        for bit in strides[1:]:
+            inter += [swap(value, 2 * bit) for value in inter]
+        inter = [inter[order.index(k)] for k in range(na)]
+        all_rows = [own_rows] + other_rows
+        next_parts = parts_of(far_tokens[:1], all_rows)
+        next_arrived = over_tp(next_parts)
+
+        ticket, next_parts = settle(forwarded(2), [], ticket, next_parts)
+        keep, send_half = gradient_part(saved_list, [blocks_of(j) for j in order], group, part)
+        ticket, keep, send_half = together(ticket, keep, send_half)
+        last_parts = parts_of(far_tokens[1:], all_rows) if far_tokens[1:] else None
+
+        (ticket, far, inter, near_arrived, near_parts, next_arrived, next_parts, last_parts, keep, send_half) = together(
+            ticket, far, inter, near_arrived, near_parts, next_arrived, next_parts, last_parts, keep, send_half
+        )
+        got = swap(send_half, 1)
+        last_arrived = over_tp(last_parts) if far_tokens[1:] else None
+        far_other = {dz: swap(far[dz], 1) for dz in tops}
+        g = (keep + got).reshape(t, na * rows, part)
+        late_g = [swap(g[dz].astype(jnp.float16), dz * top_unit) for dz in tops]
+
+        def go_home(js, parts, arrived):
+            total = total_of(parts, arrived)
+            blocks = {j: total[k * tokens : (k + 1) * tokens] for k, j in enumerate(js)}
+            return {j: swap(block, 2 * j) if j else block for j, block in blocks.items()}
+
+        sums = go_home(near_tokens, near_parts, near_arrived)
+        sums.update(go_home(far_tokens[:1], next_parts, next_arrived))
+        ticket = anchor(ticket)
+        ticket, inter, near, near_other = together(ticket, inter, near, near_other)
+        inter = exact_dot(jnp.concatenate(xor_order(inter, group), axis=0), arrival)
+        codes = [near, near_other]
+        for dz in tops:
+            codes += [far[dz], far_other[dz]]
+        rot_first, rot_second = rotate(inter, codes)
+
+        ticket, last_arrived, sums, rot_first, rot_second = together(ticket, last_arrived, sums, rot_first, rot_second)
+        if far_tokens[1:]:
+            sums.update(go_home(far_tokens[1:], last_parts, last_arrived))
         ticket = anchor(ticket)
         group = ticket[0, 0]
-        ticket, local, near, own_rows = together(ticket, local, near, [weight, w_core])
-        local = functools.reduce(jnp.add, local)
-        near = jnp.concatenate(near, axis=1)
-        near_other = swap(near, 1)
-
-        ticket, local, near, more_tokens, more_weight = settle(1, ticket, local, near, token_cuts[2], weight_cuts[2])
-        forward(1)
-        a[last, 2] = swap(more_tokens, 2 * last)
-        send_weight(more_weight, 2)
-        far = {dz: swap(near, dz * top_unit) for dz in tops}
-        ticket = anchor(ticket)
-        group_late = ticket[0, 0]
-        ticket, local = together(ticket, local)
-
-        (ticket,) = settle(2, ticket)
-        forward(2)
-
-        def blocks_of(j):
-            if j == 0:
-                return [grad_out]
-            return [a[j, p] for p in range(3) if (j, p) in a]
-
-        own = scatter([local[k] for k in range(t)], top, top_unit)
-
-        moments = [rooted(jnp.concatenate([near, near_other], axis=1))]
-        for dz in tops:
-            moments.append(rooted(jnp.concatenate([far[dz], swap(far[dz], 1)], axis=1)))
-
-        inter = jnp.stack(
-            xor_order([own] + [swap(own, 2 * j) for j in range(1, na)], group), axis=0
-        ).reshape(na * rows, t, na, 2, rows)
-        inter = xor_order([inter[:, k] for k in range(t)], top)
-        rot_first = rot_second = None
-        for dz in range(t):
-            part_of = jnp.stack(xor_order([inter[dz][:, :, k] for k in range(2)], core), axis=1)
-            part_of = jnp.stack(xor_order([part_of[:, :, k] for k in range(na)], group), axis=2)
-            part_of = part_of.reshape(na * rows, 2 * na * rows)
-            f = exact_dot(part_of, moments[dz][0])
-            v = exact_dot(part_of * part_of, moments[dz][1])
-            rot_first = f if dz == 0 else rot_first + f
-            rot_second = v if dz == 0 else rot_second + v
-
-        keep, send = gradient_part(saved_all, [blocks_of(j) for j in range(na)], group, part)
-        g = (keep + swap(send, 1)).reshape(t, na * rows, part)
+        g, late_g, group = together(g, late_g, group)
         gradient = g[0]
-        for dz in tops:
-            gradient = gradient + swap(g[dz].astype(jnp.float16), dz * top_unit).astype(jnp.float32)
-
-        pieces = blend(rot_first, rot_second, gradient, group_late, na)
+        for value in late_g:
+            gradient = gradient + value.astype(jnp.float32)
+        pieces = blend(rot_first, rot_second, gradient, group, na)
         pieces = [pieces[0]] + [swap(pieces[j], 2 * j) for j in range(1, na)]
+        grad_input = place_columns([sums[j] for j in range(na)], 2 * group + core)
         first_new, second_new, update = finish(pieces, group)
-
-        other_rows = {dz: [w[dz, p] for p in range(3)] + [swap(w[dz, p], 1) for p in range(3)] for dz in tops}
-        sums = [None] * na
-        near_tokens = [j for j in range(na) if not j & last]
-        for some in [near_tokens] + [[j] for j in range(na) if j & last]:
-            block = [value for j in some for value in blocks_of(j)]
-            by_top = [multiply(block, own_rows)] + [multiply(block, other_rows[dz]) for dz in tops]
-            for i, j in enumerate(some):
-                rel = xor_order([c[i * tokens : (i + 1) * tokens] for c in by_top], top ^ x)
-                total = rel[0]
-                for e in tops:
-                    total = total + swap_tp(rel[e], e)
-                sums[j] = swap(total, 2 * j) if j else total
-        grad_input = place_columns(sums, 2 * group + core)
         return (grad_input, first_new, second_new, update)
 
     return per_device

time: 412 us -> 342 us (0.83)
  waiting for transfers between devices: 206 us -> 185 us
  Pallas kernels: 84.1 us -> 65.8 us
  local copies, waits for them, and re-layouts: 37.2 us -> 21.2 us
  other arithmetic: 31.2 us -> 19.3 us
    pallas_call x6 -> x1, Pallas kernels: 65.4 us -> 7.36 us  [multiply(): pl.pallas_call(functools.partial(multiply_kernel, len(tokens)), grid=(wid...]
    pallas_call x0 -> x8, Pallas kernels: none -> 37.7 us  [the longest x3 25.7 us: multiply_parts(): pl.pallas_call(functools.partial(parts_kernel, len(tokens), [len(group) f...]
    ppermute x39 -> x36, waiting for transfers between devices: 204 us -> 185 us  [swap(): return lax.ppermute(value, 'seq', [(s, s ^ mask) for s in range(n)])]
    select_n x18 -> x8, other arithmetic: 14.6 us -> 1.09 us  [xor_order(): jnp.where(odd, items[k ^ bit], items[k])]
    unnamed x72 -> x68, local copies, waits for them, and re-layouts: 13.1 us -> 5.62 us
    select_n x4 -> x0, local copies, waits for them, and re-layouts: 5.45 us -> none  [xor_order(): jnp.where(odd, items[k ^ bit], items[k])]
    slice x5 -> x8, local copies, waits for them, and re-layouts: 11.1 us -> 13.6 us  [the longest x3 8.46 us: chunks_of(): return [value[lo:hi] for lo, hi in zip(cuts[:-1], cuts[1:])]]
    ppermute x39 -> x36, starting transfers between devices: 39.1 us -> 39.8 us  [swap(): return lax.ppermute(value, 'seq', [(s, s ^ mask) for s in range(n)])]
  transfers between devices with their start and end apart: 43 -> 39, of which waited for: 19 -> 14; matrix products, arithmetic and copies ran while one was open for 16% -> 10% of each run, Pallas kernels for 19% -> 18%
where the time goes in v3:
time: 342 us; the launch traced here: 341 us
  waiting for transfers between devices  185 us (54%)
  Pallas kernels  65.8 us (19%)
  starting transfers between devices  43.3 us (13%)
  local copies, waits for them, and re-layouts  21.2 us (6%)
  other arithmetic  19.3 us (6%)
  between operations  3.84 us (1%)
    ppermute x36, waiting for transfers between devices, swap(): return lax.ppermute(value, 'seq', [(s, s ^ mask) for s in range(n)])  185 us
    ppermute x36, starting transfers between devices, swap(): return lax.ppermute(value, 'seq', [(s, s ^ mask) for s in range(n)])  39.8 us
    pallas_call x3, Pallas kernels, multiply_parts(): pl.pallas_call(functools.partial(parts_kernel, len(tokens), [len(group) f...  25.7 us
    pallas_call x1, Pallas kernels, rotate(): pl.pallas_call(functools.partial(rotate_kernel, len(codes)), grid=(part /...  8.58 us
    slice x3, local copies, waits for them, and re-layouts, chunks_of(): return [value[lo:hi] for lo, hi in zip(cuts[:-1], cuts[1:])]  8.46 us
    pallas_call x6, Pallas kernels, anchor(): pl.pallas_call(anchor_kernel, out_shape=jax.ShapeDtypeStruct(value.shape,...  7.85 us
    pallas_call x1, Pallas kernels, multiply(): pl.pallas_call(functools.partial(multiply_kernel, len(tokens)), grid=(wid...  7.36 us
  transfers between devices with their start and end apart: 39, of which 14 were waited for; matrix products, arithmetic and copies ran while one was open for 10% of the time, Pallas kernels for 18%

profile of v3, /device:TPU:0, one launch (start us, length us, event | category | flops | bytes accessed | tf_op | source)
XLA Modules:
  0.0 341.1 jit_solution(14719349975411158876)
XLA Ops:
  1.3 1.3 shard_map.102.source
  4.3 2.5 collective-permute-start.2
  6.8 1.7 slice.90
  8.5 1.6 collective-permute-start.1
  10.1 2.8 slice.91
  12.9 2.6 collective-permute-start.3
  15.6 4.0 %fusion.41 = (bf16[64,7168]{1,0:T(8,128)(2,1)}, bf16[64,7168]{1,0:T(8,128)(2,1)}, bf16[64,7168]{1,0:T(8,128)(2,1)}, bf16[64,7168]{1,0:T(8,128)(2,1)}) fusion(bf16[256,7168]{1,0:T(8,128)(2,1)} %refs_3_.3, bf16[256,7168]{1,0:T(8,128)(2,1)} %refs_4_.1), kind=kLoop, calls=%fused_computation.96 | loop fusion | bytes 7340032 | tf_op jit(solution)/shard_map/slice | solution.py:409
  19.5 1.2 fusion.16
  20.9 1.3 fusion.18
  24.2 70.7 %collective-permute-done.5 = f32[2,2,32,512]{3,2,1,0:T(8,128)} collective-permute-done((f32[2,2,32,512]{3,2,1,0:T(8,128)}, f32[2,2,32,512]{3,2,1,0:T(8,128)}, u32[]{:S(2)}, u32[]{:S(2)}) %collective-permute-start.5) | collective-permute-done | bytes 262176 | tf_op jit(solution)/shard_map/ppermute | solution.py:379
  94.8 2.5 collective-permute-start
  99.1 8.3 %collective-permute-done.refs_1_ = bf16[2,64,1792]{2,1,0:T(8,128)(2,1)S(1)} collective-permute-done((bf16[2,64,1792]{2,1,0:T(8,128)(2,1)S(1)}, bf16[2,64,1792]{2,1,0:T(8,128)(2,1)S(1)}, u32[]{:S(2)}, u32[]{:S(2)}) %collective-permute-start) | collective-permute-done | bytes 458784 | tf_op jit(solution)/shard_map/ppermute | solution.py:379
  110.2 1.5 collective-permute-start.11
  112.2 1.8 collective-permute-start.13
  114.0 1.3 shard_map.106.source
  115.3 7.5 %collective-permute-done.10.refs_2_.refs_3_ = bf16[2,64,1792]{2,1,0:T(8,128)(2,1)} collective-permute-done((bf16[2,64,1792]{2,1,0:T(8,128)(2,1)}, bf16[2,64,1792]{2,1,0:T(8,128)(2,1)}, u32[]{:S(2)}, u32[]{:S(2)}) %collective-permute-start.10) | collective-permute-done | bytes 458784 | tf_op jit(solution)/shard_map/ppermute | solution.py:379
  122.8 1.7 collective-permute-start.7
  124.5 2.0 shard_map.107.refs_0_
  126.6 2.5 collective-permute-start.9
  129.1 2.0 copy-done.2
  131.2 7.4 %shard_map.108.refs_8_ = f32[512,512]{1,0:T(8,128)S(1)} custom-call(bf16[256,7168]{1,0:T(8,128)(2,1)S(1)} %copy-done.2, bf16[256,7168]{1,0:T(8,128)(2,1)} %collective-permute-done.2.refs_1_.refs_8_, bf16[256,7168]{1,0:T(8,128)(2,1)} %refs_3_.3, bf16[256,7168]{1,0:T(8,128)(2,1)} %collective-permute-done.6.refs_3_.refs_4_), custom_call_target="tpu_custom_call" | custom-call | flops 1024 | bytes 1024 | tf_op jit(solution)/shard_map/pallas_call | solution.py:98
  139.5 19.2 %collective-permute-done.7.refs_1_.refs_6_ = bf16[64,7168]{1,0:T(8,128)(2,1)} collective-permute-done((bf16[64,7168]{1,0:T(8,128)(2,1)}, bf16[64,7168]{1,0:T(8,128)(2,1)}, u32[]{:S(2)}, u32[]{:S(2)}) %collective-permute-start.7) | collective-permute-done | bytes 917536 | tf_op jit(solution)/shard_map/ppermute | solution.py:379
  158.7 5.6 %collective-permute-done.9.refs_3_.refs_6_ = bf16[64,7168]{1,0:T(8,128)(2,1)} collective-permute-done((bf16[64,7168]{1,0:T(8,128)(2,1)S(1)}, bf16[64,7168]{1,0:T(8,128)(2,1)}, u32[]{:S(2)}, u32[]{:S(2)}) %collective-permute-start.9) | collective-permute-done | bytes 917536 | tf_op jit(solution)/shard_map/ppermute | solution.py:379
  165.2 1.9 pad_maximum_fusion
  167.6 2.7 collective-permute-start.14
  170.3 1.6 collective-permute-start.15
  172.1 1.3 shard_map.109.source
  173.4 1.5 bitcast_add_fusion.1
  175.0 7.3 %collective-permute-done.18.refs_2_.refs_3_ = bf16[1024,256]{1,0:T(8,128)(2,1)} collective-permute-done((bf16[1024,256]{1,0:T(8,128)(2,1)}, bf16[1024,256]{1,0:T(8,128)(2,1)}, u32[]{:S(2)}, u32[]{:S(2)}) %collective-permute-start.18) | collective-permute-done | bytes 524320 | tf_op jit(solution)/shard_map/ppermute | solution.py:379
  182.2 22.8 %collective-permute-done.14.refs_2_.refs_7_ = bf16[64,7168]{1,0:T(8,128)(2,1)} collective-permute-done((bf16[64,7168]{1,0:T(8,128)(2,1)}, bf16[64,7168]{1,0:T(8,128)(2,1)}, u32[]{:S(2)}, u32[]{:S(2)}) %collective-permute-start.14) | collective-permute-done | bytes 917536 | tf_op jit(solution)/shard_map/ppermute | solution.py:379
  205.1 5.2 %collective-permute-done.16.refs_4_.refs_7_ = bf16[64,7168]{1,0:T(8,128)(2,1)} collective-permute-done((bf16[64,7168]{1,0:T(8,128)(2,1)}, bf16[64,7168]{1,0:T(8,128)(2,1)}, u32[]{:S(2)}, u32[]{:S(2)}) %collective-permute-start.16) | collective-permute-done | bytes 917536 | tf_op jit(solution)/shard_map/ppermute | solution.py:379
  210.9 1.3 shard_map.110.source
  212.1 1.2 slice.110
  214.0 2.0 copy-done.3
  216.0 7.5 %shard_map.111 = (f32[512,512]{1,0:T(8,128)S(1)}, f32[512,512]{1,0:T(8,128)S(1)}) custom-call(s32[1]{0:T(128)} %bitcast.28.flag, bf16[256,7168]{1,0:T(8,128)(2,1)S(1)} %copy-done.3, bf16[256,7168]{1,0:T(8,128)(2,1)} %collective-permute-done.2.refs_1_.refs_8_, bf16[128,7168]{1,0:T(8,128)(2,1)} %collective-permute-done.3.refs_2_.refs_5_, ...), custom_call_target="tpu_custom_call" | custom-call | flops 1024 | bytes 1024 | tf_op jit(solution)/shard_map/pallas_call | solution.py:149
  224.7 1.5 collective-permute-start.27
  226.2 1.9 collective-permute-start.23
  228.1 4.6 %collective-permute-done.23 = f32[32,512]{1,0:T(8,128)S(1)} collective-permute-done((f32[32,512]{1,0:T(8,128)S(1)}, f32[32,512]{1,0:T(8,128)S(1)}, u32[]{:S(2)}, u32[]{:S(2)}) %collective-permute-start.23) | collective-permute-done | bytes 65568 | tf_op jit(solution)/shard_map/ppermute | solution.py:379
  232.7 1.2 slice.111
  234.5 9.1 %shard_map.112 = (f32[256,512]{1,0:T(8,128)S(1)}, f32[256,512]{1,0:T(8,128)S(1)}) custom-call(s32[1]{0:T(128)} %bitcast.30.flag, bf16[128,7168]{1,0:T(8,128)(2,1)} %collective-permute-done.1.refs_0_.refs_5_, bf16[64,7168]{1,0:T(8,128)(2,1)} %collective-permute-done.7.refs_1_.refs_6_, bf16[64,7168]{1,0:T(8,128)(2,1)} %collective-permute-done.14.refs_2_.refs_7_, ...), custom_call_target="tpu_custom_call" | custom-call | flops 1024 | bytes 1024 | tf_op jit(solution)/shard_map/pallas_call | solution.py:149
  244.4 1.5 collective-permute-start.28
  245.8 1.6 collective-permute-start.25
  247.9 5.7 %shard_map.113 = (f32[256,1792]{1,0:T(8,128)S(1)}, f32[256,1792]{1,0:T(8,128)}) custom-call(s32[1]{0:T(128)} %bitcast.group.place, bf16[512,256]{1,0:T(8,128)(2,1)} %bitcast.24.refs_0_, bf16[512,256]{1,0:T(8,128)(2,1)} %collective-permute-done.13.refs_1_, bf16[1024,256]{1,0:T(8,128)(2,1)} %collective-permute-done.18.refs_2_.refs_3_, ...), custom_call_target="tpu_custom_call" | custom-call | flops 1024 | bytes 1024 | tf_op jit(solution)/shard_map/pallas_call | solution.py:193
  253.6 1.2 slice.112
  255.5 9.1 %shard_map.114 = (f32[256,512]{1,0:T(8,128)S(1)}, f32[256,512]{1,0:T(8,128)S(1)}) custom-call(s32[1]{0:T(128)} %bitcast.32.flag, bf16[128,7168]{1,0:T(8,128)(2,1)} %collective-permute-done.8.refs_9_.refs_0_, bf16[64,7168]{1,0:T(8,128)(2,1)} %collective-permute-done.15.refs_10_.refs_1_, bf16[64,7168]{1,0:T(8,128)(2,1)} %collective-permute-done.21.refs_11_.refs_2_, ...), custom_call_target="tpu_custom_call" | custom-call | flops 1024 | bytes 1024 | tf_op jit(solution)/shard_map/pallas_call | solution.py:149
  265.6 2.5 collective-permute-start.33
  268.1 1.2 convert_add_fusion
  270.2 1.6 collective-permute-start.32
  271.8 1.3 shard_map.115.source
  273.8 1.9 fusion.19.inter
  275.8 8.6 %shard_map.116 = (f32[128,1792]{1,0:T(8,128)S(1)}, f32[128,1792]{1,0:T(8,128)S(1)}) custom-call(f32[128,512]{1,0:T(8,128)S(1)} %fusion.19.inter, bf16[2,128,1792]{2,1,0:T(8,128)(2,1)} %shard_map.107.refs_0_, bf16[2,128,1792]{2,1,0:T(8,128)(2,1)S(1)} %copy-done.13, bf16[2,128,1792]{2,1,0:T(8,128)(2,1)} %collective-permute-done.24.refs_2_, ...), custom_call_target="tpu_custom_call" | custom-call | flops 1024 | bytes 1024 | tf_op jit(solution)/shard_map/pallas_call | solution.py:269
  284.6 1.9 add.82
  288.6 1.3 shard_map.117
  290.0 1.3 slice.116
  292.1 2.2 collective-permute-start.35
  294.3 17.3 %collective-permute-done.30 = f16[128,1792]{1,0:T(8,128)(2,1)} collective-permute-done((f16[128,1792]{1,0:T(8,128)(2,1)}, f16[128,1792]{1,0:T(8,128)(2,1)}, u32[]{:S(2)}, u32[]{:S(2)}) %collective-permute-start.30) | collective-permute-done | bytes 458784 | tf_op jit(solution)/shard_map/ppermute | solution.py:379
  311.7 1.4 bitcast_add_fusion.gradient
  313.1 1.9 shard_map.119
  315.5 3.0 collective-permute-start.38
  319.1 2.7 shard_map.118
  321.9 5.9 %collective-permute-done.36.refs_1_ = f32[2,32,1792]{2,1,0:T(8,128)S(1)} collective-permute-done((f32[2,32,1792]{2,1,0:T(8,128)}, f32[2,32,1792]{2,1,0:T(8,128)S(1)}, u32[]{:S(2)}, u32[]{:S(2)}) %collective-permute-start.36) | collective-permute-done | bytes 458784 | tf_op jit(solution)/shard_map/ppermute | solution.py:379
  327.7 1.4 collective-permute-done.37.refs_2_
  329.1 9.4 %collective-permute-done.38.refs_3_ = f32[2,32,1792]{2,1,0:T(8,128)S(1)} collective-permute-done((f32[2,32,1792]{2,1,0:T(8,128)}, f32[2,32,1792]{2,1,0:T(8,128)S(1)}, u32[]{:S(2)}, u32[]{:S(2)}) %collective-permute-start.38) | collective-permute-done | bytes 458784 | tf_op jit(solution)/shard_map/ppermute | solution.py:379
  338.6 2.5 shard_map.120
  (142 shorter events, 21.3 us)
Async XLA Ops:
  3.8 17.0 %collective-permute-start.4 = (f32[2,4,32,512]{3,2,1,0:T(8,128)}, f32[2,4,32,512]{3,2,1,0:T(8,128)}, u32[]{:S(2)}, u32[]{:S(2)}) collective-permute-start(f32[2,4,32,512]{3,2,1,0:T(8,128)} %select_bitcast_fusion), channel_id=1, source_target_pairs={{0,2},{2,0},{4,6},{6,4},{8,10},{10,8},{12,14},{14,12},{16,18},{18,... | collective-permute-start | bytes 1572872 | tf_op jit(solution)/shard_map/ppermute | solution.py:379
  4.3 94.8 %collective-permute-start.2 = (bf16[256,7168]{1,0:T(8,128)(2,1)}, bf16[256,7168]{1,0:T(8,128)(2,1)}, u32[]{:S(2)}, u32[]{:S(2)}) collective-permute-start(bf16[256,7168]{1,0:T(8,128)(2,1)} %refs_4_.1), channel_id=1, source_target_pairs={{0,4},{2,6},{4,0},{6,2},{8,12},{10,14},{12,8},{14,10},{16,20},{18,... | collective-permute-start | bytes 11010056 | tf_op jit(solution)/shard_map/ppermute | solution.py:379
  8.5 90.6 %collective-permute-start.1 = (bf16[128,7168]{1,0:T(8,128)(2,1)S(1)}, bf16[128,7168]{1,0:T(8,128)(2,1)}, u32[]{:S(2)}, u32[]{:S(2)}) collective-permute-start(bf16[128,7168]{1,0:T(8,128)(2,1)S(1)} %slice.90), channel_id=1, source_target_pairs={{0,8},{2,10},{4,12},{6,14},{8,0},{10,2},{12,4},{14,6},{16,24},{18,... | collective-permute-start | bytes 5505032 | tf_op jit(solution)/shard_map/ppermute | solution.py:379
  10.1 89.0 %collective-permute-start.6 = (bf16[256,7168]{1,0:T(8,128)(2,1)}, bf16[256,7168]{1,0:T(8,128)(2,1)}, u32[]{:S(2)}, u32[]{:S(2)}) collective-permute-start(bf16[256,7168]{1,0:T(8,128)(2,1)} %refs_3_.3), channel_id=1, source_target_pairs={{0,2},{2,0},{4,6},{6,4},{8,10},{10,8},{12,14},{14,12},{16,18},{18,... | collective-permute-start | bytes 11010056 | tf_op jit(solution)/shard_map/ppermute | solution.py:379
  12.9 86.2 %collective-permute-start.3 = (bf16[128,7168]{1,0:T(8,128)(2,1)}, bf16[128,7168]{1,0:T(8,128)(2,1)}, u32[]{:S(2)}, u32[]{:S(2)}) collective-permute-start(bf16[128,7168]{1,0:T(8,128)(2,1)} %slice.91), channel_id=1, source_target_pairs={{0,16},{2,18},{4,20},{6,22},{8,24},{10,26},{12,28},{14,30},{16,0},... | collective-permute-start | bytes 5505032 | tf_op jit(solution)/shard_map/ppermute | solution.py:379
  15.6 5.1 %copy-start.23 = (bf16[256,512]{1,0:T(8,128)(2,1)S(1)}, bf16[256,512]{1,0:T(8,128)(2,1)}, u32[]{:S(2)}) copy-start(bf16[256,512]{1,0:T(8,128)(2,1)} %param.9) | copy-start | bytes 786436
  20.8 2.7 copy-start.8
  20.9 2.7 copy-start.9
  23.0 71.8 %collective-permute-start.5 = (f32[2,2,32,512]{3,2,1,0:T(8,128)}, f32[2,2,32,512]{3,2,1,0:T(8,128)}, u32[]{:S(2)}, u32[]{:S(2)}) collective-permute-start(f32[2,2,32,512]{3,2,1,0:T(8,128)} %pad_maximum_fusion.1), channel_id=1, source_target_pairs={{0,8},{2,10},{4,12},{6,14},{8,0},{10,2},{12,4},{14,6},{16,24},{18,... | collective-permute-start | bytes 786440 | tf_op jit(solution)/shard_map/ppermute | solution.py:379
  94.8 12.6 %collective-permute-start = (bf16[2,64,1792]{2,1,0:T(8,128)(2,1)S(1)}, bf16[2,64,1792]{2,1,0:T(8,128)(2,1)S(1)}, u32[]{:S(2)}, u32[]{:S(2)}) collective-permute-start(bf16[2,64,1792]{2,1,0:T(8,128)(2,1)S(1)} %shard_map.104), channel_id=1, source_target_pairs={{0,8},{2,10},{4,12},{6,14},{8,0},{10,2},{12,4},{14,6},{16,24},{18,... | collective-permute-start | bytes 1376264 | tf_op jit(solution)/shard_map/ppermute | solution.py:379
  99.1 14.9 %copy-start.18 = (f32[2,2,32,512]{3,2,1,0:T(8,128)}, f32[2,2,32,512]{3,2,1,0:T(8,128)S(1)}, u32[]{:S(2)}) copy-start(f32[2,2,32,512]{3,2,1,0:T(8,128)S(1)} %maximum_add_fusion) | copy-start | bytes 786436
  109.0 13.8 %collective-permute-start.10 = (bf16[2,64,1792]{2,1,0:T(8,128)(2,1)}, bf16[2,64,1792]{2,1,0:T(8,128)(2,1)}, u32[]{:S(2)}, u32[]{:S(2)}) collective-permute-start(bf16[2,64,1792]{2,1,0:T(8,128)(2,1)} %shard_map.105), channel_id=1, source_target_pairs={{0,4},{2,6},{4,0},{6,2},{8,12},{10,14},{12,8},{14,10},{16,20},{18,... | collective-permute-start | bytes 1376264 | tf_op jit(solution)/shard_map/ppermute | solution.py:379
  110.2 16.4 %collective-permute-start.11 = (f32[1,2,32,512]{3,2,1,0:T(8,128)}, f32[1,2,32,512]{3,2,1,0:T(8,128)}, u32[]{:S(2)}, u32[]{:S(2)}) collective-permute-start(f32[1,2,32,512]{3,2,1,0:T(8,128)} %slice.105), channel_id=1, source_target_pairs={{0,4},{2,6},{4,0},{6,2},{8,12},{10,14},{12,8},{14,10},{16,20},{18,... | collective-permute-start | bytes 393224 | tf_op jit(solution)/shard_map/ppermute | solution.py:379
  111.7 52.6 %collective-permute-start.8 = (bf16[128,7168]{1,0:T(8,128)(2,1)}, bf16[128,7168]{1,0:T(8,128)(2,1)}, u32[]{:S(2)}, u32[]{:S(2)}) collective-permute-start(bf16[128,7168]{1,0:T(8,128)(2,1)} %collective-permute-done.1.refs_0_.refs_5_), channel_id=1, source_target_pairs={{0,4},{2,6},{4,0},{6,2},{8,12},{10,14},{12,8},{14,10},{16,20},{18,... | collective-permute-start | bytes 5505032 | tf_op jit(solution)/shard_map/ppermute | solution.py:379
  112.2 16.9 %collective-permute-start.13 = (bf16[512,256]{1,0:T(8,128)(2,1)}, bf16[512,256]{1,0:T(8,128)(2,1)}, u32[]{:S(2)}, u32[]{:S(2)}) collective-permute-start(bf16[512,256]{1,0:T(8,128)(2,1)} %bitcast.24.refs_0_), channel_id=1, source_target_pairs={{0,8},{2,10},{4,12},{6,14},{8,0},{10,2},{12,4},{14,6},{16,24},{18,... | collective-permute-start | bytes 786440 | tf_op jit(solution)/shard_map/ppermute | solution.py:379
  114.0 57.9 %collective-permute-start.19 = (bf16[128,7168]{1,0:T(8,128)(2,1)}, bf16[128,7168]{1,0:T(8,128)(2,1)}, u32[]{:S(2)}, u32[]{:S(2)}) collective-permute-start(bf16[128,7168]{1,0:T(8,128)(2,1)} %collective-permute-done.3.refs_2_.refs_5_), channel_id=1, source_target_pairs={{0,2},{2,0},{4,6},{6,4},{8,10},{10,8},{12,14},{14,12},{16,18},{18,... | collective-permute-start | bytes 5505032 | tf_op jit(solution)/shard_map/ppermute | solution.py:379
  114.0 10.5 %copy-start.5 = (bf16[2,64,1792]{2,1,0:T(8,128)(2,1)S(1)}, bf16[2,64,1792]{2,1,0:T(8,128)(2,1)}, u32[]{:S(2)}) copy-start(bf16[2,64,1792]{2,1,0:T(8,128)(2,1)} %copy-done.4) | copy-start | bytes 1376260
  115.3 11.3 %copy-start.20 = (bf16[64,7168]{1,0:T(8,128)(2,1)S(1)}, bf16[64,7168]{1,0:T(8,128)(2,1)}, u32[]{:S(2)}) copy-start(bf16[64,7168]{1,0:T(8,128)(2,1)} %get-tuple-element.137) | copy-start | bytes 2752516
  122.8 35.9 %collective-permute-start.7 = (bf16[64,7168]{1,0:T(8,128)(2,1)}, bf16[64,7168]{1,0:T(8,128)(2,1)}, u32[]{:S(2)}, u32[]{:S(2)}) collective-permute-start(bf16[64,7168]{1,0:T(8,128)(2,1)} %get-tuple-element.135), channel_id=1, source_target_pairs={{0,8},{2,10},{4,12},{6,14},{8,0},{10,2},{12,4},{14,6},{16,24},{18,... | collective-permute-start | bytes 2752520 | tf_op jit(solution)/shard_map/ppermute | solution.py:379
  126.6 37.7 %collective-permute-start.9 = (bf16[64,7168]{1,0:T(8,128)(2,1)S(1)}, bf16[64,7168]{1,0:T(8,128)(2,1)}, u32[]{:S(2)}, u32[]{:S(2)}) collective-permute-start(bf16[64,7168]{1,0:T(8,128)(2,1)S(1)} %copy-done.20), channel_id=1, source_target_pairs={{0,16},{2,18},{4,20},{6,22},{8,24},{10,26},{12,28},{14,30},{16,0},... | collective-permute-start | bytes 2752520 | tf_op jit(solution)/shard_map/ppermute | solution.py:379
  129.1 35.2 %collective-permute-start.12 = (bf16[2,128,1792]{2,1,0:T(8,128)(2,1)}, bf16[2,128,1792]{2,1,0:T(8,128)(2,1)S(1)}, u32[]{:S(2)}, u32[]{:S(2)}) collective-permute-start(bf16[2,128,1792]{2,1,0:T(8,128)(2,1)} %shard_map.107.refs_0_), channel_id=1, source_target_pairs={{0,2},{2,0},{4,6},{6,4},{8,10},{10,8},{12,14},{14,12},{16,18},{18,... | collective-permute-start | bytes 2752520 | tf_op jit(solution)/shard_map/ppermute | solution.py:379
  129.1 2.0 copy-start.2
  131.2 7.4 %copy-start.19 = (f32[2,2,32,512]{3,2,1,0:T(8,128)S(1)}, f32[2,2,32,512]{3,2,1,0:T(8,128)}, u32[]{:S(2)}) copy-start(f32[2,2,32,512]{3,2,1,0:T(8,128)} %copy-done.18) | copy-start | bytes 786436
  139.5 33.9 %copy-start.17 = (f32[1,2,32,512]{3,2,1,0:T(8,128)}, f32[1,2,32,512]{3,2,1,0:T(8,128)S(1)}, u32[]{:S(2)}) copy-start(f32[1,2,32,512]{3,2,1,0:T(8,128)S(1)} %slice_add_fusion) | copy-start | bytes 393220
  164.3 9.1 %copy-start.12 = (bf16[2,128,1792]{2,1,0:T(8,128)(2,1)}, bf16[2,128,1792]{2,1,0:T(8,128)(2,1)S(1)}, u32[]{:S(2)}) copy-start(bf16[2,128,1792]{2,1,0:T(8,128)(2,1)S(1)} %collective-permute-done.12.refs_1_) | copy-start | bytes 2752516
  164.3 7.8 %collective-permute-start.17 = (f32[32,512]{1,0:T(8,128)S(1)}, f32[32,512]{1,0:T(8,128)S(1)}, u32[]{:S(2)}, u32[]{:S(2)}) collective-permute-start(f32[32,512]{1,0:T(8,128)S(1)} %select_bitcast_fusion.3), channel_id=1, source_target_pairs={{0,16},{2,18},{4,20},{6,22},{8,24},{10,26},{12,28},{14,30},{16,0},... | collective-permute-start | bytes 196616 | tf_op jit(solution)/shard_map/ppermute | solution.py:379
  167.1 15.2 %collective-permute-start.18 = (bf16[1024,256]{1,0:T(8,128)(2,1)}, bf16[1024,256]{1,0:T(8,128)(2,1)}, u32[]{:S(2)}, u32[]{:S(2)}) collective-permute-start(bf16[1024,256]{1,0:T(8,128)(2,1)} %pad_maximum_fusion), channel_id=1, source_target_pairs={{0,4},{2,6},{4,0},{6,2},{8,12},{10,14},{12,8},{14,10},{16,20},{18,... | collective-permute-start | bytes 1572872 | tf_op jit(solution)/shard_map/ppermute | solution.py:379
  167.6 37.5 %collective-permute-start.14 = (bf16[64,7168]{1,0:T(8,128)(2,1)}, bf16[64,7168]{1,0:T(8,128)(2,1)}, u32[]{:S(2)}, u32[]{:S(2)}) collective-permute-start(bf16[64,7168]{1,0:T(8,128)(2,1)} %get-tuple-element.152), channel_id=1, source_target_pairs={{0,8},{2,10},{4,12},{6,14},{8,0},{10,2},{12,4},{14,6},{16,24},{18,... | collective-permute-start | bytes 2752520 | tf_op jit(solution)/shard_map/ppermute | solution.py:379
  170.3 34.8 %collective-permute-start.15 = (bf16[64,7168]{1,0:T(8,128)(2,1)}, bf16[64,7168]{1,0:T(8,128)(2,1)}, u32[]{:S(2)}, u32[]{:S(2)}) collective-permute-start(bf16[64,7168]{1,0:T(8,128)(2,1)} %collective-permute-done.7.refs_1_.refs_6_), channel_id=1, source_target_pairs={{0,4},{2,6},{4,0},{6,2},{8,12},{10,14},{12,8},{14,10},{16,20},{18,... | collective-permute-start | bytes 2752520 | tf_op jit(solution)/shard_map/ppermute | solution.py:379
  171.9 38.4 %collective-permute-start.16 = (bf16[64,7168]{1,0:T(8,128)(2,1)}, bf16[64,7168]{1,0:T(8,128)(2,1)}, u32[]{:S(2)}, u32[]{:S(2)}) collective-permute-start(bf16[64,7168]{1,0:T(8,128)(2,1)} %get-tuple-element.154), channel_id=1, source_target_pairs={{0,16},{2,18},{4,20},{6,22},{8,24},{10,26},{12,28},{14,30},{16,0},... | collective-permute-start | bytes 2752520 | tf_op jit(solution)/shard_map/ppermute | solution.py:379
  172.1 38.1 %collective-permute-start.20 = (bf16[64,7168]{1,0:T(8,128)(2,1)}, bf16[64,7168]{1,0:T(8,128)(2,1)}, u32[]{:S(2)}, u32[]{:S(2)}) collective-permute-start(bf16[64,7168]{1,0:T(8,128)(2,1)} %collective-permute-done.9.refs_3_.refs_6_), channel_id=1, source_target_pairs={{0,2},{2,0},{4,6},{6,4},{8,10},{10,8},{12,14},{14,12},{16,18},{18,... | collective-permute-start | bytes 2752520 | tf_op jit(solution)/shard_map/ppermute | solution.py:379
  210.2 3.7 %collective-permute-start.22 = (bf16[64,7168]{1,0:T(8,128)(2,1)}, bf16[64,7168]{1,0:T(8,128)(2,1)}, u32[]{:S(2)}, u32[]{:S(2)}) collective-permute-start(bf16[64,7168]{1,0:T(8,128)(2,1)} %collective-permute-done.16.refs_4_.refs_7_), channel_id=1, source_target_pairs={{0,2},{2,0},{4,6},{6,4},{8,10},{10,8},{12,14},{14,12},{16,18},{18,... | collective-permute-start | bytes 2752520 | tf_op jit(solution)/shard_map/ppermute | solution.py:379
  210.3 37.2 %collective-permute-start.21 = (bf16[64,7168]{1,0:T(8,128)(2,1)}, bf16[64,7168]{1,0:T(8,128)(2,1)}, u32[]{:S(2)}, u32[]{:S(2)}) collective-permute-start(bf16[64,7168]{1,0:T(8,128)(2,1)} %collective-permute-done.14.refs_2_.refs_7_), channel_id=1, source_target_pairs={{0,4},{2,6},{4,0},{6,2},{8,12},{10,14},{12,8},{14,10},{16,20},{18,... | collective-permute-start | bytes 2752520 | tf_op jit(solution)/shard_map/ppermute | solution.py:379
  210.7 53.9 %collective-permute-start.24 = (bf16[2,128,1792]{2,1,0:T(8,128)(2,1)}, bf16[2,128,1792]{2,1,0:T(8,128)(2,1)}, u32[]{:S(2)}, u32[]{:S(2)}) collective-permute-start(bf16[2,128,1792]{2,1,0:T(8,128)(2,1)} %shard_map.107.refs_0_), channel_id=1, source_target_pairs={{0,16},{2,18},{4,20},{6,22},{8,24},{10,26},{12,28},{14,30},{16,0},... | collective-permute-start | bytes 2752520 | tf_op jit(solution)/shard_map/ppermute | solution.py:379
  214.0 2.0 copy-start.3
  216.0 10.2 %copy-start.25 = (f32[32,512]{1,0:T(8,128)S(1)}, f32[32,512]{1,0:T(8,128)}, u32[]{:S(2)}) copy-start(f32[32,512]{1,0:T(8,128)} %bitcast_add_fusion.1) | copy-start | bytes 196612
  224.7 40.0 %collective-permute-start.27 = (f16[512,512]{1,0:T(8,128)(2,1)}, f16[512,512]{1,0:T(8,128)(2,1)}, u32[]{:S(2)}, u32[]{:S(2)}) collective-permute-start(f16[512,512]{1,0:T(8,128)(2,1)} %convert_element_type.32), channel_id=1, source_target_pairs={{0,1},{1,0},{2,3},{3,2},{4,5},{5,4},{6,7},{7,6},{8,9},{9,8},{10,11... | collective-permute-start | bytes 1572872 | tf_op jit(solution)/shard_map/ppermute | solution.py:382
  226.2 6.5 %collective-permute-start.23 = (f32[32,512]{1,0:T(8,128)S(1)}, f32[32,512]{1,0:T(8,128)S(1)}, u32[]{:S(2)}, u32[]{:S(2)}) collective-permute-start(f32[32,512]{1,0:T(8,128)S(1)} %copy-done.25), channel_id=1, source_target_pairs={{0,8},{2,10},{4,12},{6,14},{8,0},{10,2},{12,4},{14,6},{16,24},{18,... | collective-permute-start | bytes 196616 | tf_op jit(solution)/shard_map/ppermute | solution.py:379
  232.7 14.7 %copy-start.28 = (f32[32,512]{1,0:T(8,128)}, f32[32,512]{1,0:T(8,128)S(1)}, u32[]{:S(2)}) copy-start(f32[32,512]{1,0:T(8,128)S(1)} %collective-permute-done.23) | copy-start | bytes 196612
  244.4 20.3 %collective-permute-start.28 = (f16[256,512]{1,0:T(8,128)(2,1)}, f16[256,512]{1,0:T(8,128)(2,1)S(1)}, u32[]{:S(2)}, u32[]{:S(2)}) collective-permute-start(f16[256,512]{1,0:T(8,128)(2,1)} %convert_element_type.33), channel_id=1, source_target_pairs={{0,1},{1,0},{2,3},{3,2},{4,5},{5,4},{6,7},{7,6},{8,9},{9,8},{10,11... | collective-permute-start | bytes 786440 | tf_op jit(solution)/shard_map/ppermute | solution.py:382
  245.8 18.8 %collective-permute-start.25 = (f32[32,512]{1,0:T(8,128)S(1)}, f32[32,512]{1,0:T(8,128)S(1)}, u32[]{:S(2)}, u32[]{:S(2)}) collective-permute-start(f32[32,512]{1,0:T(8,128)S(1)} %copy-done.25), channel_id=1, source_target_pairs={{0,4},{2,6},{4,0},{6,2},{8,12},{10,14},{12,8},{14,10},{16,20},{18,... | collective-permute-start | bytes 196616 | tf_op jit(solution)/shard_map/ppermute | solution.py:379
  247.4 17.2 %collective-permute-start.26 = (f32[32,512]{1,0:T(8,128)S(1)}, f32[32,512]{1,0:T(8,128)S(1)}, u32[]{:S(2)}, u32[]{:S(2)}) collective-permute-start(f32[32,512]{1,0:T(8,128)S(1)} %collective-permute-done.23), channel_id=1, source_target_pairs={{0,4},{2,6},{4,0},{6,2},{8,12},{10,14},{12,8},{14,10},{16,20},{18,... | collective-permute-start | bytes 196616 | tf_op jit(solution)/shard_map/ppermute | solution.py:379
  264.6 4.8 %copy-start.14 = (f32[256,512]{1,0:T(8,128)}, f32[256,512]{1,0:T(8,128)S(1)}, u32[]{:S(2)}) copy-start(f32[256,512]{1,0:T(8,128)S(1)} %get-tuple-element.221) | copy-start | bytes 1572868
  264.6 3.5 %copy-start.7 = (f32[512,512]{1,0:T(8,128)S(1)}, f32[512,512]{1,0:T(8,128)}, u32[]{:S(2)}) copy-start(f32[512,512]{1,0:T(8,128)} %copy-done.6) | copy-start | bytes 3145732
  264.6 4.7 %copy-start.30 = (f32[32,512]{1,0:T(8,128)}, f32[32,512]{1,0:T(8,128)S(1)}, u32[]{:S(2)}) copy-start(f32[32,512]{1,0:T(8,128)S(1)} %collective-permute-done.25) | copy-start | bytes 196612
  264.6 4.7 %copy-start.32 = (f32[32,512]{1,0:T(8,128)}, f32[32,512]{1,0:T(8,128)S(1)}, u32[]{:S(2)}) copy-start(f32[32,512]{1,0:T(8,128)S(1)} %collective-permute-done.26) | copy-start | bytes 196612
  264.7 11.1 %collective-permute-start.34 = (bf16[2,128,1792]{2,1,0:T(8,128)(2,1)}, bf16[2,128,1792]{2,1,0:T(8,128)(2,1)}, u32[]{:S(2)}, u32[]{:S(2)}) collective-permute-start(bf16[2,128,1792]{2,1,0:T(8,128)(2,1)} %collective-permute-done.24.refs_2_), channel_id=1, source_target_pairs={{0,2},{2,0},{4,6},{6,4},{8,10},{10,8},{12,14},{14,12},{16,18},{18,... | collective-permute-start | bytes 2752520 | tf_op jit(solution)/shard_map/ppermute | solution.py:379
  265.6 18.8 %collective-permute-start.33 = (f32[256,512]{1,0:T(8,128)}, f32[256,512]{1,0:T(8,128)}, u32[]{:S(2)}, u32[]{:S(2)}) collective-permute-start(f32[256,512]{1,0:T(8,128)} %convert_add_fusion.2), channel_id=1, source_target_pairs={{0,8},{2,10},{4,12},{6,14},{8,0},{10,2},{12,4},{14,6},{16,24},{18,... | collective-permute-start | bytes 1572872 | tf_op jit(solution)/shard_map/ppermute | solution.py:379
  270.2 14.4 %collective-permute-start.32 = (f32[256,512]{1,0:T(8,128)}, f32[256,512]{1,0:T(8,128)}, u32[]{:S(2)}, u32[]{:S(2)}) collective-permute-start(f32[256,512]{1,0:T(8,128)} %get-tuple-element.238), channel_id=1, source_target_pairs={{0,4},{2,6},{4,0},{6,2},{8,12},{10,14},{12,8},{14,10},{16,20},{18,... | collective-permute-start | bytes 1572872 | tf_op jit(solution)/shard_map/ppermute | solution.py:379
  271.8 12.8 %collective-permute-start.29 = (f32[256,1792]{1,0:T(8,128)}, f32[256,1792]{1,0:T(8,128)}, u32[]{:S(2)}, u32[]{:S(2)}) collective-permute-start(f32[256,1792]{1,0:T(8,128)} %get-tuple-element.193), channel_id=1, source_target_pairs={{0,2},{2,0},{4,6},{6,4},{8,10},{10,8},{12,14},{14,12},{16,18},{18,... | collective-permute-start | bytes 5505032 | tf_op jit(solution)/shard_map/ppermute | solution.py:379
  271.8 2.0 copy-start.31
  273.1 2.6 copy-start.13
  273.2 11.2 %collective-permute-start.31 = (f16[256,512]{1,0:T(8,128)(2,1)S(1)}, f16[256,512]{1,0:T(8,128)(2,1)S(1)}, u32[]{:S(2)}, u32[]{:S(2)}) collective-permute-start(f16[256,512]{1,0:T(8,128)(2,1)S(1)} %convert_element_type.34), channel_id=1, source_target_pairs={{0,1},{1,0},{2,3},{3,2},{4,5},{5,4},{6,7},{7,6},{8,9},{9,8},{10,11... | collective-permute-start | bytes 786440 | tf_op jit(solution)/shard_map/ppermute | solution.py:382
  284.4 2.1 copy-start.10
  284.4 2.1 copy-start.21
  287.9 23.8 %collective-permute-start.30 = (f16[128,1792]{1,0:T(8,128)(2,1)}, f16[128,1792]{1,0:T(8,128)(2,1)}, u32[]{:S(2)}, u32[]{:S(2)}) collective-permute-start(f16[128,1792]{1,0:T(8,128)(2,1)} %slice_convert_fusion), channel_id=1, source_target_pairs={{0,16},{2,18},{4,20},{6,22},{8,24},{10,26},{12,28},{14,30},{16,0},... | collective-permute-start | bytes 1376264 | tf_op jit(solution)/shard_map/ppermute | solution.py:379
  288.6 2.6 copy-start.15
  288.6 2.6 copy-start.22
  290.0 23.1 %copy-start.11 = (f32[128,1792]{1,0:T(8,128)S(1)}, f32[128,1792]{1,0:T(8,128)}, u32[]{:S(2)}) copy-start(f32[128,1792]{1,0:T(8,128)} %copy-done.10) | copy-start | bytes 2752516
  292.1 27.0 %collective-permute-start.35 = (f32[256,512]{1,0:T(8,128)}, f32[256,512]{1,0:T(8,128)S(1)}, u32[]{:S(2)}, u32[]{:S(2)}) collective-permute-start(f32[256,512]{1,0:T(8,128)} %convert_add_fusion.1), channel_id=1, source_target_pairs={{0,12},{2,14},{4,8},{6,10},{8,4},{10,6},{12,0},{14,2},{16,28},{18,... | collective-permute-start | bytes 1572872 | tf_op jit(solution)/shard_map/ppermute | solution.py:379
  315.0 12.7 %collective-permute-start.36 = (f32[2,32,1792]{2,1,0:T(8,128)}, f32[2,32,1792]{2,1,0:T(8,128)S(1)}, u32[]{:S(2)}, u32[]{:S(2)}) collective-permute-start(f32[2,32,1792]{2,1,0:T(8,128)} %get-tuple-element.228), channel_id=1, source_target_pairs={{0,4},{2,6},{4,0},{6,2},{8,12},{10,14},{12,8},{14,10},{16,20},{18,... | collective-permute-start | bytes 1376264 | tf_op jit(solution)/shard_map/ppermute | solution.py:379
  315.5 13.6 %collective-permute-start.37 = (f32[2,32,1792]{2,1,0:T(8,128)}, f32[2,32,1792]{2,1,0:T(8,128)S(1)}, u32[]{:S(2)}, u32[]{:S(2)}) collective-permute-start(f32[2,32,1792]{2,1,0:T(8,128)} %get-tuple-element.229), channel_id=1, source_target_pairs={{0,8},{2,10},{4,12},{6,14},{8,0},{10,2},{12,4},{14,6},{16,24},{18,... | collective-permute-start | bytes 1376264 | tf_op jit(solution)/shard_map/ppermute | solution.py:379
  315.5 23.1 %collective-permute-start.38 = (f32[2,32,1792]{2,1,0:T(8,128)}, f32[2,32,1792]{2,1,0:T(8,128)S(1)}, u32[]{:S(2)}, u32[]{:S(2)}) collective-permute-start(f32[2,32,1792]{2,1,0:T(8,128)} %get-tuple-element.230), channel_id=1, source_target_pairs={{0,12},{2,14},{4,8},{6,10},{8,4},{10,6},{12,0},{14,2},{16,28},{18,... | collective-permute-start | bytes 1376264 | tf_op jit(solution)/shard_map/ppermute | solution.py:379
  319.1 21.9 %copy-start.1 = (bf16[256,512]{1,0:T(8,128)(2,1)S(1)}, bf16[256,512]{1,0:T(8,128)(2,1)}, u32[]{:S(2)}) copy-start(bf16[256,512]{1,0:T(8,128)(2,1)} %param.13) | copy-start | bytes 786436
  (9 other events, 13.8 us)

commit v4 on v3

--- a/solution.py
+++ b/solution.py
@@ -64,9 +64,9 @@
     out[...] = source[...]
 
 
-def anchor(value):
-    return pl.pallas_call(
-        anchor_kernel, out_shape=jax.ShapeDtypeStruct(value.shape, value.dtype), cost_estimate=long_op()
+def anchor(value, cost=long_op):
+    return pl.pallas_call(
+        anchor_kernel, out_shape=jax.ShapeDtypeStruct(value.shape, value.dtype), cost_estimate=cost()
     )(value)
 
 
@@ -159,7 +159,7 @@
         out_shape=[jax.ShapeDtypeStruct((depth, extent), jnp.float32)] * (t * blocks),
         compiler_params=pltpu.CompilerParams(vmem_limit_bytes=VMEM),
         cost_estimate=short_op(),
-    )(flag.reshape(1), *tokens, *flat, *ready)
+    )(flag, *tokens, *flat, *ready)
     return [list(outs[e * blocks : (e + 1) * blocks]) for e in range(t)]
 
 
@@ -184,7 +184,7 @@
         for (value, k, _), pieces in zip(saved, tokens):
             value = value[k * rank : (k + 1) * rank]
             block = jnp.concatenate(pieces, axis=0)
-            block = lax.dynamic_slice(block, (0, place * part), (depth, part))
+            block = lax.dynamic_slice(block, (0, place[0] * part), (depth, part))
             total = total + jnp.dot(value, block, preferred_element_type=jnp.float32)
         return total[: rank // 2], total[rank // 2 :]
     tile = part // 2 if part % 256 == 0 else part
@@ -202,7 +202,7 @@
         out_shape=[jax.ShapeDtypeStruct((rank // 2, part), jnp.float32)] * 2,
         compiler_params=pltpu.CompilerParams(vmem_limit_bytes=VMEM),
         cost_estimate=short_op(),
-    )(place.reshape(1), *[value for value, _, _ in saved], *flat)
+    )(place, *[value for value, _, _ in saved], *flat)
 
 
 def encode_kernel(na, group, first, second, *outs):
@@ -218,7 +218,7 @@
     part = width // na
     if part % 128:
         both = powered(jnp.stack([first, second])).reshape(2, rows, na, part)
-        return xor_order([both[:, :, k] for k in range(na)], group)
+        return xor_order([both[:, :, k] for k in range(na)], group[0])
     return list(
         pl.pallas_call(
             functools.partial(encode_kernel, na),
@@ -231,7 +231,7 @@
             out_shape=[jax.ShapeDtypeStruct((2, rows, part), jnp.bfloat16)] * na,
             compiler_params=pltpu.CompilerParams(vmem_limit_bytes=VMEM),
             cost_estimate=short_op(),
-        )(group.reshape(1), first, second)
+        )(group, first, second)
     )
 
 
@@ -294,7 +294,7 @@
         first = 0.9 * rot_first + 0.1 * gradient
         second = 0.95 * rot_second + 0.05 * gradient * gradient
         both = jnp.stack([first, second]).reshape(2, na, rows, part)
-        return xor_order([both[:, k] for k in range(na)], group)
+        return xor_order([both[:, k] for k in range(na)], group[0])
     whole = pl.BlockSpec((height, part), lambda i, g: (0, 0))
     return pl.pallas_call(
         functools.partial(blend_kernel, na),
@@ -307,7 +307,7 @@
         out_shape=[jax.ShapeDtypeStruct((2, rows, part), jnp.float32)] * na,
         compiler_params=pltpu.CompilerParams(vmem_limit_bytes=VMEM),
         cost_estimate=short_op(),
-    )(group.reshape(1), rot_first, rot_second, gradient)
+    )(group, rot_first, rot_second, gradient)
 
 
 def finish_kernel(na, group, *refs):
@@ -325,7 +325,7 @@
     na = len(pieces)
     _, rows, part = pieces[0].shape
     if part % 128:
-        both = jnp.concatenate(xor_order(pieces, group), axis=2)
+        both = jnp.concatenate(xor_order(pieces, group[0]), axis=2)
         return both[0], both[1], both[0] / (jnp.sqrt(both[1]) + 1e-08)
     return pl.pallas_call(
         functools.partial(finish_kernel, na),
@@ -338,7 +338,7 @@
         out_shape=[jax.ShapeDtypeStruct((rows, na * part), jnp.float32)] * 3,
         compiler_params=pltpu.CompilerParams(vmem_limit_bytes=VMEM),
         cost_estimate=short_op(),
-    )(group.reshape(1), *pieces)
+    )(group, *pieces)
 
 
 def place_kernel(na, place, *refs):
@@ -355,7 +355,7 @@
     tokens, extent = pieces[0].shape
     if extent % 256:
         halves = [p[:, k * extent // 2 : (k + 1) * extent // 2] for p in pieces for k in range(2)]
-        return jnp.concatenate(xor_order(halves, place), axis=1)
+        return jnp.concatenate(xor_order(halves, place[0]), axis=1)
     return pl.pallas_call(
         functools.partial(place_kernel, na),
         grid_spec=pltpu.PrefetchScalarGridSpec(
@@ -367,7 +367,7 @@
         out_shape=jax.ShapeDtypeStruct((tokens, na * extent), jnp.float32),
         compiler_params=pltpu.CompilerParams(vmem_limit_bytes=VMEM),
         cost_estimate=short_op(),
-    )(place.reshape(1), *pieces)
+    )(place, *pieces)
 
 
 def make_step(n, t):
@@ -398,15 +398,11 @@
         drows = weight.shape[0]
         tops = range(1, t)
 
-        def pieces_of(value):
-            cuts = [0, value.shape[0] // 2, value.shape[0] * 3 // 4, value.shape[0]]
-            return [value[lo:hi] for lo, hi in zip(cuts[:-1], cuts[1:])]
-
         last, others = strides[0], strides[1:]
 
         def chunks_of(value):
-            cuts = [0, value.shape[0] // 2, value.shape[0] * 3 // 4, value.shape[0]]
-            return [value[lo:hi] for lo, hi in zip(cuts[:-1], cuts[1:])]
+            cut = value.shape[0] * 5 // 8
+            return [value[:cut], value[cut:]]
 
         token_cuts, weight_cuts = chunks_of(grad_out), chunks_of(weight)
         a, w = {}, {}
@@ -434,7 +430,7 @@
             return [k for k in a if k[1] == p and k[0] & last and k[0] != last]
 
         def blocks_of(j):
-            return [grad_out] if j == 0 else [a[j, p] for p in range(3) if (j, p) in a]
+            return [grad_out] if j == 0 else [a[j, p] for p in range(2) if (j, p) in a]
 
         def hypercube(bits):
             order = [0]
@@ -442,28 +438,23 @@
                 order += [k ^ bit for k in order]
             return order
 
-        order = hypercube(strides)
+        order = hypercube(others + [last])
+        at_group, flag, at_column = group.reshape(1), (top ^ x).reshape(1), (2 * group + core).reshape(1)
 
         for bit in others:
             a[bit, 0] = swap(grad_out, 2 * bit)
         send(0, token_cuts[0], weight_cuts[0])
         w_core = swap(weight, 1)
-        ticket = anchor(jnp.full((8, 128), group, jnp.int32))
-        ticket, first_moment, second_moment, saved, new_basis = together(
-            ticket, first_moment, second_moment, saved, new_basis
-        )
+        ticket = jnp.full((8, 128), group, jnp.int32)
 
         local = contract_rows(new_basis, basis).reshape(t, na, 2, rows, rank)
         local = scatter([local[:, :, 0], local[:, :, 1]], core, 1)
-        local = jnp.stack(xor_order([local[:, k] for k in range(na)], group))
+        local = dict(enumerate(xor_order([local[:, k] for k in range(na)], group)))
 
         def halve(local, bit):
-            keep, give = local[: local.shape[0] // 2], local[local.shape[0] // 2 :]
-            return keep + swap(give, 2 * bit)
-
-        local = halve(local, strides[0])
-
-        ready = {k: [(code, 0)] for k, code in enumerate(encode(first_moment, second_moment, group, na))}
+            give = [k for k in local if k & bit]
+            found = swap(jnp.stack([local[k] for k in give]), 2 * bit)
+            return {k ^ bit: local[k ^ bit] + found[i] for i, k in enumerate(give)}
 
         def exchange_codes(bit):
             moving = [k for k in ready if k & bit]
@@ -474,21 +465,34 @@
                 ready[k ^ bit] += [(buffer, at + m) for m in range(count)]
                 at += count
 
-        def settle_codes(*values):
-            arrays = {id(block[0]): block[0] for blocks in ready.values() for block in blocks}
+        def settle_blocks(blocks, *values):
+            arrays = {id(block[0]): block[0] for block in blocks}
             held, values = together(list(arrays.values()), values)
             names = dict(zip(arrays, held))
+            return [(names[id(block[0])], *block[1:]) for block in blocks], *values
+
+        def settle_codes(*values):
+            keys = [k for k in ready for _ in ready[k]]
+            blocks, *values = settle_blocks([block for k in ready for block in ready[k]], *values)
             for k in ready:
-                ready[k] = [(names[id(value)], m) for value, m in ready[k]]
+                ready[k] = [block for key, block in zip(keys, blocks) if key == k]
             return values
-
-        exchange_codes(strides[0])
 
         saved = saved.reshape(tokens, t, na, 2, rows)
         saved = jnp.stack(xor_order([saved[:, :, :, k] for k in range(2)], core), axis=1)
         saved = jnp.stack(xor_order([saved[:, :, k] for k in range(t)], top), axis=2)
-        saved_all = saved.reshape(tokens, rank).T
-        saved_list = [(saved_all, 0, 1)]
+        saved_list = [(saved.reshape(tokens, rank).T, 0, 1)]
+        for bit in others:
+            local = halve(local, bit)
+        w_core, first_moment, second_moment = together(w_core, first_moment, second_moment)
+        ready = {k: [(code, 0)] for k, code in enumerate(encode(first_moment, second_moment, at_group, na))}
+        for bit in others:
+            exchange_codes(bit)
+
+        def exchange_saved(bit):
+            both = [value[k * rank : (k + 1) * rank] for value, k, _ in saved_list]
+            both = swap(jnp.concatenate(both, axis=0), 2 * bit)
+            saved_list.extend([(both, k, len(saved_list)) for k in range(len(saved_list))])
 
         spot = lax.broadcasted_iota(jnp.int32, (rank, rank), 1)
         block, within = spot // rows, spot % rows
@@ -497,75 +501,51 @@
         arrival = (lax.broadcasted_iota(jnp.int32, (rank, rank), 0) == source * rows + within).astype(jnp.float32)
 
         keys_a, keys_w = keys_of(0)
-        (ticket, local, saved_all, arrival, token_cut, weight_cut, w_core) = settle_codes(
+        ticket, local, arrival, token_cut, weight_cut, w_core = settle_codes(
             *settle(
                 keys_a + [(bit, 0) for bit in others],
                 keys_w,
                 ticket,
                 local,
-                saved_all,
                 arrival,
                 token_cuts[1],
                 weight_cuts[1],
                 w_core,
             )
         )
-        for bit in others:
-            exchange_codes(bit)
-            local = halve(local, bit)
+        exchange_codes(last)
+        local = halve(local, last)
+        send(1, token_cut, weight_cut)
         forward(0)
-        send(1, token_cut, weight_cut)
         ticket = anchor(ticket)
         ticket, w_core = together(ticket, w_core)
         own_rows = [weight, w_core]
         near_tokens = [j for j in range(na) if not j & last]
         far_tokens = [j for j in range(na) if j & last]
         own_products = multiply([value for j in near_tokens for value in blocks_of(j)], own_rows)
-        (ticket,) = settle_codes(ticket)
+        saved_list, ticket, local, own_products = settle_blocks(saved_list, *settle_codes(ticket, local, own_products))
+        for bit in others:
+            exchange_saved(bit)
+        own = scatter([local[0][k] for k in range(t)], top, top_unit)
         near = stack_rows(ready[0], rows)
-        near_other = swap(near, 1)
-        saved_list = [(saved_all, 0, 1), (swap(saved_all, 2 * last), 0, 1)]
+        saved_list, ticket, own, near = settle_blocks(saved_list, ticket, own, near)
+        ticket = anchor(ticket, short_op)
 
         keys_a, keys_w = keys_of(1)
-        ticket, local, near, near_other, saved_next, own_products, token_cut, weight_cut = settle(
-            keys_a + forwarded(0),
-            keys_w,
-            ticket,
-            local,
-            near,
-            near_other,
-            saved_list[1][0],
-            own_products,
-            token_cuts[2],
-            weight_cuts[2],
+        ticket, own, near, own_products = settle(
+            keys_a + forwarded(0), keys_w + [(dz, 0) for dz in tops], ticket, own, near, own_products
         )
-        saved_list[1] = (saved_next, 0, 1)
-        own = scatter([local[0, k] for k in range(t)], top, top_unit)
         forward(1)
-        send(2, token_cut, weight_cut)
-        for bit in others:
-            both = [value[k * rank : (k + 1) * rank] for value, k, _ in saved_list]
-            both = swap(jnp.concatenate(both, axis=0), 2 * bit)
-            saved_list += [(both, k, len(saved_list)) for k in range(len(saved_list))]
-        other_rows = {dz: [swap(w[dz, p], 1) for p in (0, 1)] for dz in tops}
-        ticket = anchor(ticket)
-
-        keys_a, keys_w = keys_of(2)
-        saved_arrays = {id(value): value for value, _, _ in saved_list}
-        ticket, own, near, held, other_rows = settle(
-            keys_a + forwarded(1), keys_w, ticket, own, near, list(saved_arrays.values()), other_rows
-        )
-        names = dict(zip(saved_arrays, held))
-        saved_list = [(names[id(value)], k, count) for value, k, count in saved_list]
-        forward(2)
         far = {dz: swap(near, dz * top_unit) for dz in tops}
         inter = [own] + [swap(own, 2 * bit) for bit in strides[:1]]
-        other_rows = [[w[dz, p] for p in range(3)] + other_rows[dz] + [swap(w[dz, 2], 1)] for dz in tops]
+        other_rows = [[w[dz, p] for p in range(2)] + [swap(w[dz, p], 1) for p in range(2)] for dz in tops]
         ticket = anchor(ticket)
-
-        def parts_of(js, rows_of, ready_products=()):
+        saved_list, ticket, near = settle_blocks(saved_list, ticket, near)
+        exchange_saved(last)
+        near_other = swap(near, 1)
+
+        def parts_of(js, rows_of, flag, ready_products=()):
             blocks = [value for j in js for value in blocks_of(j)]
-            flag = ticket[0, 0] ^ group ^ top ^ x
             made = multiply_parts(blocks, rows_of, flag, tokens * len(js), ready_products)
             return [m[0] for m in made]
 
@@ -575,20 +555,18 @@
         def total_of(parts, arrived):
             return functools.reduce(jnp.add, [parts[0]] + [value.astype(jnp.float32) for value in arrived])
 
-        near_parts = parts_of(near_tokens, other_rows, [own_products])
+        ticket, flag = together(ticket, flag)
+        near_parts = parts_of(near_tokens, other_rows, flag, [own_products])
         near_arrived = over_tp(near_parts)
-        ticket, near_parts, inter = together(ticket, near_parts, inter)
-        for bit in strides[1:]:
-            inter += [swap(value, 2 * bit) for value in inter]
-        inter = [inter[order.index(k)] for k in range(na)]
+        ticket, near_parts, flag = together(ticket, near_parts, flag)
         all_rows = [own_rows] + other_rows
-        next_parts = parts_of(far_tokens[:1], all_rows)
+        next_parts = parts_of(far_tokens[:1], all_rows, flag)
         next_arrived = over_tp(next_parts)
 
-        ticket, next_parts = settle(forwarded(2), [], ticket, next_parts)
-        keep, send_half = gradient_part(saved_list, [blocks_of(j) for j in order], group, part)
-        ticket, keep, send_half = together(ticket, keep, send_half)
-        last_parts = parts_of(far_tokens[1:], all_rows) if far_tokens[1:] else None
+        ticket, next_parts, at_group = settle(forwarded(1), [], ticket, next_parts, at_group)
+        keep, send_half = gradient_part(saved_list, [blocks_of(j) for j in order], at_group, part)
+        ticket, keep, send_half, flag = together(ticket, keep, send_half, flag)
+        last_parts = parts_of(far_tokens[1:], all_rows, flag) if far_tokens[1:] else None
 
         (ticket, far, inter, near_arrived, near_parts, next_arrived, next_parts, last_parts, keep, send_half) = together(
             ticket, far, inter, near_arrived, near_parts, next_arrived, next_parts, last_parts, keep, send_half
@@ -597,7 +575,9 @@
         last_arrived = over_tp(last_parts) if far_tokens[1:] else None
         far_other = {dz: swap(far[dz], 1) for dz in tops}
         g = (keep + got).reshape(t, na * rows, part)
-        late_g = [swap(g[dz].astype(jnp.float16), dz * top_unit) for dz in tops]
+        far_g = [g[dz].astype(jnp.float16) for dz in tops]
+        ticket, g, far_g = together(ticket, g[0], far_g)
+        late_g = [swap(value, dz * top_unit) for dz, value in zip(tops, far_g)]
 
         def go_home(js, parts, arrived):
             total = total_of(parts, arrived)
@@ -608,6 +588,9 @@
         sums.update(go_home(far_tokens[:1], next_parts, next_arrived))
         ticket = anchor(ticket)
         ticket, inter, near, near_other = together(ticket, inter, near, near_other)
+        for bit in strides[1:]:
+            inter += [swap(value, 2 * bit) for value in inter]
+        inter = [inter[hypercube(strides).index(k)] for k in range(na)]
         inter = exact_dot(jnp.concatenate(xor_order(inter, group), axis=0), arrival)
         codes = [near, near_other]
         for dz in tops:
@@ -617,16 +600,14 @@
         ticket, last_arrived, sums, rot_first, rot_second = together(ticket, last_arrived, sums, rot_first, rot_second)
         if far_tokens[1:]:
             sums.update(go_home(far_tokens[1:], last_parts, last_arrived))
-        ticket = anchor(ticket)
-        group = ticket[0, 0]
-        g, late_g, group = together(g, late_g, group)
-        gradient = g[0]
+        g, late_g, at_group, ticket = together(g, late_g, at_group, ticket)
+        gradient = g
         for value in late_g:
             gradient = gradient + value.astype(jnp.float32)
-        pieces = blend(rot_first, rot_second, gradient, group, na)
+        pieces = blend(rot_first, rot_second, gradient, at_group, na)
         pieces = [pieces[0]] + [swap(pieces[j], 2 * j) for j in range(1, na)]
-        grad_input = place_columns([sums[j] for j in range(na)], 2 * group + core)
-        first_new, second_new, update = finish(pieces, group)
+        grad_input = place_columns([sums[j] for j in range(na)], at_column)
+        first_new, second_new, update = finish(pieces, ticket[0, :1])
         return (grad_input, first_new, second_new, update)
 
     return per_device

time: 342 us -> 314 us (0.918)
  other arithmetic: 19.3 us -> 10.1 us
  starting transfers between devices: 43.3 us -> 38.2 us
  waiting for transfers between devices: 185 us -> 181 us
  Pallas kernels: 65.8 us -> 62.1 us
    ppermute x36 -> x32, starting transfers between devices: 39.8 us -> 34.5 us  [swap(): return lax.ppermute(value, 'seq', [(s, s ^ mask) for s in range(n)])]
    ppermute x36 -> x32, waiting for transfers between devices: 185 us -> 181 us  [swap(): return lax.ppermute(value, 'seq', [(s, s ^ mask) for s in range(n)])]
    slice x8 -> x5, local copies, waits for them, and re-layouts: 14 us -> 11.2 us  [the longest x4 9.98 us: chunks_of(): return [value[:cut], value[cut:]]]
    pallas_call x6 -> x4, Pallas kernels: 7.85 us -> 5.24 us  [anchor(): pl.pallas_call(anchor_kernel, out_shape=jax.ShapeDtypeStruct(value.shape,...]
    unnamed x68 -> x45, local copies, waits for them, and re-layouts: 5.62 us -> 7.1 us
  transfers between devices with their start and end apart: 39 -> 35, of which waited for: 14 -> 15; matrix products, arithmetic and copies ran while one was open for 10% -> 8% of each run, Pallas kernels for 18% -> 19%
where the time goes in v4:
time: 314 us
  waiting for transfers between devices  181 us (58%)
  Pallas kernels  62.1 us (20%)
  starting transfers between devices  38.2 us (12%)
  local copies, waits for them, and re-layouts  19 us (6%)
  other arithmetic  10.1 us (3%)
    ppermute x32, waiting for transfers between devices, swap(): return lax.ppermute(value, 'seq', [(s, s ^ mask) for s in range(n)])  181 us
    ppermute x32, starting transfers between devices, swap(): return lax.ppermute(value, 'seq', [(s, s ^ mask) for s in range(n)])  34.5 us
    pallas_call x3, Pallas kernels, multiply_parts(): pl.pallas_call(functools.partial(parts_kernel, len(tokens), [len(group) f...  25.5 us
    slice x4, local copies, waits for them, and re-layouts, chunks_of(): return [value[:cut], value[cut:]]  9.98 us
    pallas_call x1, Pallas kernels, rotate(): pl.pallas_call(functools.partial(rotate_kernel, len(codes)), grid=(part /...  8.97 us
    unnamed x45, local copies, waits for them, and re-layouts  7.1 us
    pallas_call x1, Pallas kernels, multiply(): pl.pallas_call(functools.partial(multiply_kernel, len(tokens)), grid=(wid...  6.96 us
  transfers between devices with their start and end apart: 35, of which 15 were waited for; matrix products, arithmetic and copies ran while one was open for 8% of the time, Pallas kernels for 19%

profile of v4, /device:TPU:0, one launch (start us, length us, event | category | flops | bytes accessed | tf_op | source)
XLA Modules:
  0.0 313.7 jit_solution(13554529414897020854)
XLA Ops:
  1.2 2.6 collective-permute-start.3
  3.8 1.3 fusion.44
  5.4 3.3 %slice.72 = bf16[160,7168]{1,0:T(8,128)(2,1)} slice(bf16[256,7168]{1,0:T(8,128)(2,1)} %refs_4_.1), slice={[0:160], [0:7168]} | slice | bytes 4587520 | tf_op jit(solution)/shard_map/slice | solution.py:405
  8.7 1.6 collective-permute-start.2
  10.2 1.5 slice.73
  11.8 2.6 collective-permute-start.4
  14.6 1.2 fusion.16
  16.8 2.7 slice.82
  19.5 2.5 slice.83
  22.6 1.4 collective-permute-start.1
  24.8 65.0 %collective-permute-done.6 = f32[2,2,32,512]{3,2,1,0:T(8,128)S(1)} collective-permute-done((f32[2,2,32,512]{3,2,1,0:T(8,128)S(1)}, f32[2,2,32,512]{3,2,1,0:T(8,128)S(1)}, u32[]{:S(2)}, u32[]{:S(2)}) %collective-permute-start.6) | collective-permute-done | bytes 262176 | tf_op jit(solution)/shard_map/ppermute | solution.py:379
  89.8 0.8 fusion.29
  90.6 18.1 %collective-permute-done.2.refs_0_.refs_6_ = bf16[160,7168]{1,0:T(8,128)(2,1)} collective-permute-done((bf16[160,7168]{1,0:T(8,128)(2,1)}, bf16[160,7168]{1,0:T(8,128)(2,1)}, u32[]{:S(2)}, u32[]{:S(2)}) %collective-permute-start.2) | collective-permute-done | bytes 2293792 | tf_op jit(solution)/shard_map/ppermute | solution.py:379
  108.7 5.4 %collective-permute-done.4.refs_2_.refs_4_ = bf16[160,7168]{1,0:T(8,128)(2,1)} collective-permute-done((bf16[160,7168]{1,0:T(8,128)(2,1)}, bf16[160,7168]{1,0:T(8,128)(2,1)}, u32[]{:S(2)}, u32[]{:S(2)}) %collective-permute-start.4) | collective-permute-done | bytes 2293792 | tf_op jit(solution)/shard_map/ppermute | solution.py:379
  114.7 0.9 collective-permute-start.8
  115.6 0.8 shard_map.104
  117.2 2.0 collective-permute-start.10
  119.2 3.0 collective-permute-start.9
  122.2 1.3 shard_map.105.source
  123.5 2.0 copy-done.2
  125.6 2.0 copy-done.5
  127.6 7.0 %shard_map.106.refs_6_ = f32[512,512]{1,0:T(8,128)S(1)} custom-call(bf16[256,7168]{1,0:T(8,128)(2,1)S(1)} %copy-done.2, bf16[256,7168]{1,0:T(8,128)(2,1)} %collective-permute-done.3.refs_1_.refs_5_, bf16[256,7168]{1,0:T(8,128)(2,1)S(1)} %copy-done.5, bf16[256,7168]{1,0:T(8,128)(2,1)} %collective-permute-done.refs_3_), custom_call_target="tpu_custom_call" | custom-call | flops 1024 | bytes 1024 | tf_op jit(solution)/shard_map/pallas_call | solution.py:98
  134.6 17.2 %collective-permute-done.11 = f32[1,2,32,512]{3,2,1,0:T(8,128)} collective-permute-done((f32[1,2,32,512]{3,2,1,0:T(8,128)}, f32[1,2,32,512]{3,2,1,0:T(8,128)}, u32[]{:S(2)}, u32[]{:S(2)}) %collective-permute-start.11) | collective-permute-done | bytes 131104 | tf_op jit(solution)/shard_map/ppermute | solution.py:379
  151.8 0.9 bitcast_add_fusion
  152.7 8.9 %collective-permute-done.10.refs_2_.refs_3_ = bf16[2,64,1792]{2,1,0:T(8,128)(2,1)} collective-permute-done((bf16[2,64,1792]{2,1,0:T(8,128)(2,1)}, bf16[2,64,1792]{2,1,0:T(8,128)(2,1)}, u32[]{:S(2)}, u32[]{:S(2)}) %collective-permute-start.10) | collective-permute-done | bytes 458784 | tf_op jit(solution)/shard_map/ppermute | solution.py:379
  162.3 1.0 collective-permute-start.12
  163.3 2.0 shard_map.107.refs_0_
  165.3 27.6 %collective-permute-done.13 = f32[32,512]{1,0:T(8,128)S(1)} collective-permute-done((f32[32,512]{1,0:T(8,128)S(1)}, f32[32,512]{1,0:T(8,128)S(1)}, u32[]{:S(2)}, u32[]{:S(2)}) %collective-permute-start.13) | collective-permute-done | bytes 65568 | tf_op jit(solution)/shard_map/ppermute | solution.py:379
  193.6 1.3 shard_map.108.source
  196.0 1.3 shard_map.109.source
  197.3 1.0 pad_maximum_fusion
  198.3 2.4 collective-permute-start.17
  200.8 0.9 collective-permute-done.16.refs_5_.refs_7_
  201.7 2.0 copy-done.3
  203.7 7.5 %shard_map.110 = (f32[512,512]{1,0:T(8,128)S(1)}, f32[512,512]{1,0:T(8,128)S(1)}) custom-call(s32[1]{0:T(128)} %bitcast.32.flag, bf16[256,7168]{1,0:T(8,128)(2,1)S(1)} %copy-done.3, bf16[256,7168]{1,0:T(8,128)(2,1)} %collective-permute-done.3.refs_1_.refs_5_, bf16[160,7168]{1,0:T(8,128)(2,1)} %collective-permute-done.4.refs_2_.refs_4_, ...), custom_call_target="tpu_custom_call" | custom-call | flops 1024 | bytes 1024 | tf_op jit(solution)/shard_map/pallas_call | solution.py:149
  211.3 1.6 collective-permute-start.20
  212.9 9.0 %shard_map.111 = (f32[256,512]{1,0:T(8,128)S(1)}, f32[256,512]{1,0:T(8,128)S(1)}) custom-call(s32[1]{0:T(128)} %bitcast.32.flag, bf16[160,7168]{1,0:T(8,128)(2,1)} %collective-permute-done.2.refs_0_.refs_6_, bf16[96,7168]{1,0:T(8,128)(2,1)} %collective-permute-done.7.refs_1_.refs_7_, bf16[256,7168]{1,0:T(8,128)(2,1)} %refs_2_.5, ...), custom_call_target="tpu_custom_call" | custom-call | flops 1024 | bytes 1024 | tf_op jit(solution)/shard_map/pallas_call | solution.py:149
  222.5 5.4 %collective-permute-done.14.refs_9_.refs_1_ = bf16[96,7168]{1,0:T(8,128)(2,1)} collective-permute-done((bf16[96,7168]{1,0:T(8,128)(2,1)}, bf16[96,7168]{1,0:T(8,128)(2,1)}, u32[]{:S(2)}, u32[]{:S(2)}) %collective-permute-start.14) | collective-permute-done | bytes 1376288 | tf_op jit(solution)/shard_map/ppermute | solution.py:379
  228.0 4.6 %shard_map.112 = (f32[256,1792]{1,0:T(8,128)S(1)}, f32[256,1792]{1,0:T(8,128)S(1)}) custom-call(s32[1]{0:T(128)} %bitcast.1.group.place, bf16[512,256]{1,0:T(8,128)(2,1)S(1)} %bitcast.129, bf16[512,256]{1,0:T(8,128)(2,1)} %collective-permute-done.12.refs_1_, bf16[1024,256]{1,0:T(8,128)(2,1)S(1)} %collective-permute-done.17.refs_2_.refs_3_, ...), custom_call_target="tpu_custom_call" | custom-call | flops 1024 | bytes 1024 | tf_op jit(solution)/shard_map/pallas_call | solution.py:193
  232.6 9.0 %shard_map.113 = (f32[256,512]{1,0:T(8,128)S(1)}, f32[256,512]{1,0:T(8,128)S(1)}) custom-call(s32[1]{0:T(128)} %bitcast.32.flag, bf16[160,7168]{1,0:T(8,128)(2,1)} %collective-permute-done.8.refs_8_.refs_0_, bf16[96,7168]{1,0:T(8,128)(2,1)} %collective-permute-done.14.refs_9_.refs_1_, bf16[256,7168]{1,0:T(8,128)(2,1)} %refs_2_.5, ...), custom_call_target="tpu_custom_call" | custom-call | flops 1024 | bytes 1024 | tf_op jit(solution)/shard_map/pallas_call | solution.py:149
  242.3 0.9 convert_add_fusion.3
  243.2 2.0 collective-permute-start.26
  245.2 1.1 convert_add_fusion
  246.3 1.0 collective-permute-done.22
  247.6 1.2 slice_convert_fusion
  248.7 1.4 shard_map.114
  250.1 1.5 collective-permute-start.27
  252.3 1.5 collective-permute-start.25
  253.9 1.0 collective-permute-done.27
  254.9 1.5 collective-permute-start.24
  256.6 2.3 collective-permute-start.31
  259.7 9.0 %shard_map.115 = (f32[128,1792]{1,0:T(8,128)S(1)}, f32[128,1792]{1,0:T(8,128)S(1)}) custom-call(f32[128,512]{1,0:T(8,128)S(1)} %fusion.19.inter, bf16[2,128,1792]{2,1,0:T(8,128)(2,1)} %shard_map.107.refs_0_, bf16[2,128,1792]{2,1,0:T(8,128)(2,1)} %collective-permute-done.23.refs_1_, bf16[2,128,1792]{2,1,0:T(8,128)(2,1)} %collective-permute-done.18.refs_2_, ...), custom_call_target="tpu_custom_call" | custom-call | flops 1024 | bytes 1024 | tf_op jit(solution)/shard_map/pallas_call | solution.py:269
  268.7 0.9 convert_add_fusion.2
  269.6 1.6 collective-permute-start.30
  271.2 7.4 %collective-permute-done.31 = f16[128,1792]{1,0:T(8,128)(2,1)S(1)} collective-permute-done((f16[128,1792]{1,0:T(8,128)(2,1)S(1)}, f16[128,1792]{1,0:T(8,128)(2,1)S(1)}, u32[]{:S(2)}, u32[]{:S(2)}) %collective-permute-start.31) | collective-permute-done | bytes 458784 | tf_op jit(solution)/shard_map/ppermute | solution.py:379
  278.7 1.3 shard_map.117
  280.0 1.2 collective-permute-start.32
  281.3 2.2 collective-permute-start.34
  283.5 1.2 slice.94
  284.7 5.9 %collective-permute-done.30.refs_3_ = f32[256,512]{1,0:T(8,128)S(1)} collective-permute-done((f32[256,512]{1,0:T(8,128)}, f32[256,512]{1,0:T(8,128)S(1)}, u32[]{:S(2)}, u32[]{:S(2)}) %collective-permute-start.30) | collective-permute-done | bytes 524320 | tf_op jit(solution)/shard_map/ppermute | solution.py:379
  290.6 2.6 shard_map.116
  293.1 7.2 %collective-permute-done.32.refs_1_ = f32[2,32,1792]{2,1,0:T(8,128)S(1)} collective-permute-done((f32[2,32,1792]{2,1,0:T(8,128)}, f32[2,32,1792]{2,1,0:T(8,128)S(1)}, u32[]{:S(2)}, u32[]{:S(2)}) %collective-permute-start.32) | collective-permute-done | bytes 458784 | tf_op jit(solution)/shard_map/ppermute | solution.py:379
  300.3 9.9 %collective-permute-done.34.refs_3_ = f32[2,32,1792]{2,1,0:T(8,128)} collective-permute-done((f32[2,32,1792]{2,1,0:T(8,128)}, f32[2,32,1792]{2,1,0:T(8,128)}, u32[]{:S(2)}, u32[]{:S(2)}) %collective-permute-start.34) | collective-permute-done | bytes 458784 | tf_op jit(solution)/shard_map/ppermute | solution.py:379
  310.3 3.5 %shard_map.118 = (f32[32,7168]{1,0:T(8,128)}, f32[32,7168]{1,0:T(8,128)}, f32[32,7168]{1,0:T(8,128)}) custom-call(s32[1]{0:T(128)} %bitcast.33.group, f32[2,32,1792]{2,1,0:T(8,128)S(1)} %get-tuple-element.231.refs_0_, f32[2,32,1792]{2,1,0:T(8,128)S(1)} %collective-permute-done.32.refs_1_, f32[2,32,1792]{2,1,0:T(8,128)S(1)} %collective-permute-done.33.refs_2_, ...), custom_call_target="tpu_custom_call" | custom-call | flops 1024 | bytes 1024 | tf_op jit(solution)/shard_map/pallas_call | solution.py:330
  (105 shorter events, 10.6 us)
Async XLA Ops:
  0.6 3.1 copy-start
  0.6 21.3 %collective-permute-start = (bf16[256,7168]{1,0:T(8,128)(2,1)}, bf16[256,7168]{1,0:T(8,128)(2,1)}, u32[]{:S(2)}, u32[]{:S(2)}) collective-permute-start(bf16[256,7168]{1,0:T(8,128)(2,1)} %refs_2_.5), channel_id=1, source_target_pairs={{0,2},{2,0},{4,6},{6,4},{8,10},{10,8},{12,14},{14,12},{16,18},{18,... | collective-permute-start | bytes 11010056 | tf_op jit(solution)/shard_map/ppermute | solution.py:379
  1.2 112.9 %collective-permute-start.3 = (bf16[256,7168]{1,0:T(8,128)(2,1)}, bf16[256,7168]{1,0:T(8,128)(2,1)}, u32[]{:S(2)}, u32[]{:S(2)}) collective-permute-start(bf16[256,7168]{1,0:T(8,128)(2,1)} %refs_4_.1), channel_id=1, source_target_pairs={{0,4},{2,6},{4,0},{6,2},{8,12},{10,14},{12,8},{14,10},{16,20},{18,... | collective-permute-start | bytes 11010056 | tf_op jit(solution)/shard_map/ppermute | solution.py:379
  5.1 5.1 %copy-start.4 = (bf16[256,7168]{1,0:T(8,128)(2,1)S(1)}, bf16[256,7168]{1,0:T(8,128)(2,1)}, u32[]{:S(2)}) copy-start(bf16[256,7168]{1,0:T(8,128)(2,1)} %refs_2_.5) | copy-start | bytes 11010052
  5.1 10.6 %collective-permute-start.5 = (f32[2,4,32,512]{3,2,1,0:T(8,128)S(1)}, f32[2,4,32,512]{3,2,1,0:T(8,128)S(1)}, u32[]{:S(2)}, u32[]{:S(2)}) collective-permute-start(f32[2,4,32,512]{3,2,1,0:T(8,128)S(1)} %select_bitcast_fusion), channel_id=1, source_target_pairs={{0,2},{2,0},{4,6},{6,4},{8,10},{10,8},{12,14},{14,12},{16,18},{18,... | collective-permute-start | bytes 1572872 | tf_op jit(solution)/shard_map/ppermute | solution.py:379
  8.7 5.7 %copy-start.17 = (bf16[256,512]{1,0:T(8,128)(2,1)S(1)}, bf16[256,512]{1,0:T(8,128)(2,1)}, u32[]{:S(2)}) copy-start(bf16[256,512]{1,0:T(8,128)(2,1)} %param.9) | copy-start | bytes 786436
  8.7 100.0 %collective-permute-start.2 = (bf16[160,7168]{1,0:T(8,128)(2,1)}, bf16[160,7168]{1,0:T(8,128)(2,1)}, u32[]{:S(2)}, u32[]{:S(2)}) collective-permute-start(bf16[160,7168]{1,0:T(8,128)(2,1)} %slice.72), channel_id=1, source_target_pairs={{0,8},{2,10},{4,12},{6,14},{8,0},{10,2},{12,4},{14,6},{16,24},{18,... | collective-permute-start | bytes 6881288 | tf_op jit(solution)/shard_map/ppermute | solution.py:379
  11.8 102.3 %collective-permute-start.4 = (bf16[160,7168]{1,0:T(8,128)(2,1)}, bf16[160,7168]{1,0:T(8,128)(2,1)}, u32[]{:S(2)}, u32[]{:S(2)}) collective-permute-start(bf16[160,7168]{1,0:T(8,128)(2,1)} %slice.73), channel_id=1, source_target_pairs={{0,16},{2,18},{4,20},{6,22},{8,24},{10,26},{12,28},{14,30},{16,0},... | collective-permute-start | bytes 6881288 | tf_op jit(solution)/shard_map/ppermute | solution.py:379
  16.0 73.7 %collective-permute-start.6 = (f32[2,2,32,512]{3,2,1,0:T(8,128)S(1)}, f32[2,2,32,512]{3,2,1,0:T(8,128)S(1)}, u32[]{:S(2)}, u32[]{:S(2)}) collective-permute-start(f32[2,2,32,512]{3,2,1,0:T(8,128)S(1)} %pad_maximum_fusion.1), channel_id=1, source_target_pairs={{0,4},{2,6},{4,0},{6,2},{8,12},{10,14},{12,8},{14,10},{16,20},{18,... | collective-permute-start | bytes 786440 | tf_op jit(solution)/shard_map/ppermute | solution.py:379
  16.8 5.2 %copy-start.10 = (f32[32,7168]{1,0:T(8,128)S(1)}, f32[32,7168]{1,0:T(8,128)}, u32[]{:S(2)}) copy-start(f32[32,7168]{1,0:T(8,128)} %first) | copy-start | bytes 2752516
  16.8 5.2 %copy-start.11 = (f32[32,7168]{1,0:T(8,128)S(1)}, f32[32,7168]{1,0:T(8,128)}, u32[]{:S(2)}) copy-start(f32[32,7168]{1,0:T(8,128)} %second) | copy-start | bytes 2752516
  22.6 93.0 %collective-permute-start.1 = (bf16[2,64,1792]{2,1,0:T(8,128)(2,1)S(1)}, bf16[2,64,1792]{2,1,0:T(8,128)(2,1)S(1)}, u32[]{:S(2)}, u32[]{:S(2)}) collective-permute-start(bf16[2,64,1792]{2,1,0:T(8,128)(2,1)S(1)} %shard_map.103), channel_id=1, source_target_pairs={{0,4},{2,6},{4,0},{6,2},{8,12},{10,14},{12,8},{14,10},{16,20},{18,... | collective-permute-start | bytes 1376264 | tf_op jit(solution)/shard_map/ppermute | solution.py:379
  114.7 80.2 %collective-permute-start.8 = (bf16[160,7168]{1,0:T(8,128)(2,1)}, bf16[160,7168]{1,0:T(8,128)(2,1)}, u32[]{:S(2)}, u32[]{:S(2)}) collective-permute-start(bf16[160,7168]{1,0:T(8,128)(2,1)} %collective-permute-done.2.refs_0_.refs_6_), channel_id=1, source_target_pairs={{0,4},{2,6},{4,0},{6,2},{8,12},{10,14},{12,8},{14,10},{16,20},{18,... | collective-permute-start | bytes 6881288 | tf_op jit(solution)/shard_map/ppermute | solution.py:379
  115.6 36.2 %collective-permute-start.11 = (f32[1,2,32,512]{3,2,1,0:T(8,128)}, f32[1,2,32,512]{3,2,1,0:T(8,128)}, u32[]{:S(2)}, u32[]{:S(2)}) collective-permute-start(f32[1,2,32,512]{3,2,1,0:T(8,128)} %bitcast.28), channel_id=1, source_target_pairs={{0,8},{2,10},{4,12},{6,14},{8,0},{10,2},{12,4},{14,6},{16,24},{18,... | collective-permute-start | bytes 393224 | tf_op jit(solution)/shard_map/ppermute | solution.py:379
  116.4 0.8 copy-start.8
  117.2 44.4 %collective-permute-start.10 = (bf16[2,64,1792]{2,1,0:T(8,128)(2,1)}, bf16[2,64,1792]{2,1,0:T(8,128)(2,1)}, u32[]{:S(2)}, u32[]{:S(2)}) collective-permute-start(bf16[2,64,1792]{2,1,0:T(8,128)(2,1)} %shard_map.104), channel_id=1, source_target_pairs={{0,8},{2,10},{4,12},{6,14},{8,0},{10,2},{12,4},{14,6},{16,24},{18,... | collective-permute-start | bytes 1376264 | tf_op jit(solution)/shard_map/ppermute | solution.py:379
  119.2 75.7 %collective-permute-start.7 = (bf16[96,7168]{1,0:T(8,128)(2,1)}, bf16[96,7168]{1,0:T(8,128)(2,1)}, u32[]{:S(2)}, u32[]{:S(2)}) collective-permute-start(bf16[96,7168]{1,0:T(8,128)(2,1)} %slice.82), channel_id=1, source_target_pairs={{0,8},{2,10},{4,12},{6,14},{8,0},{10,2},{12,4},{14,6},{16,24},{18,... | collective-permute-start | bytes 4128776 | tf_op jit(solution)/shard_map/ppermute | solution.py:379
  119.2 75.6 %collective-permute-start.9 = (bf16[96,7168]{1,0:T(8,128)(2,1)}, bf16[96,7168]{1,0:T(8,128)(2,1)}, u32[]{:S(2)}, u32[]{:S(2)}) collective-permute-start(bf16[96,7168]{1,0:T(8,128)(2,1)} %slice.83), channel_id=1, source_target_pairs={{0,16},{2,18},{4,20},{6,22},{8,24},{10,26},{12,28},{14,30},{16,0},... | collective-permute-start | bytes 4128776 | tf_op jit(solution)/shard_map/ppermute | solution.py:379
  123.5 2.0 copy-start.2
  125.5 2.0 copy-start.5
  127.6 24.2 %copy-start.15 = (f32[2,32,512]{2,1,0:T(8,128)S(1)}, f32[2,32,512]{2,1,0:T(8,128)}, u32[]{:S(2)}) copy-start(f32[2,32,512]{2,1,0:T(8,128)} %get-tuple-element.145) | copy-start | bytes 393220
  127.6 34.7 %copy-start.6 = (bf16[256,2,2,4,32]{0,4,3,2,1:T(8,128)(2,1)S(1)}, bf16[256,2,2,4,32]{0,4,3,2,1:T(8,128)(2,1)}, u32[]{:S(2)}) copy-start(bf16[256,2,2,4,32]{0,4,3,2,1:T(8,128)(2,1)} %pad_maximum_fusion.2) | copy-start | bytes 786436
  127.6 35.7 %copy-start.9 = (bf16[2,64,1792]{2,1,0:T(8,128)(2,1)S(1)}, bf16[2,64,1792]{2,1,0:T(8,128)(2,1)}, u32[]{:S(2)}) copy-start(bf16[2,64,1792]{2,1,0:T(8,128)(2,1)} %copy-done.8) | copy-start | bytes 1376260
  161.6 31.3 %collective-permute-start.13 = (f32[32,512]{1,0:T(8,128)S(1)}, f32[32,512]{1,0:T(8,128)S(1)}, u32[]{:S(2)}, u32[]{:S(2)}) collective-permute-start(f32[32,512]{1,0:T(8,128)S(1)} %select_bitcast_fusion.1), channel_id=1, source_target_pairs={{0,16},{2,18},{4,20},{6,22},{8,24},{10,26},{12,28},{14,30},{16,0},... | collective-permute-start | bytes 196616 | tf_op jit(solution)/shard_map/ppermute | solution.py:379
  162.3 31.3 %collective-permute-start.12 = (bf16[512,256]{1,0:T(8,128)(2,1)S(1)}, bf16[512,256]{1,0:T(8,128)(2,1)}, u32[]{:S(2)}, u32[]{:S(2)}) collective-permute-start(bf16[512,256]{1,0:T(8,128)(2,1)S(1)} %bitcast.127), channel_id=1, source_target_pairs={{0,4},{2,6},{4,0},{6,2},{8,12},{10,14},{12,8},{14,10},{16,20},{18,... | collective-permute-start | bytes 786440 | tf_op jit(solution)/shard_map/ppermute | solution.py:379
  194.9 6.8 %collective-permute-start.15 = (bf16[160,7168]{1,0:T(8,128)(2,1)}, bf16[160,7168]{1,0:T(8,128)(2,1)}, u32[]{:S(2)}, u32[]{:S(2)}) collective-permute-start(bf16[160,7168]{1,0:T(8,128)(2,1)} %collective-permute-done.4.refs_2_.refs_4_), channel_id=1, source_target_pairs={{0,2},{2,0},{4,6},{6,4},{8,10},{10,8},{12,14},{14,12},{16,18},{18,... | collective-permute-start | bytes 6881288 | tf_op jit(solution)/shard_map/ppermute | solution.py:379
  195.0 6.7 %collective-permute-start.16 = (bf16[96,7168]{1,0:T(8,128)(2,1)}, bf16[96,7168]{1,0:T(8,128)(2,1)}, u32[]{:S(2)}, u32[]{:S(2)}) collective-permute-start(bf16[96,7168]{1,0:T(8,128)(2,1)} %collective-permute-done.9.refs_3_.refs_5_), channel_id=1, source_target_pairs={{0,2},{2,0},{4,6},{6,4},{8,10},{10,8},{12,14},{14,12},{16,18},{18,... | collective-permute-start | bytes 4128776 | tf_op jit(solution)/shard_map/ppermute | solution.py:379
  195.5 32.5 %collective-permute-start.14 = (bf16[96,7168]{1,0:T(8,128)(2,1)}, bf16[96,7168]{1,0:T(8,128)(2,1)}, u32[]{:S(2)}, u32[]{:S(2)}) collective-permute-start(bf16[96,7168]{1,0:T(8,128)(2,1)} %collective-permute-done.7.refs_1_.refs_7_), channel_id=1, source_target_pairs={{0,4},{2,6},{4,0},{6,2},{8,12},{10,14},{12,8},{14,10},{16,20},{18,... | collective-permute-start | bytes 4128776 | tf_op jit(solution)/shard_map/ppermute | solution.py:379
  196.0 45.6 %collective-permute-start.18 = (bf16[2,128,1792]{2,1,0:T(8,128)(2,1)}, bf16[2,128,1792]{2,1,0:T(8,128)(2,1)}, u32[]{:S(2)}, u32[]{:S(2)}) collective-permute-start(bf16[2,128,1792]{2,1,0:T(8,128)(2,1)} %shard_map.107.refs_0_), channel_id=1, source_target_pairs={{0,16},{2,18},{4,20},{6,22},{8,24},{10,26},{12,28},{14,30},{16,0},... | collective-permute-start | bytes 2752520 | tf_op jit(solution)/shard_map/ppermute | solution.py:379
  196.0 1.3 copy-start.7
  198.3 29.6 %collective-permute-start.17 = (bf16[1024,256]{1,0:T(8,128)(2,1)S(1)}, bf16[1024,256]{1,0:T(8,128)(2,1)S(1)}, u32[]{:S(2)}, u32[]{:S(2)}) collective-permute-start(bf16[1024,256]{1,0:T(8,128)(2,1)S(1)} %pad_maximum_fusion), channel_id=1, source_target_pairs={{0,8},{2,10},{4,12},{6,14},{8,0},{10,2},{12,4},{14,6},{16,24},{18,... | collective-permute-start | bytes 1572872 | tf_op jit(solution)/shard_map/ppermute | solution.py:379
  201.7 2.0 copy-start.3
  211.3 30.4 %collective-permute-start.20 = (f16[512,512]{1,0:T(8,128)(2,1)S(1)}, f16[512,512]{1,0:T(8,128)(2,1)S(1)}, u32[]{:S(2)}, u32[]{:S(2)}) collective-permute-start(f16[512,512]{1,0:T(8,128)(2,1)S(1)} %convert_element_type.32), channel_id=1, source_target_pairs={{0,1},{1,0},{2,3},{3,2},{4,5},{5,4},{6,7},{7,6},{8,9},{9,8},{10,11... | collective-permute-start | bytes 1572872 | tf_op jit(solution)/shard_map/ppermute | solution.py:382
  212.9 15.1 %copy-start.18 = (f32[32,512]{1,0:T(8,128)S(1)}, f32[32,512]{1,0:T(8,128)}, u32[]{:S(2)}) copy-start(f32[32,512]{1,0:T(8,128)} %bitcast_add_fusion.1) | copy-start | bytes 196612
  221.9 19.7 %collective-permute-start.21 = (f16[256,512]{1,0:T(8,128)(2,1)S(1)}, f16[256,512]{1,0:T(8,128)(2,1)S(1)}, u32[]{:S(2)}, u32[]{:S(2)}) collective-permute-start(f16[256,512]{1,0:T(8,128)(2,1)S(1)} %convert_element_type.33), channel_id=1, source_target_pairs={{0,1},{1,0},{2,3},{3,2},{4,5},{5,4},{6,7},{7,6},{8,9},{9,8},{10,11... | collective-permute-start | bytes 786440 | tf_op jit(solution)/shard_map/ppermute | solution.py:382
  227.9 13.7 %collective-permute-start.19 = (f32[32,512]{1,0:T(8,128)S(1)}, f32[32,512]{1,0:T(8,128)S(1)}, u32[]{:S(2)}, u32[]{:S(2)}) collective-permute-start(f32[32,512]{1,0:T(8,128)S(1)} %copy-done.18), channel_id=1, source_target_pairs={{0,8},{2,10},{4,12},{6,14},{8,0},{10,2},{12,4},{14,6},{16,24},{18,... | collective-permute-start | bytes 196616 | tf_op jit(solution)/shard_map/ppermute | solution.py:379
  241.6 5.9 %copy-start.20 = (f32[32,512]{1,0:T(8,128)}, f32[32,512]{1,0:T(8,128)S(1)}, u32[]{:S(2)}) copy-start(f32[32,512]{1,0:T(8,128)S(1)} %collective-permute-done.19) | copy-start | bytes 196612
  241.7 5.7 %collective-permute-start.22 = (f32[256,1792]{1,0:T(8,128)S(1)}, f32[256,1792]{1,0:T(8,128)S(1)}, u32[]{:S(2)}, u32[]{:S(2)}) collective-permute-start(f32[256,1792]{1,0:T(8,128)S(1)} %get-tuple-element.198), channel_id=1, source_target_pairs={{0,2},{2,0},{4,6},{6,4},{8,10},{10,8},{12,14},{14,12},{16,18},{18,... | collective-permute-start | bytes 5505032 | tf_op jit(solution)/shard_map/ppermute | solution.py:379
  241.7 8.4 %collective-permute-start.23 = (bf16[2,128,1792]{2,1,0:T(8,128)(2,1)}, bf16[2,128,1792]{2,1,0:T(8,128)(2,1)}, u32[]{:S(2)}, u32[]{:S(2)}) collective-permute-start(bf16[2,128,1792]{2,1,0:T(8,128)(2,1)} %shard_map.107.refs_0_), channel_id=1, source_target_pairs={{0,2},{2,0},{4,6},{6,4},{8,10},{10,8},{12,14},{14,12},{16,18},{18,... | collective-permute-start | bytes 2752520 | tf_op jit(solution)/shard_map/ppermute | solution.py:379
  242.2 17.5 %collective-permute-start.29 = (bf16[2,128,1792]{2,1,0:T(8,128)(2,1)}, bf16[2,128,1792]{2,1,0:T(8,128)(2,1)}, u32[]{:S(2)}, u32[]{:S(2)}) collective-permute-start(bf16[2,128,1792]{2,1,0:T(8,128)(2,1)} %collective-permute-done.18.refs_2_), channel_id=1, source_target_pairs={{0,2},{2,0},{4,6},{6,4},{8,10},{10,8},{12,14},{14,12},{16,18},{18,... | collective-permute-start | bytes 2752520 | tf_op jit(solution)/shard_map/ppermute | solution.py:379
  243.2 25.5 %collective-permute-start.26 = (f32[256,512]{1,0:T(8,128)}, f32[256,512]{1,0:T(8,128)}, u32[]{:S(2)}, u32[]{:S(2)}) collective-permute-start(f32[256,512]{1,0:T(8,128)} %convert_add_fusion.3), channel_id=1, source_target_pairs={{0,8},{2,10},{4,12},{6,14},{8,0},{10,2},{12,4},{14,6},{16,24},{18,... | collective-permute-start | bytes 1572872 | tf_op jit(solution)/shard_map/ppermute | solution.py:379
  248.7 1.4 copy-start.21
  248.7 2.9 copy-start.19
  248.7 3.5 %copy-start.13 = (f32[512,512]{1,0:T(8,128)S(1)}, f32[512,512]{1,0:T(8,128)}, u32[]{:S(2)}) copy-start(f32[512,512]{1,0:T(8,128)} %convert_add_fusion) | copy-start | bytes 3145732
  250.1 6.5 %copy-start.16 = (f16[128,1792]{1,0:T(8,128)(2,1)S(1)}, f16[128,1792]{1,0:T(8,128)(2,1)}, u32[]{:S(2)}) copy-start(f16[128,1792]{1,0:T(8,128)(2,1)} %get-tuple-element.223) | copy-start | bytes 1376260
  250.1 8.9 %copy-start.12 = (f32[512,512]{1,0:T(8,128)S(1)}, f32[512,512]{1,0:T(8,128)}, u32[]{:S(2)}) copy-start(f32[512,512]{1,0:T(8,128)} %fusion.16) | copy-start | bytes 3145732
  250.1 4.8 %collective-permute-start.27 = (f32[32,512]{1,0:T(8,128)S(1)}, f32[32,512]{1,0:T(8,128)S(1)}, u32[]{:S(2)}, u32[]{:S(2)}) collective-permute-start(f32[32,512]{1,0:T(8,128)S(1)} %copy-done.21), channel_id=1, source_target_pairs={{0,4},{2,6},{4,0},{6,2},{8,12},{10,14},{12,8},{14,10},{16,20},{18,... | collective-permute-start | bytes 196616 | tf_op jit(solution)/shard_map/ppermute | solution.py:379
  251.7 5.0 %collective-permute-start.28 = (f32[32,512]{1,0:T(8,128)S(1)}, f32[32,512]{1,0:T(8,128)S(1)}, u32[]{:S(2)}, u32[]{:S(2)}) collective-permute-start(f32[32,512]{1,0:T(8,128)S(1)} %copy-done.19), channel_id=1, source_target_pairs={{0,4},{2,6},{4,0},{6,2},{8,12},{10,14},{12,8},{14,10},{16,20},{18,... | collective-permute-start | bytes 196616 | tf_op jit(solution)/shard_map/ppermute | solution.py:379
  252.3 16.4 %collective-permute-start.25 = (f32[256,512]{1,0:T(8,128)S(1)}, f32[256,512]{1,0:T(8,128)S(1)}, u32[]{:S(2)}, u32[]{:S(2)}) collective-permute-start(f32[256,512]{1,0:T(8,128)S(1)} %get-tuple-element.240), channel_id=1, source_target_pairs={{0,4},{2,6},{4,0},{6,2},{8,12},{10,14},{12,8},{14,10},{16,20},{18,... | collective-permute-start | bytes 1572872 | tf_op jit(solution)/shard_map/ppermute | solution.py:379
  254.9 13.8 %collective-permute-start.24 = (f16[256,512]{1,0:T(8,128)(2,1)S(1)}, f16[256,512]{1,0:T(8,128)(2,1)S(1)}, u32[]{:S(2)}, u32[]{:S(2)}) collective-permute-start(f16[256,512]{1,0:T(8,128)(2,1)S(1)} %convert_element_type.34), channel_id=1, source_target_pairs={{0,1},{1,0},{2,3},{3,2},{4,5},{5,4},{6,7},{7,6},{8,9},{9,8},{10,11... | collective-permute-start | bytes 786440 | tf_op jit(solution)/shard_map/ppermute | solution.py:382
  256.6 22.0 %collective-permute-start.31 = (f16[128,1792]{1,0:T(8,128)(2,1)S(1)}, f16[128,1792]{1,0:T(8,128)(2,1)S(1)}, u32[]{:S(2)}, u32[]{:S(2)}) collective-permute-start(f16[128,1792]{1,0:T(8,128)(2,1)S(1)} %copy-done.16), channel_id=1, source_target_pairs={{0,16},{2,18},{4,20},{6,22},{8,24},{10,26},{12,28},{14,30},{16,0},... | collective-permute-start | bytes 1376264 | tf_op jit(solution)/shard_map/ppermute | solution.py:379
  259.7 18.9 %copy-start.14 = (f32[128,1792]{1,0:T(8,128)S(1)}, f32[128,1792]{1,0:T(8,128)}, u32[]{:S(2)}) copy-start(f32[128,1792]{1,0:T(8,128)} %get-tuple-element.229) | copy-start | bytes 2752516
  269.6 21.0 %collective-permute-start.30 = (f32[256,512]{1,0:T(8,128)}, f32[256,512]{1,0:T(8,128)S(1)}, u32[]{:S(2)}, u32[]{:S(2)}) collective-permute-start(f32[256,512]{1,0:T(8,128)} %convert_add_fusion.2), channel_id=1, source_target_pairs={{0,12},{2,14},{4,8},{6,10},{8,4},{10,6},{12,0},{14,2},{16,28},{18,... | collective-permute-start | bytes 1572872 | tf_op jit(solution)/shard_map/ppermute | solution.py:379
  280.0 20.3 %collective-permute-start.32 = (f32[2,32,1792]{2,1,0:T(8,128)}, f32[2,32,1792]{2,1,0:T(8,128)S(1)}, u32[]{:S(2)}, u32[]{:S(2)}) collective-permute-start(f32[2,32,1792]{2,1,0:T(8,128)} %get-tuple-element.232), channel_id=1, source_target_pairs={{0,4},{2,6},{4,0},{6,2},{8,12},{10,14},{12,8},{14,10},{16,20},{18,... | collective-permute-start | bytes 1376264 | tf_op jit(solution)/shard_map/ppermute | solution.py:379
  281.3 19.1 %collective-permute-start.33 = (f32[2,32,1792]{2,1,0:T(8,128)}, f32[2,32,1792]{2,1,0:T(8,128)S(1)}, u32[]{:S(2)}, u32[]{:S(2)}) collective-permute-start(f32[2,32,1792]{2,1,0:T(8,128)} %get-tuple-element.233), channel_id=1, source_target_pairs={{0,8},{2,10},{4,12},{6,14},{8,0},{10,2},{12,4},{14,6},{16,24},{18,... | collective-permute-start | bytes 1376264 | tf_op jit(solution)/shard_map/ppermute | solution.py:379
  281.3 29.0 %collective-permute-start.34 = (f32[2,32,1792]{2,1,0:T(8,128)}, f32[2,32,1792]{2,1,0:T(8,128)}, u32[]{:S(2)}, u32[]{:S(2)}) collective-permute-start(f32[2,32,1792]{2,1,0:T(8,128)} %get-tuple-element.234), channel_id=1, source_target_pairs={{0,12},{2,14},{4,8},{6,10},{8,4},{10,6},{12,0},{14,2},{16,28},{18,... | collective-permute-start | bytes 1376264 | tf_op jit(solution)/shard_map/ppermute | solution.py:379
  290.6 23.1 %copy-start.1 = (bf16[256,512]{1,0:T(8,128)(2,1)S(1)}, bf16[256,512]{1,0:T(8,128)(2,1)}, u32[]{:S(2)}) copy-start(bf16[256,512]{1,0:T(8,128)(2,1)} %param.13) | copy-start | bytes 786436

commit v5 on v4

--- a/solution.py
+++ b/solution.py
@@ -9,6 +9,8 @@
 
 SCALE = 40.0
 POWER = 16
+GRAD_BOUND = 6.0
+WEIGHT_BOUND = 0.046875
 VMEM = 40 * 2**20
 
 
@@ -39,6 +41,22 @@
     return jnp.where(code < 0, -root, root)
 
 
+def sum_code(value, limit):
+    size = jnp.abs(value) * (1500.0 / limit)
+    size = size * size
+    size = size * size
+    size = size * size * size
+    return jnp.where(value < 0, -size, size).astype(jnp.bfloat16)
+
+
+def sum_value(code, limit):
+    code = code.astype(jnp.float32)
+    size = jnp.abs(code)
+    root = jnp.exp(jnp.log(jnp.maximum(size, 1e-38)) * (1.0 / 12)) * (limit / 1500.0)
+    root = jnp.where(size < 1e-38, 0.0, root)
+    return jnp.where(code < 0, -root, root)
+
+
 def xor_order(items, index):
     bit = 1
     while bit < len(items):
@@ -106,7 +124,7 @@
     )(*tokens, *rows)
 
 
-def parts_kernel(n_tokens, counts, given, blocks, flag, *refs):
+def parts_kernel(n_tokens, counts, given, blocks, limit, flag, *refs):
     t = len(counts) + given
     token_refs, at = refs[:n_tokens], n_tokens
     row_refs = []
@@ -135,10 +153,11 @@
             def _():
                 for e in range(t):
                     for j in range(blocks):
-                        outs[e * blocks + j][...] = candidates[e ^ f][j * depth : (j + 1) * depth, :]
-
-
-def multiply_parts(tokens, rows, flag, depth, ready=()):
+                        value = candidates[e ^ f][j * depth : (j + 1) * depth, :]
+                        outs[e * blocks + j][...] = sum_code(value, limit) if e else value
+
+
+def multiply_parts(tokens, rows, flag, depth, limit, ready=()):
     width = tokens[0].shape[1]
     tile = tile_of(width)
     height = sum(value.shape[0] for value in tokens)
@@ -147,7 +166,7 @@
     t = len(rows) + len(ready)
     flat = [value for group in rows for value in group]
     outs = pl.pallas_call(
-        functools.partial(parts_kernel, len(tokens), [len(group) for group in rows], len(ready), blocks),
+        functools.partial(parts_kernel, len(tokens), [len(group) for group in rows], len(ready), blocks, limit),
         grid_spec=pltpu.PrefetchScalarGridSpec(
             num_scalar_prefetch=1,
             grid=(width // tile,),
@@ -156,11 +175,38 @@
             out_specs=[pl.BlockSpec((depth, extent), lambda k, f: (0, 0))] * (t * blocks),
             scratch_shapes=[pltpu.VMEM((height, extent), jnp.float32)] * len(rows),
         ),
-        out_shape=[jax.ShapeDtypeStruct((depth, extent), jnp.float32)] * (t * blocks),
+        out_shape=[
+            jax.ShapeDtypeStruct((depth, extent), jnp.bfloat16 if e else jnp.float32)
+            for e in range(t)
+            for _ in range(blocks)
+        ],
         compiler_params=pltpu.CompilerParams(vmem_limit_bytes=VMEM),
         cost_estimate=short_op(),
     )(flag, *tokens, *flat, *ready)
     return [list(outs[e * blocks : (e + 1) * blocks]) for e in range(t)]
+
+
+def sum_kernel(n_codes, limit, keep, *refs):
+    codes, outs = refs[:n_codes], refs[n_codes:]
+    depth = outs[0].shape[0]
+    for k, out in enumerate(outs):
+        mine = slice(k * depth, (k + 1) * depth)
+        total = keep[mine, :]
+        for code in codes:
+            total = total + sum_value(code[mine, :], limit)
+        out[...] = total if out.dtype == jnp.float32 else sum_code(total, limit)
+
+
+def sum_parts(keep, codes, stay, limit):
+    depth = keep.shape[0] // len(stay)
+    return pl.pallas_call(
+        functools.partial(sum_kernel, len(codes), limit),
+        out_shape=[
+            jax.ShapeDtypeStruct((depth, keep.shape[1]), jnp.float32 if here else jnp.bfloat16) for here in stay
+        ],
+        compiler_params=pltpu.CompilerParams(vmem_limit_bytes=VMEM),
+        cost_estimate=short_op(),
+    )(keep, *codes)
 
 
 def gradient_kernel(counts, place, *refs):
@@ -306,7 +352,7 @@
         ),
         out_shape=[jax.ShapeDtypeStruct((2, rows, part), jnp.float32)] * na,
         compiler_params=pltpu.CompilerParams(vmem_limit_bytes=VMEM),
-        cost_estimate=short_op(),
+        cost_estimate=long_op(),
     )(group, rot_first, rot_second, gradient)
 
 
@@ -341,23 +387,25 @@
     )(group, *pieces)
 
 
-def place_kernel(na, place, *refs):
+def place_kernel(na, limit, place, *refs):
     out = refs[na]
     extent = refs[0].shape[1] // 2
     for j in range(na):
         for core in range(2):
             mine = pl.ds(pl.multiple_of((place[0] ^ (2 * j + core)) * extent, 128), extent)
-            out[:, mine] = refs[j][:, core * extent : (core + 1) * extent]
-
-
-def place_columns(pieces, place):
+            value = refs[j][:, core * extent : (core + 1) * extent]
+            out[:, mine] = value if value.dtype == jnp.float32 else sum_value(value, limit)
+
+
+def place_columns(pieces, place, limit):
     na = len(pieces)
     tokens, extent = pieces[0].shape
     if extent % 256:
+        pieces = [p if p.dtype == jnp.float32 else sum_value(p, limit) for p in pieces]
         halves = [p[:, k * extent // 2 : (k + 1) * extent // 2] for p in pieces for k in range(2)]
         return jnp.concatenate(xor_order(halves, place[0]), axis=1)
     return pl.pallas_call(
-        functools.partial(place_kernel, na),
+        functools.partial(place_kernel, na, limit),
         grid_spec=pltpu.PrefetchScalarGridSpec(
             num_scalar_prefetch=1,
             grid=(1,),
@@ -397,6 +445,7 @@
         rank = saved.shape[1]
         drows = weight.shape[0]
         tops = range(1, t)
+        limit = GRAD_BOUND * WEIGHT_BOUND * width * t
 
         last, others = strides[0], strides[1:]
 
@@ -546,14 +595,11 @@
 
         def parts_of(js, rows_of, flag, ready_products=()):
             blocks = [value for j in js for value in blocks_of(j)]
-            made = multiply_parts(blocks, rows_of, flag, tokens * len(js), ready_products)
+            made = multiply_parts(blocks, rows_of, flag, tokens * len(js), limit, ready_products)
             return [m[0] for m in made]
 
         def over_tp(parts):
-            return [swap_tp(parts[e].astype(jnp.float16), e) for e in tops]
-
-        def total_of(parts, arrived):
-            return functools.reduce(jnp.add, [parts[0]] + [value.astype(jnp.float32) for value in arrived])
+            return [swap_tp(parts[e], e) for e in tops]
 
         ticket, flag = together(ticket, flag)
         near_parts = parts_of(near_tokens, other_rows, flag, [own_products])
@@ -565,48 +611,49 @@
 
         ticket, next_parts, at_group = settle(forwarded(1), [], ticket, next_parts, at_group)
         keep, send_half = gradient_part(saved_list, [blocks_of(j) for j in order], at_group, part)
-        ticket, keep, send_half, flag = together(ticket, keep, send_half, flag)
-        last_parts = parts_of(far_tokens[1:], all_rows, flag) if far_tokens[1:] else None
-
-        (ticket, far, inter, near_arrived, near_parts, next_arrived, next_parts, last_parts, keep, send_half) = together(
-            ticket, far, inter, near_arrived, near_parts, next_arrived, next_parts, last_parts, keep, send_half
+
+        (ticket, far, inter, near_arrived, near_parts, next_arrived, next_parts, keep, send_half) = together(
+            ticket, far, inter, near_arrived, near_parts, next_arrived, next_parts, keep, send_half
         )
         got = swap(send_half, 1)
-        last_arrived = over_tp(last_parts) if far_tokens[1:] else None
         far_other = {dz: swap(far[dz], 1) for dz in tops}
+        for bit in strides[1:]:
+            found = swap(jnp.stack(inter), 2 * bit)
+            inter += [found[k] for k in range(len(inter))]
+        inter = [inter[hypercube(strides).index(k)] for k in range(na)]
         g = (keep + got).reshape(t, na * rows, part)
         far_g = [g[dz].astype(jnp.float16) for dz in tops]
         ticket, g, far_g = together(ticket, g[0], far_g)
         late_g = [swap(value, dz * top_unit) for dz, value in zip(tops, far_g)]
+        ticket = anchor(ticket)
+        ticket, near_parts, next_parts, inter = together(ticket, near_parts, next_parts, inter)
 
         def go_home(js, parts, arrived):
-            total = total_of(parts, arrived)
-            blocks = {j: total[k * tokens : (k + 1) * tokens] for k, j in enumerate(js)}
-            return {j: swap(block, 2 * j) if j else block for j, block in blocks.items()}
+            blocks = sum_parts(parts[0], arrived, [j == 0 for j in js], limit)
+            return {j: swap(block, 2 * j) if j else block for j, block in zip(js, blocks)}
 
         sums = go_home(near_tokens, near_parts, near_arrived)
         sums.update(go_home(far_tokens[:1], next_parts, next_arrived))
-        ticket = anchor(ticket)
-        ticket, inter, near, near_other = together(ticket, inter, near, near_other)
-        for bit in strides[1:]:
-            inter += [swap(value, 2 * bit) for value in inter]
-        inter = [inter[hypercube(strides).index(k)] for k in range(na)]
         inter = exact_dot(jnp.concatenate(xor_order(inter, group), axis=0), arrival)
         codes = [near, near_other]
         for dz in tops:
             codes += [far[dz], far_other[dz]]
         rot_first, rot_second = rotate(inter, codes)
-
-        ticket, last_arrived, sums, rot_first, rot_second = together(ticket, last_arrived, sums, rot_first, rot_second)
+        last_parts = []
         if far_tokens[1:]:
+            rot_first, rot_second, flag = together(rot_first, rot_second, flag)
+            last_parts = parts_of(far_tokens[1:], all_rows, flag)
+
+        g, late_g, at_group, ticket, sums, last_parts = together(g, late_g, at_group, ticket, sums, last_parts)
+        if far_tokens[1:]:
+            last_arrived = over_tp(last_parts)
             sums.update(go_home(far_tokens[1:], last_parts, last_arrived))
-        g, late_g, at_group, ticket = together(g, late_g, at_group, ticket)
         gradient = g
         for value in late_g:
             gradient = gradient + value.astype(jnp.float32)
         pieces = blend(rot_first, rot_second, gradient, at_group, na)
         pieces = [pieces[0]] + [swap(pieces[j], 2 * j) for j in range(1, na)]
-        grad_input = place_columns([sums[j] for j in range(na)], at_column)
+        grad_input = place_columns([sums[j] for j in range(na)], at_column, limit)
         first_new, second_new, update = finish(pieces, ticket[0, :1])
         return (grad_input, first_new, second_new, update)
 

time: 314 us -> 308 us (0.981)
  starting transfers between devices: 38.2 us -> 34.3 us
    ppermute x32 -> x31, waiting for transfers between devices: 181 us -> 177 us  [swap(): return lax.ppermute(value, 'seq', [(s, s ^ mask) for s in range(n)])]
    ppermute x32 -> x31, starting transfers between devices: 34.5 us -> 30.6 us  [swap(): return lax.ppermute(value, 'seq', [(s, s ^ mask) for s in range(n)])]
    unnamed x45 -> x67, local copies, waits for them, and re-layouts: 7.1 us -> 7.15 us
  transfers between devices with their start and end apart: 35 -> 34, of which waited for: 15 -> 16; matrix products, arithmetic and copies ran while one was open for 8% -> 7% of each run, Pallas kernels for 19% -> 20%
where the time goes in v5:
time: 308 us; the launch traced here: 307 us
  waiting for transfers between devices  178 us (58%)
  Pallas kernels  64.7 us (21%)
  starting transfers between devices  34.3 us (11%)
  local copies, waits for them, and re-layouts  19.6 us (6%)
  other arithmetic  7.81 us (3%)
    ppermute x31, waiting for transfers between devices, swap(): return lax.ppermute(value, 'seq', [(s, s ^ mask) for s in range(n)])  177 us
    ppermute x31, starting transfers between devices, swap(): return lax.ppermute(value, 'seq', [(s, s ^ mask) for s in range(n)])  30.6 us
    pallas_call x3, Pallas kernels, multiply_parts(): pl.pallas_call(functools.partial(parts_kernel, len(tokens), [len(group) f...  26.8 us
    slice x4, local copies, waits for them, and re-layouts, chunks_of(): return [value[:cut], value[cut:]]  10.1 us
    pallas_call x1, Pallas kernels, rotate(): pl.pallas_call(functools.partial(rotate_kernel, len(codes)), grid=(part /...  8.95 us
    unnamed x67, local copies, waits for them, and re-layouts  7.15 us
    pallas_call x1, Pallas kernels, multiply(): pl.pallas_call(functools.partial(multiply_kernel, len(tokens)), grid=(wid...  6.97 us
  transfers between devices with their start and end apart: 34, of which 16 were waited for; matrix products, arithmetic and copies ran while one was open for 7% of the time, Pallas kernels for 20%

profile of v5, /device:TPU:0, one launch (start us, length us, event | category | flops | bytes accessed | tf_op | source)
XLA Modules:
  0.0 307.0 jit_solution(6231676197700037198)
XLA Ops:
  1.2 2.6 collective-permute-start.3
  3.8 1.3 fusion.43
  5.4 3.4 %slice.72 = bf16[160,7168]{1,0:T(8,128)(2,1)} slice(bf16[256,7168]{1,0:T(8,128)(2,1)} %refs_4_.1), slice={[0:160], [0:7168]} | slice | bytes 4587520 | tf_op jit(solution)/shard_map/slice | solution.py:454
  8.8 1.6 collective-permute-start.2
  10.3 1.5 slice.73
  11.8 2.6 collective-permute-start.4
  14.7 1.2 fusion.16
  16.1 0.7 pad_maximum_fusion.1
  17.5 2.7 slice.82
  20.2 2.5 slice.83
  23.3 1.4 collective-permute-start.1
  24.8 0.7 pad_maximum_fusion.2
  25.5 64.3 %collective-permute-done.6 = f32[2,2,32,512]{3,2,1,0:T(8,128)S(1)} collective-permute-done((f32[2,2,32,512]{3,2,1,0:T(8,128)}, f32[2,2,32,512]{3,2,1,0:T(8,128)S(1)}, u32[]{:S(2)}, u32[]{:S(2)}) %collective-permute-start.6) | collective-permute-done | bytes 262176 | tf_op jit(solution)/shard_map/ppermute | solution.py:427
  89.8 0.8 fusion.29
  90.5 18.2 %collective-permute-done.2.refs_0_.refs_6_ = bf16[160,7168]{1,0:T(8,128)(2,1)} collective-permute-done((bf16[160,7168]{1,0:T(8,128)(2,1)}, bf16[160,7168]{1,0:T(8,128)(2,1)}, u32[]{:S(2)}, u32[]{:S(2)}) %collective-permute-start.2) | collective-permute-done | bytes 2293792 | tf_op jit(solution)/shard_map/ppermute | solution.py:427
  108.8 5.4 %collective-permute-done.4.refs_2_.refs_4_ = bf16[160,7168]{1,0:T(8,128)(2,1)} collective-permute-done((bf16[160,7168]{1,0:T(8,128)(2,1)}, bf16[160,7168]{1,0:T(8,128)(2,1)}, u32[]{:S(2)}, u32[]{:S(2)}) %collective-permute-start.4) | collective-permute-done | bytes 2293792 | tf_op jit(solution)/shard_map/ppermute | solution.py:427
  114.7 0.9 collective-permute-start.8
  115.7 0.8 shard_map.104
  116.5 0.8 copy-done.8
  117.2 2.0 collective-permute-start.10
  119.3 3.0 collective-permute-start.9
  122.3 1.3 shard_map.105.source
  123.6 2.0 copy-done.2
  125.6 2.0 copy-done.5
  127.7 7.0 %shard_map.106.refs_6_ = f32[512,512]{1,0:T(8,128)S(1)} custom-call(bf16[256,7168]{1,0:T(8,128)(2,1)S(1)} %copy-done.2, bf16[256,7168]{1,0:T(8,128)(2,1)} %collective-permute-done.3.refs_1_.refs_5_, bf16[256,7168]{1,0:T(8,128)(2,1)S(1)} %copy-done.5, bf16[256,7168]{1,0:T(8,128)(2,1)} %collective-permute-done.refs_3_), custom_call_target="tpu_custom_call" | custom-call | flops 1024 | bytes 1024 | tf_op jit(solution)/shard_map/pallas_call | solution.py:116
  134.6 17.2 %collective-permute-done.11 = f32[1,2,32,512]{3,2,1,0:T(8,128)} collective-permute-done((f32[1,2,32,512]{3,2,1,0:T(8,128)}, f32[1,2,32,512]{3,2,1,0:T(8,128)}, u32[]{:S(2)}, u32[]{:S(2)}) %collective-permute-start.11) | collective-permute-done | bytes 131104 | tf_op jit(solution)/shard_map/ppermute | solution.py:427
  151.9 0.9 bitcast_add_fusion
  152.8 8.9 %collective-permute-done.10.refs_2_.refs_3_ = bf16[2,64,1792]{2,1,0:T(8,128)(2,1)} collective-permute-done((bf16[2,64,1792]{2,1,0:T(8,128)(2,1)}, bf16[2,64,1792]{2,1,0:T(8,128)(2,1)}, u32[]{:S(2)}, u32[]{:S(2)}) %collective-permute-start.10) | collective-permute-done | bytes 458784 | tf_op jit(solution)/shard_map/ppermute | solution.py:427
  162.3 1.0 collective-permute-start.12
  163.3 2.0 shard_map.107.refs_0_
  165.4 27.6 %collective-permute-done.13 = f32[32,512]{1,0:T(8,128)S(1)} collective-permute-done((f32[32,512]{1,0:T(8,128)S(1)}, f32[32,512]{1,0:T(8,128)S(1)}, u32[]{:S(2)}, u32[]{:S(2)}) %collective-permute-start.13) | collective-permute-done | bytes 65568 | tf_op jit(solution)/shard_map/ppermute | solution.py:427
  193.7 1.3 shard_map.108.source
  196.1 1.3 shard_map.109.source
  197.4 1.0 pad_maximum_fusion
  198.4 2.4 collective-permute-start.21
  200.8 0.9 collective-permute-done.16.refs_5_.refs_7_
  201.8 2.0 copy-done.3
  203.8 7.7 %shard_map.110 = (f32[512,512]{1,0:T(8,128)S(1)}, bf16[512,512]{1,0:T(8,128)(2,1)S(1)}) custom-call(s32[1]{0:T(128)} %bitcast.32.flag, bf16[256,7168]{1,0:T(8,128)(2,1)S(1)} %copy-done.3, bf16[256,7168]{1,0:T(8,128)(2,1)} %collective-permute-done.3.refs_1_.refs_5_, bf16[160,7168]{1,0:T(8,128)(2,1)} %collective-permute-done.4.refs_2_.refs_4_, ...), custom_call_target="tpu_custom_call" | custom-call | flops 1024 | bytes 1024 | tf_op jit(solution)/shard_map/pallas_call | solution.py:168
  211.5 1.6 collective-permute-start.19
  213.1 9.2 %shard_map.111 = (f32[256,512]{1,0:T(8,128)S(1)}, bf16[256,512]{1,0:T(8,128)(2,1)S(1)}) custom-call(s32[1]{0:T(128)} %bitcast.32.flag, bf16[160,7168]{1,0:T(8,128)(2,1)} %collective-permute-done.2.refs_0_.refs_6_, bf16[96,7168]{1,0:T(8,128)(2,1)} %collective-permute-done.7.refs_1_.refs_7_, bf16[256,7168]{1,0:T(8,128)(2,1)} %refs_2_.5, ...), custom_call_target="tpu_custom_call" | custom-call | flops 1024 | bytes 1024 | tf_op jit(solution)/shard_map/pallas_call | solution.py:168
  222.9 5.1 %collective-permute-done.14.refs_9_.refs_1_ = bf16[96,7168]{1,0:T(8,128)(2,1)} collective-permute-done((bf16[96,7168]{1,0:T(8,128)(2,1)}, bf16[96,7168]{1,0:T(8,128)(2,1)}, u32[]{:S(2)}, u32[]{:S(2)}) %collective-permute-start.14) | collective-permute-done | bytes 1376288 | tf_op jit(solution)/shard_map/ppermute | solution.py:427
  228.0 4.3 %shard_map.112 = (f32[256,1792]{1,0:T(8,128)S(1)}, f32[256,1792]{1,0:T(8,128)S(1)}) custom-call(s32[1]{0:T(128)} %bitcast.1.group.place, bf16[512,256]{1,0:T(8,128)(2,1)S(1)} %bitcast.135, bf16[512,256]{1,0:T(8,128)(2,1)S(1)} %copy-done.11, bf16[1024,256]{1,0:T(8,128)(2,1)S(1)} %collective-permute-done.21.refs_2_.refs_3_, ...), custom_call_target="tpu_custom_call" | custom-call | flops 1024 | bytes 1024 | tf_op jit(solution)/shard_map/pallas_call | solution.py:239
  232.4 7.1 %collective-permute-done.18 = f32[32,512]{1,0:T(8,128)S(1)} collective-permute-done((f32[32,512]{1,0:T(8,128)S(1)}, f32[32,512]{1,0:T(8,128)S(1)}, u32[]{:S(2)}, u32[]{:S(2)}) %collective-permute-start.18) | collective-permute-done | bytes 65568 | tf_op jit(solution)/shard_map/ppermute | solution.py:427
  239.6 1.3 collective-permute-start.24
  241.4 4.2 %collective-permute-done.24 = f32[2,32,512]{2,1,0:T(8,128)S(1)} collective-permute-done((f32[2,32,512]{2,1,0:T(8,128)S(1)}, f32[2,32,512]{2,1,0:T(8,128)S(1)}, u32[]{:S(2)}, u32[]{:S(2)}) %collective-permute-start.24) | collective-permute-done | bytes 131104 | tf_op jit(solution)/shard_map/ppermute | solution.py:427
  246.4 1.2 slice_convert_fusion
  247.6 1.3 shard_map.113
  250.2 1.3 collective-permute-start.25
  251.5 2.8 collective-permute-start.23
  254.4 0.7 fusion.19.inter
  255.1 9.0 %shard_map.116 = (f32[128,1792]{1,0:T(8,128)S(1)}, f32[128,1792]{1,0:T(8,128)S(1)}) custom-call(f32[128,512]{1,0:T(8,128)S(1)} %fusion.19.inter, bf16[2,128,1792]{2,1,0:T(8,128)(2,1)} %shard_map.107.refs_0_, bf16[2,128,1792]{2,1,0:T(8,128)(2,1)} %collective-permute-done.27.refs_1_, bf16[2,128,1792]{2,1,0:T(8,128)(2,1)} %collective-permute-done.17.refs_2_, ...), custom_call_target="tpu_custom_call" | custom-call | flops 1024 | bytes 1024 | tf_op jit(solution)/shard_map/pallas_call | solution.py:315
  264.1 9.9 %shard_map.117 = (f32[256,512]{1,0:T(8,128)S(1)}, bf16[256,512]{1,0:T(8,128)(2,1)}) custom-call(s32[1]{0:T(128)} %bitcast.32.flag, bf16[160,7168]{1,0:T(8,128)(2,1)} %collective-permute-done.8.refs_8_.refs_0_, bf16[96,7168]{1,0:T(8,128)(2,1)} %collective-permute-done.14.refs_9_.refs_1_, bf16[256,7168]{1,0:T(8,128)(2,1)} %refs_2_.5, ...), custom_call_target="tpu_custom_call" | custom-call | flops 1024 | bytes 1024 | tf_op jit(solution)/shard_map/pallas_call | solution.py:168
  274.1 1.5 collective-permute-start.29
  275.7 1.3 shard_map.120
  277.0 0.9 collective-permute-start.31
  277.9 2.7 collective-permute-start.33
  280.6 0.9 collective-permute-done.29.refs_0_
  281.5 2.1 shard_map.118
  283.8 1.2 slice.94
  285.0 4.9 %collective-permute-done.31.refs_1_ = f32[2,32,1792]{2,1,0:T(8,128)S(1)} collective-permute-done((f32[2,32,1792]{2,1,0:T(8,128)}, f32[2,32,1792]{2,1,0:T(8,128)S(1)}, u32[]{:S(2)}, u32[]{:S(2)}) %collective-permute-start.31) | collective-permute-done | bytes 458784 | tf_op jit(solution)/shard_map/ppermute | solution.py:427
  289.9 1.7 collective-permute-done.32.refs_2_
  291.6 10.5 %collective-permute-done.33.refs_3_ = f32[2,32,1792]{2,1,0:T(8,128)S(1)} collective-permute-done((f32[2,32,1792]{2,1,0:T(8,128)}, f32[2,32,1792]{2,1,0:T(8,128)S(1)}, u32[]{:S(2)}, u32[]{:S(2)}) %collective-permute-start.33) | collective-permute-done | bytes 458784 | tf_op jit(solution)/shard_map/ppermute | solution.py:427
  302.1 2.4 shard_map.121
  304.9 2.1 shard_map.119
  (123 shorter events, 9.8 us)
Async XLA Ops:
  0.6 3.1 %copy-start = (bf16[256,512]{1,0:T(8,128)(2,1)S(1)}, bf16[256,512]{1,0:T(8,128)(2,1)}, u32[]{:S(2)}) copy-start(bf16[256,512]{1,0:T(8,128)(2,1)} %param.13) | copy-start | bytes 786436
  0.6 22.0 %collective-permute-start = (bf16[256,7168]{1,0:T(8,128)(2,1)}, bf16[256,7168]{1,0:T(8,128)(2,1)}, u32[]{:S(2)}, u32[]{:S(2)}) collective-permute-start(bf16[256,7168]{1,0:T(8,128)(2,1)} %refs_2_.5), channel_id=1, source_target_pairs={{0,2},{2,0},{4,6},{6,4},{8,10},{10,8},{12,14},{14,12},{16,18},{18,... | collective-permute-start | bytes 11010056 | tf_op jit(solution)/shard_map/ppermute | solution.py:427
  1.2 113.0 %collective-permute-start.3 = (bf16[256,7168]{1,0:T(8,128)(2,1)}, bf16[256,7168]{1,0:T(8,128)(2,1)}, u32[]{:S(2)}, u32[]{:S(2)}) collective-permute-start(bf16[256,7168]{1,0:T(8,128)(2,1)} %refs_4_.1), channel_id=1, source_target_pairs={{0,4},{2,6},{4,0},{6,2},{8,12},{10,14},{12,8},{14,10},{16,20},{18,... | collective-permute-start | bytes 11010056 | tf_op jit(solution)/shard_map/ppermute | solution.py:427
  5.1 5.2 %copy-start.4 = (bf16[256,7168]{1,0:T(8,128)(2,1)S(1)}, bf16[256,7168]{1,0:T(8,128)(2,1)}, u32[]{:S(2)}) copy-start(bf16[256,7168]{1,0:T(8,128)(2,1)} %refs_2_.5) | copy-start | bytes 11010052
  5.1 10.7 %collective-permute-start.5 = (f32[2,4,32,512]{3,2,1,0:T(8,128)S(1)}, f32[2,4,32,512]{3,2,1,0:T(8,128)S(1)}, u32[]{:S(2)}, u32[]{:S(2)}) collective-permute-start(f32[2,4,32,512]{3,2,1,0:T(8,128)S(1)} %select_bitcast_fusion), channel_id=1, source_target_pairs={{0,2},{2,0},{4,6},{6,4},{8,10},{10,8},{12,14},{14,12},{16,18},{18,... | collective-permute-start | bytes 1572872 | tf_op jit(solution)/shard_map/ppermute | solution.py:427
  8.8 5.7 %copy-start.28 = (bf16[256,512]{1,0:T(8,128)(2,1)S(1)}, bf16[256,512]{1,0:T(8,128)(2,1)}, u32[]{:S(2)}) copy-start(bf16[256,512]{1,0:T(8,128)(2,1)} %param.9) | copy-start | bytes 786436
  8.8 100.0 %collective-permute-start.2 = (bf16[160,7168]{1,0:T(8,128)(2,1)}, bf16[160,7168]{1,0:T(8,128)(2,1)}, u32[]{:S(2)}, u32[]{:S(2)}) collective-permute-start(bf16[160,7168]{1,0:T(8,128)(2,1)} %slice.72), channel_id=1, source_target_pairs={{0,8},{2,10},{4,12},{6,14},{8,0},{10,2},{12,4},{14,6},{16,24},{18,... | collective-permute-start | bytes 6881288 | tf_op jit(solution)/shard_map/ppermute | solution.py:427
  11.8 102.3 %collective-permute-start.4 = (bf16[160,7168]{1,0:T(8,128)(2,1)}, bf16[160,7168]{1,0:T(8,128)(2,1)}, u32[]{:S(2)}, u32[]{:S(2)}) collective-permute-start(bf16[160,7168]{1,0:T(8,128)(2,1)} %slice.73), channel_id=1, source_target_pairs={{0,16},{2,18},{4,20},{6,22},{8,24},{10,26},{12,28},{14,30},{16,0},... | collective-permute-start | bytes 6881288 | tf_op jit(solution)/shard_map/ppermute | solution.py:427
  16.8 73.0 %collective-permute-start.6 = (f32[2,2,32,512]{3,2,1,0:T(8,128)}, f32[2,2,32,512]{3,2,1,0:T(8,128)S(1)}, u32[]{:S(2)}, u32[]{:S(2)}) collective-permute-start(f32[2,2,32,512]{3,2,1,0:T(8,128)} %pad_maximum_fusion.1), channel_id=1, source_target_pairs={{0,4},{2,6},{4,0},{6,2},{8,12},{10,14},{12,8},{14,10},{16,20},{18,... | collective-permute-start | bytes 786440 | tf_op jit(solution)/shard_map/ppermute | solution.py:427
  17.5 5.2 %copy-start.12 = (f32[32,7168]{1,0:T(8,128)S(1)}, f32[32,7168]{1,0:T(8,128)}, u32[]{:S(2)}) copy-start(f32[32,7168]{1,0:T(8,128)} %first) | copy-start | bytes 2752516
  17.5 5.2 %copy-start.13 = (f32[32,7168]{1,0:T(8,128)S(1)}, f32[32,7168]{1,0:T(8,128)}, u32[]{:S(2)}) copy-start(f32[32,7168]{1,0:T(8,128)} %second) | copy-start | bytes 2752516
  23.3 92.4 %collective-permute-start.1 = (bf16[2,64,1792]{2,1,0:T(8,128)(2,1)S(1)}, bf16[2,64,1792]{2,1,0:T(8,128)(2,1)S(1)}, u32[]{:S(2)}, u32[]{:S(2)}) collective-permute-start(bf16[2,64,1792]{2,1,0:T(8,128)(2,1)S(1)} %shard_map.103), channel_id=1, source_target_pairs={{0,4},{2,6},{4,0},{6,2},{8,12},{10,14},{12,8},{14,10},{16,20},{18,... | collective-permute-start | bytes 1376264 | tf_op jit(solution)/shard_map/ppermute | solution.py:427
  114.7 80.2 %collective-permute-start.8 = (bf16[160,7168]{1,0:T(8,128)(2,1)}, bf16[160,7168]{1,0:T(8,128)(2,1)}, u32[]{:S(2)}, u32[]{:S(2)}) collective-permute-start(bf16[160,7168]{1,0:T(8,128)(2,1)} %collective-permute-done.2.refs_0_.refs_6_), channel_id=1, source_target_pairs={{0,4},{2,6},{4,0},{6,2},{8,12},{10,14},{12,8},{14,10},{16,20},{18,... | collective-permute-start | bytes 6881288 | tf_op jit(solution)/shard_map/ppermute | solution.py:427
  115.7 36.2 %collective-permute-start.11 = (f32[1,2,32,512]{3,2,1,0:T(8,128)}, f32[1,2,32,512]{3,2,1,0:T(8,128)}, u32[]{:S(2)}, u32[]{:S(2)}) collective-permute-start(f32[1,2,32,512]{3,2,1,0:T(8,128)} %bitcast.28), channel_id=1, source_target_pairs={{0,8},{2,10},{4,12},{6,14},{8,0},{10,2},{12,4},{14,6},{16,24},{18,... | collective-permute-start | bytes 393224 | tf_op jit(solution)/shard_map/ppermute | solution.py:427
  117.2 44.4 %collective-permute-start.10 = (bf16[2,64,1792]{2,1,0:T(8,128)(2,1)}, bf16[2,64,1792]{2,1,0:T(8,128)(2,1)}, u32[]{:S(2)}, u32[]{:S(2)}) collective-permute-start(bf16[2,64,1792]{2,1,0:T(8,128)(2,1)} %shard_map.104), channel_id=1, source_target_pairs={{0,8},{2,10},{4,12},{6,14},{8,0},{10,2},{12,4},{14,6},{16,24},{18,... | collective-permute-start | bytes 1376264 | tf_op jit(solution)/shard_map/ppermute | solution.py:427
  119.3 75.7 %collective-permute-start.7 = (bf16[96,7168]{1,0:T(8,128)(2,1)}, bf16[96,7168]{1,0:T(8,128)(2,1)}, u32[]{:S(2)}, u32[]{:S(2)}) collective-permute-start(bf16[96,7168]{1,0:T(8,128)(2,1)} %slice.82), channel_id=1, source_target_pairs={{0,8},{2,10},{4,12},{6,14},{8,0},{10,2},{12,4},{14,6},{16,24},{18,... | collective-permute-start | bytes 4128776 | tf_op jit(solution)/shard_map/ppermute | solution.py:427
  119.3 75.6 %collective-permute-start.9 = (bf16[96,7168]{1,0:T(8,128)(2,1)}, bf16[96,7168]{1,0:T(8,128)(2,1)}, u32[]{:S(2)}, u32[]{:S(2)}) collective-permute-start(bf16[96,7168]{1,0:T(8,128)(2,1)} %slice.83), channel_id=1, source_target_pairs={{0,16},{2,18},{4,20},{6,22},{8,24},{10,26},{12,28},{14,30},{16,0},... | collective-permute-start | bytes 4128776 | tf_op jit(solution)/shard_map/ppermute | solution.py:427
  123.6 2.0 copy-start.2
  125.6 2.0 copy-start.5
  127.6 24.2 %copy-start.26 = (f32[2,32,512]{2,1,0:T(8,128)S(1)}, f32[2,32,512]{2,1,0:T(8,128)}, u32[]{:S(2)}) copy-start(f32[2,32,512]{2,1,0:T(8,128)} %get-tuple-element.144) | copy-start | bytes 393220
  127.6 34.7 %copy-start.6 = (bf16[256,2,2,4,32]{0,4,3,2,1:T(8,128)(2,1)S(1)}, bf16[256,2,2,4,32]{0,4,3,2,1:T(8,128)(2,1)}, u32[]{:S(2)}) copy-start(bf16[256,2,2,4,32]{0,4,3,2,1:T(8,128)(2,1)} %pad_maximum_fusion.2) | copy-start | bytes 786436
  127.6 35.7 %copy-start.9 = (bf16[2,64,1792]{2,1,0:T(8,128)(2,1)S(1)}, bf16[2,64,1792]{2,1,0:T(8,128)(2,1)}, u32[]{:S(2)}) copy-start(bf16[2,64,1792]{2,1,0:T(8,128)(2,1)} %copy-done.8) | copy-start | bytes 1376260
  161.7 31.3 %collective-permute-start.13 = (f32[32,512]{1,0:T(8,128)S(1)}, f32[32,512]{1,0:T(8,128)S(1)}, u32[]{:S(2)}, u32[]{:S(2)}) collective-permute-start(f32[32,512]{1,0:T(8,128)S(1)} %select_bitcast_fusion.1), channel_id=1, source_target_pairs={{0,16},{2,18},{4,20},{6,22},{8,24},{10,26},{12,28},{14,30},{16,0},... | collective-permute-start | bytes 196616 | tf_op jit(solution)/shard_map/ppermute | solution.py:427
  162.3 31.3 %collective-permute-start.12 = (bf16[512,256]{1,0:T(8,128)(2,1)S(1)}, bf16[512,256]{1,0:T(8,128)(2,1)S(1)}, u32[]{:S(2)}, u32[]{:S(2)}) collective-permute-start(bf16[512,256]{1,0:T(8,128)(2,1)S(1)} %bitcast.133), channel_id=1, source_target_pairs={{0,4},{2,6},{4,0},{6,2},{8,12},{10,14},{12,8},{14,10},{16,20},{18,... | collective-permute-start | bytes 786440 | tf_op jit(solution)/shard_map/ppermute | solution.py:427
  193.7 3.7 %copy-start.10 = (bf16[512,256]{1,0:T(8,128)(2,1)}, bf16[512,256]{1,0:T(8,128)(2,1)S(1)}, u32[]{:S(2)}) copy-start(bf16[512,256]{1,0:T(8,128)(2,1)S(1)} %collective-permute-done.12.refs_1_) | copy-start | bytes 786436
  194.9 6.8 %collective-permute-start.15 = (bf16[160,7168]{1,0:T(8,128)(2,1)}, bf16[160,7168]{1,0:T(8,128)(2,1)}, u32[]{:S(2)}, u32[]{:S(2)}) collective-permute-start(bf16[160,7168]{1,0:T(8,128)(2,1)} %collective-permute-done.4.refs_2_.refs_4_), channel_id=1, source_target_pairs={{0,2},{2,0},{4,6},{6,4},{8,10},{10,8},{12,14},{14,12},{16,18},{18,... | collective-permute-start | bytes 6881288 | tf_op jit(solution)/shard_map/ppermute | solution.py:427
  195.0 6.7 %collective-permute-start.16 = (bf16[96,7168]{1,0:T(8,128)(2,1)}, bf16[96,7168]{1,0:T(8,128)(2,1)}, u32[]{:S(2)}, u32[]{:S(2)}) collective-permute-start(bf16[96,7168]{1,0:T(8,128)(2,1)} %collective-permute-done.9.refs_3_.refs_5_), channel_id=1, source_target_pairs={{0,2},{2,0},{4,6},{6,4},{8,10},{10,8},{12,14},{14,12},{16,18},{18,... | collective-permute-start | bytes 4128776 | tf_op jit(solution)/shard_map/ppermute | solution.py:427
  195.5 32.5 %collective-permute-start.14 = (bf16[96,7168]{1,0:T(8,128)(2,1)}, bf16[96,7168]{1,0:T(8,128)(2,1)}, u32[]{:S(2)}, u32[]{:S(2)}) collective-permute-start(bf16[96,7168]{1,0:T(8,128)(2,1)} %collective-permute-done.7.refs_1_.refs_7_), channel_id=1, source_target_pairs={{0,4},{2,6},{4,0},{6,2},{8,12},{10,14},{12,8},{14,10},{16,20},{18,... | collective-permute-start | bytes 4128776 | tf_op jit(solution)/shard_map/ppermute | solution.py:427
  196.1 43.4 %collective-permute-start.17 = (bf16[2,128,1792]{2,1,0:T(8,128)(2,1)}, bf16[2,128,1792]{2,1,0:T(8,128)(2,1)}, u32[]{:S(2)}, u32[]{:S(2)}) collective-permute-start(bf16[2,128,1792]{2,1,0:T(8,128)(2,1)} %shard_map.107.refs_0_), channel_id=1, source_target_pairs={{0,16},{2,18},{4,20},{6,22},{8,24},{10,26},{12,28},{14,30},{16,0},... | collective-permute-start | bytes 2752520 | tf_op jit(solution)/shard_map/ppermute | solution.py:427
  198.4 29.6 %collective-permute-start.21 = (bf16[1024,256]{1,0:T(8,128)(2,1)S(1)}, bf16[1024,256]{1,0:T(8,128)(2,1)S(1)}, u32[]{:S(2)}, u32[]{:S(2)}) collective-permute-start(bf16[1024,256]{1,0:T(8,128)(2,1)S(1)} %pad_maximum_fusion), channel_id=1, source_target_pairs={{0,8},{2,10},{4,12},{6,14},{8,0},{10,2},{12,4},{14,6},{16,24},{18,... | collective-permute-start | bytes 1572872 | tf_op jit(solution)/shard_map/ppermute | solution.py:427
  201.8 2.0 copy-start.3
  211.5 28.0 %collective-permute-start.19 = (bf16[512,512]{1,0:T(8,128)(2,1)S(1)}, bf16[512,512]{1,0:T(8,128)(2,1)S(1)}, u32[]{:S(2)}, u32[]{:S(2)}) collective-permute-start(bf16[512,512]{1,0:T(8,128)(2,1)S(1)} %get-tuple-element.173), channel_id=1, source_target_pairs={{0,1},{1,0},{2,3},{3,2},{4,5},{5,4},{6,7},{7,6},{8,9},{9,8},{10,11... | collective-permute-start | bytes 1572872 | tf_op jit(solution)/shard_map/ppermute | solution.py:430
  213.1 14.9 %copy-start.24 = (f32[32,512]{1,0:T(8,128)S(1)}, f32[32,512]{1,0:T(8,128)}, u32[]{:S(2)}) copy-start(f32[32,512]{1,0:T(8,128)} %bitcast_add_fusion.1) | copy-start | bytes 196612
  213.1 14.9 %copy-start.11 = (bf16[512,256]{1,0:T(8,128)(2,1)S(1)}, bf16[512,256]{1,0:T(8,128)(2,1)}, u32[]{:S(2)}) copy-start(bf16[512,256]{1,0:T(8,128)(2,1)} %copy-done.10) | copy-start | bytes 786436
  222.3 17.2 %collective-permute-start.20 = (bf16[256,512]{1,0:T(8,128)(2,1)S(1)}, bf16[256,512]{1,0:T(8,128)(2,1)S(1)}, u32[]{:S(2)}, u32[]{:S(2)}) collective-permute-start(bf16[256,512]{1,0:T(8,128)(2,1)S(1)} %get-tuple-element.177), channel_id=1, source_target_pairs={{0,1},{1,0},{2,3},{3,2},{4,5},{5,4},{6,7},{7,6},{8,9},{9,8},{10,11... | collective-permute-start | bytes 786440 | tf_op jit(solution)/shard_map/ppermute | solution.py:430
  228.0 11.5 %collective-permute-start.18 = (f32[32,512]{1,0:T(8,128)S(1)}, f32[32,512]{1,0:T(8,128)S(1)}, u32[]{:S(2)}, u32[]{:S(2)}) collective-permute-start(f32[32,512]{1,0:T(8,128)S(1)} %copy-done.24), channel_id=1, source_target_pairs={{0,8},{2,10},{4,12},{6,14},{8,0},{10,2},{12,4},{14,6},{16,24},{18,... | collective-permute-start | bytes 196616 | tf_op jit(solution)/shard_map/ppermute | solution.py:427
  239.5 6.9 %copy-start.29 = (f32[32,512]{1,0:T(8,128)}, f32[32,512]{1,0:T(8,128)S(1)}, u32[]{:S(2)}) copy-start(f32[32,512]{1,0:T(8,128)S(1)} %collective-permute-done.18) | copy-start | bytes 196612
  239.5 6.9 %copy-start.20 = (bf16[256,512]{1,0:T(8,128)(2,1)}, bf16[256,512]{1,0:T(8,128)(2,1)S(1)}, u32[]{:S(2)}) copy-start(bf16[256,512]{1,0:T(8,128)(2,1)S(1)} %collective-permute-done.20.refs_0_) | copy-start | bytes 786436
  239.5 6.9 %copy-start.14 = (bf16[512,512]{1,0:T(8,128)(2,1)}, bf16[512,512]{1,0:T(8,128)(2,1)S(1)}, u32[]{:S(2)}) copy-start(bf16[512,512]{1,0:T(8,128)(2,1)S(1)} %collective-permute-done.19.refs_0_) | copy-start | bytes 1572868
  239.5 6.7 %collective-permute-start.22 = (f32[256,1792]{1,0:T(8,128)S(1)}, f32[256,1792]{1,0:T(8,128)S(1)}, u32[]{:S(2)}, u32[]{:S(2)}) collective-permute-start(f32[256,1792]{1,0:T(8,128)S(1)} %get-tuple-element.191), channel_id=1, source_target_pairs={{0,2},{2,0},{4,6},{6,4},{8,10},{10,8},{12,14},{14,12},{16,18},{18,... | collective-permute-start | bytes 5505032 | tf_op jit(solution)/shard_map/ppermute | solution.py:427
  239.6 6.0 %collective-permute-start.24 = (f32[2,32,512]{2,1,0:T(8,128)S(1)}, f32[2,32,512]{2,1,0:T(8,128)S(1)}, u32[]{:S(2)}, u32[]{:S(2)}) collective-permute-start(f32[2,32,512]{2,1,0:T(8,128)S(1)} %pad_maximum_fusion.4), channel_id=1, source_target_pairs={{0,4},{2,6},{4,0},{6,2},{8,12},{10,14},{12,8},{14,10},{16,20},{18,... | collective-permute-start | bytes 393224 | tf_op jit(solution)/shard_map/ppermute | solution.py:427
  240.9 14.2 %collective-permute-start.27 = (bf16[2,128,1792]{2,1,0:T(8,128)(2,1)}, bf16[2,128,1792]{2,1,0:T(8,128)(2,1)}, u32[]{:S(2)}, u32[]{:S(2)}) collective-permute-start(bf16[2,128,1792]{2,1,0:T(8,128)(2,1)} %shard_map.107.refs_0_), channel_id=1, source_target_pairs={{0,2},{2,0},{4,6},{6,4},{8,10},{10,8},{12,14},{14,12},{16,18},{18,... | collective-permute-start | bytes 2752520 | tf_op jit(solution)/shard_map/ppermute | solution.py:427
  241.1 14.0 %collective-permute-start.28 = (bf16[2,128,1792]{2,1,0:T(8,128)(2,1)}, bf16[2,128,1792]{2,1,0:T(8,128)(2,1)}, u32[]{:S(2)}, u32[]{:S(2)}) collective-permute-start(bf16[2,128,1792]{2,1,0:T(8,128)(2,1)} %collective-permute-done.17.refs_2_), channel_id=1, source_target_pairs={{0,2},{2,0},{4,6},{6,4},{8,10},{10,8},{12,14},{14,12},{16,18},{18,... | collective-permute-start | bytes 2752520 | tf_op jit(solution)/shard_map/ppermute | solution.py:427
  247.6 1.9 copy-start.15
  249.0 2.5 copy-start.27
  249.0 5.3 %copy-start.25 = (f32[32,512]{1,0:T(8,128)S(1)}, f32[32,512]{1,0:T(8,128)}, u32[]{:S(2)}) copy-start(f32[32,512]{1,0:T(8,128)} %bitcast_add_fusion.1) | copy-start | bytes 196612
  249.0 5.3 %copy-start.30 = (f32[32,512]{1,0:T(8,128)S(1)}, f32[32,512]{1,0:T(8,128)}, u32[]{:S(2)}) copy-start(f32[32,512]{1,0:T(8,128)} %copy-done.29) | copy-start | bytes 196612
  249.0 5.3 %copy-start.31 = (f32[32,512]{1,0:T(8,128)S(1)}, f32[32,512]{1,0:T(8,128)}, u32[]{:S(2)}) copy-start(f32[32,512]{1,0:T(8,128)} %get-tuple-element.206) | copy-start | bytes 196612
  249.0 5.3 %copy-start.32 = (f32[32,512]{1,0:T(8,128)S(1)}, f32[32,512]{1,0:T(8,128)}, u32[]{:S(2)}) copy-start(f32[32,512]{1,0:T(8,128)} %get-tuple-element.208) | copy-start | bytes 196612
  249.0 5.4 %copy-start.22 = (f32[512,512]{1,0:T(8,128)S(1)}, f32[512,512]{1,0:T(8,128)}, u32[]{:S(2)}) copy-start(f32[512,512]{1,0:T(8,128)} %fusion.16) | copy-start | bytes 3145732
  249.4 24.5 %collective-permute-start.26 = (bf16[256,512]{1,0:T(8,128)(2,1)S(1)}, bf16[256,512]{1,0:T(8,128)(2,1)S(1)}, u32[]{:S(2)}, u32[]{:S(2)}) collective-permute-start(bf16[256,512]{1,0:T(8,128)(2,1)S(1)} %shard_map.115), channel_id=1, source_target_pairs={{0,8},{2,10},{4,12},{6,14},{8,0},{10,2},{12,4},{14,6},{16,24},{18,... | collective-permute-start | bytes 786440 | tf_op jit(solution)/shard_map/ppermute | solution.py:427
  250.2 23.8 %collective-permute-start.25 = (bf16[256,512]{1,0:T(8,128)(2,1)S(1)}, bf16[256,512]{1,0:T(8,128)(2,1)S(1)}, u32[]{:S(2)}, u32[]{:S(2)}) collective-permute-start(bf16[256,512]{1,0:T(8,128)(2,1)S(1)} %get-tuple-element.203), channel_id=1, source_target_pairs={{0,4},{2,6},{4,0},{6,2},{8,12},{10,14},{12,8},{14,10},{16,20},{18,... | collective-permute-start | bytes 786440 | tf_op jit(solution)/shard_map/ppermute | solution.py:427
  251.5 22.6 %collective-permute-start.23 = (f16[128,1792]{1,0:T(8,128)(2,1)S(1)}, f16[128,1792]{1,0:T(8,128)(2,1)S(1)}, u32[]{:S(2)}, u32[]{:S(2)}) collective-permute-start(f16[128,1792]{1,0:T(8,128)(2,1)S(1)} %copy-done.27), channel_id=1, source_target_pairs={{0,16},{2,18},{4,20},{6,22},{8,24},{10,26},{12,28},{14,30},{16,0},... | collective-permute-start | bytes 1376264 | tf_op jit(solution)/shard_map/ppermute | solution.py:427
  264.1 11.6 %copy-start.23 = (f32[128,1792]{1,0:T(8,128)S(1)}, f32[128,1792]{1,0:T(8,128)}, u32[]{:S(2)}) copy-start(f32[128,1792]{1,0:T(8,128)} %get-tuple-element.227) | copy-start | bytes 2752516
  274.0 3.1 copy-start.16
  274.0 3.0 copy-start.18
  274.1 7.3 %collective-permute-start.29 = (bf16[256,512]{1,0:T(8,128)(2,1)}, bf16[256,512]{1,0:T(8,128)(2,1)}, u32[]{:S(2)}, u32[]{:S(2)}) collective-permute-start(bf16[256,512]{1,0:T(8,128)(2,1)} %get-tuple-element.222), channel_id=1, source_target_pairs={{0,1},{1,0},{2,3},{3,2},{4,5},{5,4},{6,7},{7,6},{8,9},{9,8},{10,11... | collective-permute-start | bytes 786440 | tf_op jit(solution)/shard_map/ppermute | solution.py:430
  277.0 27.9 %copy-start.17 = (bf16[256,512]{1,0:T(8,128)(2,1)S(1)}, bf16[256,512]{1,0:T(8,128)(2,1)}, u32[]{:S(2)}) copy-start(bf16[256,512]{1,0:T(8,128)(2,1)} %copy-done.16) | copy-start | bytes 786436
  277.0 27.9 %copy-start.19 = (bf16[256,512]{1,0:T(8,128)(2,1)S(1)}, bf16[256,512]{1,0:T(8,128)(2,1)}, u32[]{:S(2)}) copy-start(bf16[256,512]{1,0:T(8,128)(2,1)} %copy-done.18) | copy-start | bytes 786436
  277.0 12.8 %collective-permute-start.31 = (f32[2,32,1792]{2,1,0:T(8,128)}, f32[2,32,1792]{2,1,0:T(8,128)S(1)}, u32[]{:S(2)}, u32[]{:S(2)}) collective-permute-start(f32[2,32,1792]{2,1,0:T(8,128)} %get-tuple-element.230), channel_id=1, source_target_pairs={{0,4},{2,6},{4,0},{6,2},{8,12},{10,14},{12,8},{14,10},{16,20},{18,... | collective-permute-start | bytes 1376264 | tf_op jit(solution)/shard_map/ppermute | solution.py:427
  277.9 13.7 %collective-permute-start.32 = (f32[2,32,1792]{2,1,0:T(8,128)}, f32[2,32,1792]{2,1,0:T(8,128)S(1)}, u32[]{:S(2)}, u32[]{:S(2)}) collective-permute-start(f32[2,32,1792]{2,1,0:T(8,128)} %get-tuple-element.231), channel_id=1, source_target_pairs={{0,8},{2,10},{4,12},{6,14},{8,0},{10,2},{12,4},{14,6},{16,24},{18,... | collective-permute-start | bytes 1376264 | tf_op jit(solution)/shard_map/ppermute | solution.py:427
  277.9 24.2 %collective-permute-start.33 = (f32[2,32,1792]{2,1,0:T(8,128)}, f32[2,32,1792]{2,1,0:T(8,128)S(1)}, u32[]{:S(2)}, u32[]{:S(2)}) collective-permute-start(f32[2,32,1792]{2,1,0:T(8,128)} %get-tuple-element.232), channel_id=1, source_target_pairs={{0,12},{2,14},{4,8},{6,10},{8,4},{10,6},{12,0},{14,2},{16,28},{18,... | collective-permute-start | bytes 1376264 | tf_op jit(solution)/shard_map/ppermute | solution.py:427
  283.6 21.4 %collective-permute-start.30 = (bf16[256,512]{1,0:T(8,128)(2,1)}, bf16[256,512]{1,0:T(8,128)(2,1)S(1)}, u32[]{:S(2)}, u32[]{:S(2)}) collective-permute-start(bf16[256,512]{1,0:T(8,128)(2,1)} %shard_map.118), channel_id=1, source_target_pairs={{0,12},{2,14},{4,8},{6,10},{8,4},{10,6},{12,0},{14,2},{16,28},{18,... | collective-permute-start | bytes 786440 | tf_op jit(solution)/shard_map/ppermute | solution.py:427
  302.1 4.9 %copy-start.1 = (bf16[256,512]{1,0:T(8,128)(2,1)S(1)}, bf16[256,512]{1,0:T(8,128)(2,1)}, u32[]{:S(2)}) copy-start(bf16[256,512]{1,0:T(8,128)(2,1)} %param.13) | copy-start | bytes 786436
  (3 other events, 3.5 us)

commit v6 on v5

--- a/solution.py
+++ b/solution.py
@@ -300,12 +300,26 @@
     )(*[value for value, _ in blocks])
 
 
+def halves(value):
+    high = value.astype(jnp.bfloat16)
+    return high, (value - high.astype(jnp.float32)).astype(jnp.bfloat16)
+
+
+def fine_dot(left, right):
+    (a, b), (c, d) = halves(left), halves(right)
+
+    def dot(x, y):
+        return jnp.dot(x, y, preferred_element_type=jnp.float32)
+
+    return dot(a, c) + (dot(a, d) + dot(b, c))
+
+
 def rotate_kernel(n_codes, inter, *refs):
     codes, (first, second) = refs[:n_codes], refs[n_codes:]
     left = inter[...]
     for k, out, matrix in ((0, first, left), (1, second, left * left)):
         moment = jnp.concatenate([rooted(c[k]) for c in codes], axis=0)
-        out[...] = exact_dot(matrix, moment)
+        out[...] = fine_dot(matrix, moment)
 
 
 def rotate(inter, codes):
@@ -612,20 +626,23 @@
         ticket, next_parts, at_group = settle(forwarded(1), [], ticket, next_parts, at_group)
         keep, send_half = gradient_part(saved_list, [blocks_of(j) for j in order], at_group, part)
 
-        (ticket, far, inter, near_arrived, near_parts, next_arrived, next_parts, keep, send_half) = together(
-            ticket, far, inter, near_arrived, near_parts, next_arrived, next_parts, keep, send_half
+        last_own = []
+        if far_tokens[1:]:
+            ticket, keep, send_half, w_core = together(ticket, keep, send_half, w_core)
+            last_own = [multiply([value for j in far_tokens[1:] for value in blocks_of(j)], [weight, w_core])]
+        (ticket, far, inter, near_arrived, near_parts, next_arrived, next_parts, keep, send_half, last_own) = together(
+            ticket, far, inter, near_arrived, near_parts, next_arrived, next_parts, keep, send_half, last_own
         )
         got = swap(send_half, 1)
         far_other = {dz: swap(far[dz], 1) for dz in tops}
+        g = (keep + got).reshape(t, na * rows, part)
+        far_g = [g[dz].astype(jnp.float16) for dz in tops]
+        ticket, g, far_g, inter = together(ticket, g[0], far_g, inter)
         for bit in strides[1:]:
             found = swap(jnp.stack(inter), 2 * bit)
             inter += [found[k] for k in range(len(inter))]
         inter = [inter[hypercube(strides).index(k)] for k in range(na)]
-        g = (keep + got).reshape(t, na * rows, part)
-        far_g = [g[dz].astype(jnp.float16) for dz in tops]
-        ticket, g, far_g = together(ticket, g[0], far_g)
         late_g = [swap(value, dz * top_unit) for dz, value in zip(tops, far_g)]
-        ticket = anchor(ticket)
         ticket, near_parts, next_parts, inter = together(ticket, near_parts, next_parts, inter)
 
         def go_home(js, parts, arrived):
@@ -642,7 +659,7 @@
         last_parts = []
         if far_tokens[1:]:
             rot_first, rot_second, flag = together(rot_first, rot_second, flag)
-            last_parts = parts_of(far_tokens[1:], all_rows, flag)
+            last_parts = parts_of(far_tokens[1:], other_rows, flag, last_own)
 
         g, late_g, at_group, ticket, sums, last_parts = together(g, late_g, at_group, ticket, sums, last_parts)
         if far_tokens[1:]:

time: 308 us -> 304 us (0.987)
    pallas_call x1 -> x2, Pallas kernels: 6.97 us -> 12.2 us  [multiply(): pl.pallas_call(functools.partial(multiply_kernel, len(tokens)), grid=(wid...]
    pallas_call x3, Pallas kernels: 26.8 us -> 23.6 us  [multiply_parts(): pl.pallas_call(functools.partial(parts_kernel, len(tokens), [len(group) f...]
    unnamed x67 -> x43, local copies, waits for them, and re-layouts: 7.15 us -> 7.1 us
  transfers between devices with their start and end apart: 34 -> 34, of which waited for: 16 -> 17; matrix products, arithmetic and copies ran while one was open for 7% -> 7% of each run, Pallas kernels for 20% -> 20%
where the time goes in v6:
time: 304 us; the launch traced here: 303 us
  waiting for transfers between devices  177 us (58%)
  Pallas kernels  63.9 us (21%)
  starting transfers between devices  34.1 us (11%)
  local copies, waits for them, and re-layouts  18.9 us (6%)
  other arithmetic  6.13 us (2%)
    ppermute x31, waiting for transfers between devices, swap(): return lax.ppermute(value, 'seq', [(s, s ^ mask) for s in range(n)])  176 us
    ppermute x31, starting transfers between devices, swap(): return lax.ppermute(value, 'seq', [(s, s ^ mask) for s in range(n)])  30.4 us
    pallas_call x3, Pallas kernels, multiply_parts(): pl.pallas_call(functools.partial(parts_kernel, len(tokens), [len(group) f...  23.6 us
    pallas_call x2, Pallas kernels, multiply(): pl.pallas_call(functools.partial(multiply_kernel, len(tokens)), grid=(wid...  12.2 us
    slice x4, local copies, waits for them, and re-layouts, chunks_of(): return [value[:cut], value[cut:]]  9.99 us
    unnamed x43, local copies, waits for them, and re-layouts  7.1 us
    pallas_call x1, Pallas kernels, rotate(): pl.pallas_call(functools.partial(rotate_kernel, len(codes)), grid=(part /...  6.9 us
  transfers between devices with their start and end apart: 34, of which 17 were waited for; matrix products, arithmetic and copies ran while one was open for 7% of the time, Pallas kernels for 20%

profile of v6, /device:TPU:0, one launch (start us, length us, event | category | flops | bytes accessed | tf_op | source)
XLA Modules:
  0.0 303.0 jit_solution(9923497842980931034)
XLA Ops:
  1.2 2.6 collective-permute-start.3
  3.8 1.3 fusion.43
  5.4 3.3 %slice.72 = bf16[160,7168]{1,0:T(8,128)(2,1)} slice(bf16[256,7168]{1,0:T(8,128)(2,1)} %refs_4_.1), slice={[0:160], [0:7168]} | slice | bytes 4587520 | tf_op jit(solution)/shard_map/slice | solution.py:468
  8.7 1.6 collective-permute-start.2
  10.3 1.5 slice.73
  11.8 2.6 collective-permute-start.4
  14.6 1.2 fusion.16
  16.8 2.7 slice.82
  19.5 2.5 slice.83
  22.6 1.4 collective-permute-start.1
  24.1 0.7 pad_maximum_fusion.2
  24.8 65.0 %collective-permute-done.6 = f32[2,2,32,512]{3,2,1,0:T(8,128)S(1)} collective-permute-done((f32[2,2,32,512]{3,2,1,0:T(8,128)S(1)}, f32[2,2,32,512]{3,2,1,0:T(8,128)S(1)}, u32[]{:S(2)}, u32[]{:S(2)}) %collective-permute-start.6) | collective-permute-done | bytes 262176 | tf_op jit(solution)/shard_map/ppermute | solution.py:441
  89.8 0.8 fusion.29
  90.6 18.1 %collective-permute-done.2.refs_0_.refs_6_ = bf16[160,7168]{1,0:T(8,128)(2,1)} collective-permute-done((bf16[160,7168]{1,0:T(8,128)(2,1)}, bf16[160,7168]{1,0:T(8,128)(2,1)}, u32[]{:S(2)}, u32[]{:S(2)}) %collective-permute-start.2) | collective-permute-done | bytes 2293792 | tf_op jit(solution)/shard_map/ppermute | solution.py:441
  108.7 5.4 %collective-permute-done.4.refs_2_.refs_4_ = bf16[160,7168]{1,0:T(8,128)(2,1)} collective-permute-done((bf16[160,7168]{1,0:T(8,128)(2,1)}, bf16[160,7168]{1,0:T(8,128)(2,1)}, u32[]{:S(2)}, u32[]{:S(2)}) %collective-permute-start.4) | collective-permute-done | bytes 2293792 | tf_op jit(solution)/shard_map/ppermute | solution.py:441
  114.7 0.9 collective-permute-start.8
  115.6 0.8 shard_map.104
  116.4 0.8 copy-done.9
  117.2 2.0 collective-permute-start.10
  119.2 3.0 collective-permute-start.9
  122.2 1.3 shard_map.105.source
  123.5 2.0 copy-done.2
  125.6 2.0 copy-done.5
  127.6 7.0 %shard_map.106.refs_6_ = f32[512,512]{1,0:T(8,128)S(1)} custom-call(bf16[256,7168]{1,0:T(8,128)(2,1)S(1)} %copy-done.2, bf16[256,7168]{1,0:T(8,128)(2,1)} %collective-permute-done.3.refs_1_.refs_5_, bf16[256,7168]{1,0:T(8,128)(2,1)S(1)} %copy-done.5, bf16[256,7168]{1,0:T(8,128)(2,1)} %collective-permute-done.refs_3_), custom_call_target="tpu_custom_call" | custom-call | flops 1024 | bytes 1024 | tf_op jit(solution)/shard_map/pallas_call | solution.py:116
  134.6 17.2 %collective-permute-done.11 = f32[1,2,32,512]{3,2,1,0:T(8,128)} collective-permute-done((f32[1,2,32,512]{3,2,1,0:T(8,128)}, f32[1,2,32,512]{3,2,1,0:T(8,128)}, u32[]{:S(2)}, u32[]{:S(2)}) %collective-permute-start.11) | collective-permute-done | bytes 131104 | tf_op jit(solution)/shard_map/ppermute | solution.py:441
  151.8 0.9 bitcast_add_fusion
  152.7 8.9 %collective-permute-done.10.refs_2_.refs_3_ = bf16[2,64,1792]{2,1,0:T(8,128)(2,1)} collective-permute-done((bf16[2,64,1792]{2,1,0:T(8,128)(2,1)}, bf16[2,64,1792]{2,1,0:T(8,128)(2,1)}, u32[]{:S(2)}, u32[]{:S(2)}) %collective-permute-start.10) | collective-permute-done | bytes 458784 | tf_op jit(solution)/shard_map/ppermute | solution.py:441
  162.3 1.0 collective-permute-start.12
  163.3 2.0 shard_map.107.refs_0_
  165.3 27.6 %collective-permute-done.13 = f32[32,512]{1,0:T(8,128)S(1)} collective-permute-done((f32[32,512]{1,0:T(8,128)S(1)}, f32[32,512]{1,0:T(8,128)S(1)}, u32[]{:S(2)}, u32[]{:S(2)}) %collective-permute-start.13) | collective-permute-done | bytes 65568 | tf_op jit(solution)/shard_map/ppermute | solution.py:441
  193.6 1.3 shard_map.108.source
  196.0 1.3 shard_map.109
  197.3 1.0 pad_maximum_fusion
  198.3 2.4 collective-permute-start.17
  200.8 0.9 collective-permute-done.16.refs_5_.refs_7_
  201.7 2.0 copy-done.3
  203.8 7.7 %shard_map.110 = (f32[512,512]{1,0:T(8,128)S(1)}, bf16[512,512]{1,0:T(8,128)(2,1)S(1)}) custom-call(s32[1]{0:T(128)} %bitcast.32.flag, bf16[256,7168]{1,0:T(8,128)(2,1)S(1)} %copy-done.3, bf16[256,7168]{1,0:T(8,128)(2,1)} %collective-permute-done.3.refs_1_.refs_5_, bf16[160,7168]{1,0:T(8,128)(2,1)} %collective-permute-done.4.refs_2_.refs_4_, ...), custom_call_target="tpu_custom_call" | custom-call | flops 1024 | bytes 1024 | tf_op jit(solution)/shard_map/pallas_call | solution.py:168
  211.5 1.6 collective-permute-start.20
  213.0 9.1 %shard_map.111 = (f32[256,512]{1,0:T(8,128)S(1)}, bf16[256,512]{1,0:T(8,128)(2,1)S(1)}) custom-call(s32[1]{0:T(128)} %bitcast.32.flag, bf16[160,7168]{1,0:T(8,128)(2,1)} %collective-permute-done.2.refs_0_.refs_6_, bf16[96,7168]{1,0:T(8,128)(2,1)} %collective-permute-done.7.refs_1_.refs_7_, bf16[256,7168]{1,0:T(8,128)(2,1)} %refs_2_.5, ...), custom_call_target="tpu_custom_call" | custom-call | flops 1024 | bytes 1024 | tf_op jit(solution)/shard_map/pallas_call | solution.py:168
  222.8 5.2 %collective-permute-done.14.refs_9_.refs_1_ = bf16[96,7168]{1,0:T(8,128)(2,1)} collective-permute-done((bf16[96,7168]{1,0:T(8,128)(2,1)}, bf16[96,7168]{1,0:T(8,128)(2,1)}, u32[]{:S(2)}, u32[]{:S(2)}) %collective-permute-start.14) | collective-permute-done | bytes 1376288 | tf_op jit(solution)/shard_map/ppermute | solution.py:441
  228.0 4.8 %shard_map.112 = (f32[256,1792]{1,0:T(8,128)S(1)}, f32[256,1792]{1,0:T(8,128)S(1)}) custom-call(s32[1]{0:T(128)} %bitcast.1.group.place, bf16[512,256]{1,0:T(8,128)(2,1)S(1)} %bitcast.135, bf16[512,256]{1,0:T(8,128)(2,1)} %collective-permute-done.12.refs_1_, bf16[1024,256]{1,0:T(8,128)(2,1)S(1)} %collective-permute-done.17.refs_2_.refs_3_, ...), custom_call_target="tpu_custom_call" | custom-call | flops 1024 | bytes 1024 | tf_op jit(solution)/shard_map/pallas_call | solution.py:239
  232.8 5.2 %shard_map.113.refs_6_ = f32[256,512]{1,0:T(8,128)S(1)} custom-call(bf16[160,7168]{1,0:T(8,128)(2,1)} %collective-permute-done.8.refs_8_.refs_0_, bf16[96,7168]{1,0:T(8,128)(2,1)} %collective-permute-done.14.refs_9_.refs_1_, bf16[256,7168]{1,0:T(8,128)(2,1)S(1)} %copy-done.6, bf16[256,7168]{1,0:T(8,128)(2,1)} %collective-permute-done.refs_3_), custom_call_target="tpu_custom_call" | custom-call | flops 1024 | bytes 1024 | tf_op jit(solution)/shard_map/pallas_call | solution.py:116
  238.0 1.4 collective-permute-done.19
  240.1 5.0 %collective-permute-done.22 = f32[256,1792]{1,0:T(8,128)S(1)} collective-permute-done((f32[256,1792]{1,0:T(8,128)S(1)}, f32[256,1792]{1,0:T(8,128)S(1)}, u32[]{:S(2)}, u32[]{:S(2)}) %collective-permute-start.22) | collective-permute-done | bytes 1835040 | tf_op jit(solution)/shard_map/ppermute | solution.py:441
  245.5 1.3 collective-permute-start.24
  246.8 1.2 collective-permute-start.23
  248.0 3.1 %collective-permute-done.24 = f32[2,32,512]{2,1,0:T(8,128)S(1)} collective-permute-done((f32[2,32,512]{2,1,0:T(8,128)S(1)}, f32[2,32,512]{2,1,0:T(8,128)S(1)}, u32[]{:S(2)}, u32[]{:S(2)}) %collective-permute-start.24) | collective-permute-done | bytes 131104 | tf_op jit(solution)/shard_map/ppermute | solution.py:441
  251.6 0.9 collective-permute-start.26
  253.2 1.8 collective-permute-start.25
  255.0 0.7 fusion.19.inter
  255.8 6.9 %shard_map.116 = (f32[128,1792]{1,0:T(8,128)S(1)}, f32[128,1792]{1,0:T(8,128)S(1)}) custom-call(f32[128,512]{1,0:T(8,128)S(1)} %fusion.19.inter, bf16[2,128,1792]{2,1,0:T(8,128)(2,1)} %shard_map.107.refs_0_, bf16[2,128,1792]{2,1,0:T(8,128)(2,1)S(1)} %collective-permute-done.27.refs_1_, bf16[2,128,1792]{2,1,0:T(8,128)(2,1)} %collective-permute-done.18.refs_2_, ...), custom_call_target="tpu_custom_call" | custom-call | flops 1024 | bytes 1024 | tf_op jit(solution)/shard_map/pallas_call | solution.py:329
  262.7 6.8 %shard_map.117 = (f32[256,512]{1,0:T(8,128)S(1)}, bf16[256,512]{1,0:T(8,128)(2,1)}) custom-call(s32[1]{0:T(128)} %bitcast.32.flag, bf16[160,7168]{1,0:T(8,128)(2,1)} %collective-permute-done.8.refs_8_.refs_0_, bf16[96,7168]{1,0:T(8,128)(2,1)} %collective-permute-done.14.refs_9_.refs_1_, bf16[160,7168]{1,0:T(8,128)(2,1)} %collective-permute-done.4.refs_2_.refs_4_, ...), custom_call_target="tpu_custom_call" | custom-call | flops 1024 | bytes 1024 | tf_op jit(solution)/shard_map/pallas_call | solution.py:168
  269.8 1.5 collective-permute-start.29
  271.4 1.3 shard_map.120
  272.7 0.9 collective-permute-start.31
  273.9 2.3 collective-permute-start.33
  276.2 1.3 collective-permute-done.29.refs_0_
  277.5 2.1 shard_map.118
  279.8 1.2 slice.94
  281.0 4.5 %collective-permute-done.31.refs_1_ = f32[2,32,1792]{2,1,0:T(8,128)S(1)} collective-permute-done((f32[2,32,1792]{2,1,0:T(8,128)}, f32[2,32,1792]{2,1,0:T(8,128)S(1)}, u32[]{:S(2)}, u32[]{:S(2)}) %collective-permute-start.31) | collective-permute-done | bytes 458784 | tf_op jit(solution)/shard_map/ppermute | solution.py:441
  285.5 1.7 collective-permute-done.32.refs_2_
  287.2 10.5 %collective-permute-done.33.refs_3_ = f32[2,32,1792]{2,1,0:T(8,128)S(1)} collective-permute-done((f32[2,32,1792]{2,1,0:T(8,128)}, f32[2,32,1792]{2,1,0:T(8,128)S(1)}, u32[]{:S(2)}, u32[]{:S(2)}) %collective-permute-start.33) | collective-permute-done | bytes 458784 | tf_op jit(solution)/shard_map/ppermute | solution.py:441
  297.7 2.6 shard_map.121
  300.9 2.1 shard_map.119
  (99 shorter events, 10.1 us)
Async XLA Ops:
  0.6 3.1 %copy-start = (bf16[256,512]{1,0:T(8,128)(2,1)S(1)}, bf16[256,512]{1,0:T(8,128)(2,1)}, u32[]{:S(2)}) copy-start(bf16[256,512]{1,0:T(8,128)(2,1)} %param.13) | copy-start | bytes 786436
  0.6 21.3 %collective-permute-start = (bf16[256,7168]{1,0:T(8,128)(2,1)}, bf16[256,7168]{1,0:T(8,128)(2,1)}, u32[]{:S(2)}, u32[]{:S(2)}) collective-permute-start(bf16[256,7168]{1,0:T(8,128)(2,1)} %refs_2_.5), channel_id=1, source_target_pairs={{0,2},{2,0},{4,6},{6,4},{8,10},{10,8},{12,14},{14,12},{16,18},{18,... | collective-permute-start | bytes 11010056 | tf_op jit(solution)/shard_map/ppermute | solution.py:441
  1.2 112.9 %collective-permute-start.3 = (bf16[256,7168]{1,0:T(8,128)(2,1)}, bf16[256,7168]{1,0:T(8,128)(2,1)}, u32[]{:S(2)}, u32[]{:S(2)}) collective-permute-start(bf16[256,7168]{1,0:T(8,128)(2,1)} %refs_4_.1), channel_id=1, source_target_pairs={{0,4},{2,6},{4,0},{6,2},{8,12},{10,14},{12,8},{14,10},{16,20},{18,... | collective-permute-start | bytes 11010056 | tf_op jit(solution)/shard_map/ppermute | solution.py:441
  5.1 5.1 %copy-start.4 = (bf16[256,7168]{1,0:T(8,128)(2,1)S(1)}, bf16[256,7168]{1,0:T(8,128)(2,1)}, u32[]{:S(2)}) copy-start(bf16[256,7168]{1,0:T(8,128)(2,1)} %refs_2_.5) | copy-start | bytes 11010052
  5.1 10.6 %collective-permute-start.5 = (f32[2,4,32,512]{3,2,1,0:T(8,128)S(1)}, f32[2,4,32,512]{3,2,1,0:T(8,128)S(1)}, u32[]{:S(2)}, u32[]{:S(2)}) collective-permute-start(f32[2,4,32,512]{3,2,1,0:T(8,128)S(1)} %select_bitcast_fusion), channel_id=1, source_target_pairs={{0,2},{2,0},{4,6},{6,4},{8,10},{10,8},{12,14},{14,12},{16,18},{18,... | collective-permute-start | bytes 1572872 | tf_op jit(solution)/shard_map/ppermute | solution.py:441
  8.7 5.7 %copy-start.20 = (bf16[256,512]{1,0:T(8,128)(2,1)S(1)}, bf16[256,512]{1,0:T(8,128)(2,1)}, u32[]{:S(2)}) copy-start(bf16[256,512]{1,0:T(8,128)(2,1)} %param.9) | copy-start | bytes 786436
  8.7 100.0 %collective-permute-start.2 = (bf16[160,7168]{1,0:T(8,128)(2,1)}, bf16[160,7168]{1,0:T(8,128)(2,1)}, u32[]{:S(2)}, u32[]{:S(2)}) collective-permute-start(bf16[160,7168]{1,0:T(8,128)(2,1)} %slice.72), channel_id=1, source_target_pairs={{0,8},{2,10},{4,12},{6,14},{8,0},{10,2},{12,4},{14,6},{16,24},{18,... | collective-permute-start | bytes 6881288 | tf_op jit(solution)/shard_map/ppermute | solution.py:441
  11.8 102.3 %collective-permute-start.4 = (bf16[160,7168]{1,0:T(8,128)(2,1)}, bf16[160,7168]{1,0:T(8,128)(2,1)}, u32[]{:S(2)}, u32[]{:S(2)}) collective-permute-start(bf16[160,7168]{1,0:T(8,128)(2,1)} %slice.73), channel_id=1, source_target_pairs={{0,16},{2,18},{4,20},{6,22},{8,24},{10,26},{12,28},{14,30},{16,0},... | collective-permute-start | bytes 6881288 | tf_op jit(solution)/shard_map/ppermute | solution.py:441
  16.1 73.7 %collective-permute-start.6 = (f32[2,2,32,512]{3,2,1,0:T(8,128)S(1)}, f32[2,2,32,512]{3,2,1,0:T(8,128)S(1)}, u32[]{:S(2)}, u32[]{:S(2)}) collective-permute-start(f32[2,2,32,512]{3,2,1,0:T(8,128)S(1)} %pad_maximum_fusion.1), channel_id=1, source_target_pairs={{0,4},{2,6},{4,0},{6,2},{8,12},{10,14},{12,8},{14,10},{16,20},{18,... | collective-permute-start | bytes 786440 | tf_op jit(solution)/shard_map/ppermute | solution.py:441
  16.8 5.2 %copy-start.11 = (f32[32,7168]{1,0:T(8,128)S(1)}, f32[32,7168]{1,0:T(8,128)}, u32[]{:S(2)}) copy-start(f32[32,7168]{1,0:T(8,128)} %first) | copy-start | bytes 2752516
  16.8 5.2 %copy-start.12 = (f32[32,7168]{1,0:T(8,128)S(1)}, f32[32,7168]{1,0:T(8,128)}, u32[]{:S(2)}) copy-start(f32[32,7168]{1,0:T(8,128)} %second) | copy-start | bytes 2752516
  22.6 93.0 %collective-permute-start.1 = (bf16[2,64,1792]{2,1,0:T(8,128)(2,1)S(1)}, bf16[2,64,1792]{2,1,0:T(8,128)(2,1)S(1)}, u32[]{:S(2)}, u32[]{:S(2)}) collective-permute-start(bf16[2,64,1792]{2,1,0:T(8,128)(2,1)S(1)} %shard_map.103), channel_id=1, source_target_pairs={{0,4},{2,6},{4,0},{6,2},{8,12},{10,14},{12,8},{14,10},{16,20},{18,... | collective-permute-start | bytes 1376264 | tf_op jit(solution)/shard_map/ppermute | solution.py:441
  114.7 80.2 %collective-permute-start.8 = (bf16[160,7168]{1,0:T(8,128)(2,1)}, bf16[160,7168]{1,0:T(8,128)(2,1)}, u32[]{:S(2)}, u32[]{:S(2)}) collective-permute-start(bf16[160,7168]{1,0:T(8,128)(2,1)} %collective-permute-done.2.refs_0_.refs_6_), channel_id=1, source_target_pairs={{0,4},{2,6},{4,0},{6,2},{8,12},{10,14},{12,8},{14,10},{16,20},{18,... | collective-permute-start | bytes 6881288 | tf_op jit(solution)/shard_map/ppermute | solution.py:441
  115.6 36.2 %collective-permute-start.11 = (f32[1,2,32,512]{3,2,1,0:T(8,128)}, f32[1,2,32,512]{3,2,1,0:T(8,128)}, u32[]{:S(2)}, u32[]{:S(2)}) collective-permute-start(f32[1,2,32,512]{3,2,1,0:T(8,128)} %bitcast.28), channel_id=1, source_target_pairs={{0,8},{2,10},{4,12},{6,14},{8,0},{10,2},{12,4},{14,6},{16,24},{18,... | collective-permute-start | bytes 393224 | tf_op jit(solution)/shard_map/ppermute | solution.py:441
  116.4 0.8 copy-start.9
  117.2 44.4 %collective-permute-start.10 = (bf16[2,64,1792]{2,1,0:T(8,128)(2,1)}, bf16[2,64,1792]{2,1,0:T(8,128)(2,1)}, u32[]{:S(2)}, u32[]{:S(2)}) collective-permute-start(bf16[2,64,1792]{2,1,0:T(8,128)(2,1)} %shard_map.104), channel_id=1, source_target_pairs={{0,8},{2,10},{4,12},{6,14},{8,0},{10,2},{12,4},{14,6},{16,24},{18,... | collective-permute-start | bytes 1376264 | tf_op jit(solution)/shard_map/ppermute | solution.py:441
  119.2 75.7 %collective-permute-start.7 = (bf16[96,7168]{1,0:T(8,128)(2,1)}, bf16[96,7168]{1,0:T(8,128)(2,1)}, u32[]{:S(2)}, u32[]{:S(2)}) collective-permute-start(bf16[96,7168]{1,0:T(8,128)(2,1)} %slice.82), channel_id=1, source_target_pairs={{0,8},{2,10},{4,12},{6,14},{8,0},{10,2},{12,4},{14,6},{16,24},{18,... | collective-permute-start | bytes 4128776 | tf_op jit(solution)/shard_map/ppermute | solution.py:441
  119.2 75.7 %collective-permute-start.9 = (bf16[96,7168]{1,0:T(8,128)(2,1)}, bf16[96,7168]{1,0:T(8,128)(2,1)}, u32[]{:S(2)}, u32[]{:S(2)}) collective-permute-start(bf16[96,7168]{1,0:T(8,128)(2,1)} %slice.83), channel_id=1, source_target_pairs={{0,16},{2,18},{4,20},{6,22},{8,24},{10,26},{12,28},{14,30},{16,0},... | collective-permute-start | bytes 4128776 | tf_op jit(solution)/shard_map/ppermute | solution.py:441
  123.5 2.0 copy-start.2
  125.6 2.0 copy-start.5
  127.6 24.2 %copy-start.19 = (f32[2,32,512]{2,1,0:T(8,128)S(1)}, f32[2,32,512]{2,1,0:T(8,128)}, u32[]{:S(2)}) copy-start(f32[2,32,512]{2,1,0:T(8,128)} %get-tuple-element.151) | copy-start | bytes 393220
  127.6 34.7 %copy-start.7 = (bf16[256,2,2,4,32]{0,4,3,2,1:T(8,128)(2,1)S(1)}, bf16[256,2,2,4,32]{0,4,3,2,1:T(8,128)(2,1)}, u32[]{:S(2)}) copy-start(bf16[256,2,2,4,32]{0,4,3,2,1:T(8,128)(2,1)} %pad_maximum_fusion.2) | copy-start | bytes 786436
  127.6 35.7 %copy-start.10 = (bf16[2,64,1792]{2,1,0:T(8,128)(2,1)S(1)}, bf16[2,64,1792]{2,1,0:T(8,128)(2,1)}, u32[]{:S(2)}) copy-start(bf16[2,64,1792]{2,1,0:T(8,128)(2,1)} %copy-done.9) | copy-start | bytes 1376260
  161.6 31.3 %collective-permute-start.13 = (f32[32,512]{1,0:T(8,128)S(1)}, f32[32,512]{1,0:T(8,128)S(1)}, u32[]{:S(2)}, u32[]{:S(2)}) collective-permute-start(f32[32,512]{1,0:T(8,128)S(1)} %select_bitcast_fusion.1), channel_id=1, source_target_pairs={{0,16},{2,18},{4,20},{6,22},{8,24},{10,26},{12,28},{14,30},{16,0},... | collective-permute-start | bytes 196616 | tf_op jit(solution)/shard_map/ppermute | solution.py:441
  162.3 31.4 %collective-permute-start.12 = (bf16[512,256]{1,0:T(8,128)(2,1)S(1)}, bf16[512,256]{1,0:T(8,128)(2,1)}, u32[]{:S(2)}, u32[]{:S(2)}) collective-permute-start(bf16[512,256]{1,0:T(8,128)(2,1)S(1)} %bitcast.133), channel_id=1, source_target_pairs={{0,4},{2,6},{4,0},{6,2},{8,12},{10,14},{12,8},{14,10},{16,20},{18,... | collective-permute-start | bytes 786440 | tf_op jit(solution)/shard_map/ppermute | solution.py:441
  194.9 6.8 %collective-permute-start.15 = (bf16[160,7168]{1,0:T(8,128)(2,1)}, bf16[160,7168]{1,0:T(8,128)(2,1)}, u32[]{:S(2)}, u32[]{:S(2)}) collective-permute-start(bf16[160,7168]{1,0:T(8,128)(2,1)} %collective-permute-done.4.refs_2_.refs_4_), channel_id=1, source_target_pairs={{0,2},{2,0},{4,6},{6,4},{8,10},{10,8},{12,14},{14,12},{16,18},{18,... | collective-permute-start | bytes 6881288 | tf_op jit(solution)/shard_map/ppermute | solution.py:441
  195.0 6.7 %collective-permute-start.16 = (bf16[96,7168]{1,0:T(8,128)(2,1)}, bf16[96,7168]{1,0:T(8,128)(2,1)}, u32[]{:S(2)}, u32[]{:S(2)}) collective-permute-start(bf16[96,7168]{1,0:T(8,128)(2,1)} %collective-permute-done.9.refs_3_.refs_5_), channel_id=1, source_target_pairs={{0,2},{2,0},{4,6},{6,4},{8,10},{10,8},{12,14},{14,12},{16,18},{18,... | collective-permute-start | bytes 4128776 | tf_op jit(solution)/shard_map/ppermute | solution.py:441
  195.5 32.5 %collective-permute-start.14 = (bf16[96,7168]{1,0:T(8,128)(2,1)}, bf16[96,7168]{1,0:T(8,128)(2,1)}, u32[]{:S(2)}, u32[]{:S(2)}) collective-permute-start(bf16[96,7168]{1,0:T(8,128)(2,1)} %collective-permute-done.7.refs_1_.refs_7_), channel_id=1, source_target_pairs={{0,4},{2,6},{4,0},{6,2},{8,12},{10,14},{12,8},{14,10},{16,20},{18,... | collective-permute-start | bytes 4128776 | tf_op jit(solution)/shard_map/ppermute | solution.py:441
  196.0 43.4 %collective-permute-start.18 = (bf16[2,128,1792]{2,1,0:T(8,128)(2,1)}, bf16[2,128,1792]{2,1,0:T(8,128)(2,1)}, u32[]{:S(2)}, u32[]{:S(2)}) collective-permute-start(bf16[2,128,1792]{2,1,0:T(8,128)(2,1)} %shard_map.107.refs_0_), channel_id=1, source_target_pairs={{0,16},{2,18},{4,20},{6,22},{8,24},{10,26},{12,28},{14,30},{16,0},... | collective-permute-start | bytes 2752520 | tf_op jit(solution)/shard_map/ppermute | solution.py:441
  196.0 1.3 copy-start.8
  198.3 29.6 %collective-permute-start.17 = (bf16[1024,256]{1,0:T(8,128)(2,1)S(1)}, bf16[1024,256]{1,0:T(8,128)(2,1)S(1)}, u32[]{:S(2)}, u32[]{:S(2)}) collective-permute-start(bf16[1024,256]{1,0:T(8,128)(2,1)S(1)} %pad_maximum_fusion), channel_id=1, source_target_pairs={{0,8},{2,10},{4,12},{6,14},{8,0},{10,2},{12,4},{14,6},{16,24},{18,... | collective-permute-start | bytes 1572872 | tf_op jit(solution)/shard_map/ppermute | solution.py:441
  201.7 2.0 copy-start.3
  211.5 28.0 %collective-permute-start.20 = (bf16[512,512]{1,0:T(8,128)(2,1)S(1)}, bf16[512,512]{1,0:T(8,128)(2,1)S(1)}, u32[]{:S(2)}, u32[]{:S(2)}) collective-permute-start(bf16[512,512]{1,0:T(8,128)(2,1)S(1)} %get-tuple-element.180), channel_id=1, source_target_pairs={{0,1},{1,0},{2,3},{3,2},{4,5},{5,4},{6,7},{7,6},{8,9},{9,8},{10,11... | collective-permute-start | bytes 1572872 | tf_op jit(solution)/shard_map/ppermute | solution.py:444
  213.0 14.9 %copy-start.18 = (f32[32,512]{1,0:T(8,128)S(1)}, f32[32,512]{1,0:T(8,128)}, u32[]{:S(2)}) copy-start(f32[32,512]{1,0:T(8,128)} %bitcast_add_fusion.1) | copy-start | bytes 196612
  222.2 17.3 %collective-permute-start.21 = (bf16[256,512]{1,0:T(8,128)(2,1)S(1)}, bf16[256,512]{1,0:T(8,128)(2,1)S(1)}, u32[]{:S(2)}, u32[]{:S(2)}) collective-permute-start(bf16[256,512]{1,0:T(8,128)(2,1)S(1)} %get-tuple-element.184), channel_id=1, source_target_pairs={{0,1},{1,0},{2,3},{3,2},{4,5},{5,4},{6,7},{7,6},{8,9},{9,8},{10,11... | collective-permute-start | bytes 786440 | tf_op jit(solution)/shard_map/ppermute | solution.py:444
  228.0 11.5 %collective-permute-start.19 = (f32[32,512]{1,0:T(8,128)S(1)}, f32[32,512]{1,0:T(8,128)S(1)}, u32[]{:S(2)}, u32[]{:S(2)}) collective-permute-start(f32[32,512]{1,0:T(8,128)S(1)} %copy-done.18), channel_id=1, source_target_pairs={{0,8},{2,10},{4,12},{6,14},{8,0},{10,2},{12,4},{14,6},{16,24},{18,... | collective-permute-start | bytes 196616 | tf_op jit(solution)/shard_map/ppermute | solution.py:441
  228.0 4.8 %copy-start.6 = (bf16[256,7168]{1,0:T(8,128)(2,1)S(1)}, bf16[256,7168]{1,0:T(8,128)(2,1)}, u32[]{:S(2)}) copy-start(bf16[256,7168]{1,0:T(8,128)(2,1)} %refs_2_.5) | copy-start | bytes 11010052
  239.4 5.7 %collective-permute-start.22 = (f32[256,1792]{1,0:T(8,128)S(1)}, f32[256,1792]{1,0:T(8,128)S(1)}, u32[]{:S(2)}, u32[]{:S(2)}) collective-permute-start(f32[256,1792]{1,0:T(8,128)S(1)} %get-tuple-element.202), channel_id=1, source_target_pairs={{0,2},{2,0},{4,6},{6,4},{8,10},{10,8},{12,14},{14,12},{16,18},{18,... | collective-permute-start | bytes 5505032 | tf_op jit(solution)/shard_map/ppermute | solution.py:441
  239.5 16.2 %collective-permute-start.27 = (bf16[2,128,1792]{2,1,0:T(8,128)(2,1)}, bf16[2,128,1792]{2,1,0:T(8,128)(2,1)S(1)}, u32[]{:S(2)}, u32[]{:S(2)}) collective-permute-start(bf16[2,128,1792]{2,1,0:T(8,128)(2,1)} %shard_map.107.refs_0_), channel_id=1, source_target_pairs={{0,2},{2,0},{4,6},{6,4},{8,10},{10,8},{12,14},{14,12},{16,18},{18,... | collective-permute-start | bytes 2752520 | tf_op jit(solution)/shard_map/ppermute | solution.py:441
  240.0 15.7 %collective-permute-start.28 = (bf16[2,128,1792]{2,1,0:T(8,128)(2,1)}, bf16[2,128,1792]{2,1,0:T(8,128)(2,1)S(1)}, u32[]{:S(2)}, u32[]{:S(2)}) collective-permute-start(bf16[2,128,1792]{2,1,0:T(8,128)(2,1)} %collective-permute-done.18.refs_2_), channel_id=1, source_target_pairs={{0,2},{2,0},{4,6},{6,4},{8,10},{10,8},{12,14},{14,12},{16,18},{18,... | collective-permute-start | bytes 2752520 | tf_op jit(solution)/shard_map/ppermute | solution.py:441
  245.5 9.5 %copy-start.17 = (f32[512,512]{1,0:T(8,128)S(1)}, f32[512,512]{1,0:T(8,128)}, u32[]{:S(2)}) copy-start(f32[512,512]{1,0:T(8,128)} %fusion.16) | copy-start | bytes 3145732
  245.5 5.6 %collective-permute-start.24 = (f32[2,32,512]{2,1,0:T(8,128)S(1)}, f32[2,32,512]{2,1,0:T(8,128)S(1)}, u32[]{:S(2)}, u32[]{:S(2)}) collective-permute-start(f32[2,32,512]{2,1,0:T(8,128)S(1)} %pad_maximum_fusion.4), channel_id=1, source_target_pairs={{0,4},{2,6},{4,0},{6,2},{8,12},{10,14},{12,8},{14,10},{16,20},{18,... | collective-permute-start | bytes 393224 | tf_op jit(solution)/shard_map/ppermute | solution.py:441
  246.8 23.0 %collective-permute-start.23 = (f16[128,1792]{1,0:T(8,128)(2,1)S(1)}, f16[128,1792]{1,0:T(8,128)(2,1)S(1)}, u32[]{:S(2)}, u32[]{:S(2)}) collective-permute-start(f16[128,1792]{1,0:T(8,128)(2,1)S(1)} %get-tuple-element.206), channel_id=1, source_target_pairs={{0,16},{2,18},{4,20},{6,22},{8,24},{10,26},{12,28},{14,30},{16,0},... | collective-permute-start | bytes 1376264 | tf_op jit(solution)/shard_map/ppermute | solution.py:441
  251.6 17.9 %collective-permute-start.26 = (bf16[256,512]{1,0:T(8,128)(2,1)S(1)}, bf16[256,512]{1,0:T(8,128)(2,1)S(1)}, u32[]{:S(2)}, u32[]{:S(2)}) collective-permute-start(bf16[256,512]{1,0:T(8,128)(2,1)S(1)} %shard_map.115), channel_id=1, source_target_pairs={{0,8},{2,10},{4,12},{6,14},{8,0},{10,2},{12,4},{14,6},{16,24},{18,... | collective-permute-start | bytes 786440 | tf_op jit(solution)/shard_map/ppermute | solution.py:441
  253.2 16.3 %collective-permute-start.25 = (bf16[256,512]{1,0:T(8,128)(2,1)S(1)}, bf16[256,512]{1,0:T(8,128)(2,1)S(1)}, u32[]{:S(2)}, u32[]{:S(2)}) collective-permute-start(bf16[256,512]{1,0:T(8,128)(2,1)S(1)} %get-tuple-element.216), channel_id=1, source_target_pairs={{0,4},{2,6},{4,0},{6,2},{8,12},{10,14},{12,8},{14,10},{16,20},{18,... | collective-permute-start | bytes 786440 | tf_op jit(solution)/shard_map/ppermute | solution.py:441
  269.4 3.2 %copy-start.13 = (bf16[256,512]{1,0:T(8,128)(2,1)}, bf16[256,512]{1,0:T(8,128)(2,1)S(1)}, u32[]{:S(2)}) copy-start(bf16[256,512]{1,0:T(8,128)(2,1)S(1)} %collective-permute-done.26.refs_2_) | copy-start | bytes 786436
  269.5 3.2 %copy-start.15 = (bf16[256,512]{1,0:T(8,128)(2,1)}, bf16[256,512]{1,0:T(8,128)(2,1)S(1)}, u32[]{:S(2)}) copy-start(bf16[256,512]{1,0:T(8,128)(2,1)S(1)} %collective-permute-done.25.refs_1_) | copy-start | bytes 786436
  269.8 7.7 %collective-permute-start.29 = (bf16[256,512]{1,0:T(8,128)(2,1)}, bf16[256,512]{1,0:T(8,128)(2,1)}, u32[]{:S(2)}, u32[]{:S(2)}) collective-permute-start(bf16[256,512]{1,0:T(8,128)(2,1)} %get-tuple-element.236), channel_id=1, source_target_pairs={{0,1},{1,0},{2,3},{3,2},{4,5},{5,4},{6,7},{7,6},{8,9},{9,8},{10,11... | collective-permute-start | bytes 786440 | tf_op jit(solution)/shard_map/ppermute | solution.py:444
  272.7 28.2 %copy-start.14 = (bf16[256,512]{1,0:T(8,128)(2,1)S(1)}, bf16[256,512]{1,0:T(8,128)(2,1)}, u32[]{:S(2)}) copy-start(bf16[256,512]{1,0:T(8,128)(2,1)} %copy-done.13) | copy-start | bytes 786436
  272.7 28.2 %copy-start.16 = (bf16[256,512]{1,0:T(8,128)(2,1)S(1)}, bf16[256,512]{1,0:T(8,128)(2,1)}, u32[]{:S(2)}) copy-start(bf16[256,512]{1,0:T(8,128)(2,1)} %copy-done.15) | copy-start | bytes 786436
  272.7 12.8 %collective-permute-start.31 = (f32[2,32,1792]{2,1,0:T(8,128)}, f32[2,32,1792]{2,1,0:T(8,128)S(1)}, u32[]{:S(2)}, u32[]{:S(2)}) collective-permute-start(f32[2,32,1792]{2,1,0:T(8,128)} %get-tuple-element.244), channel_id=1, source_target_pairs={{0,4},{2,6},{4,0},{6,2},{8,12},{10,14},{12,8},{14,10},{16,20},{18,... | collective-permute-start | bytes 1376264 | tf_op jit(solution)/shard_map/ppermute | solution.py:441
  273.5 13.7 %collective-permute-start.32 = (f32[2,32,1792]{2,1,0:T(8,128)}, f32[2,32,1792]{2,1,0:T(8,128)S(1)}, u32[]{:S(2)}, u32[]{:S(2)}) collective-permute-start(f32[2,32,1792]{2,1,0:T(8,128)} %get-tuple-element.245), channel_id=1, source_target_pairs={{0,8},{2,10},{4,12},{6,14},{8,0},{10,2},{12,4},{14,6},{16,24},{18,... | collective-permute-start | bytes 1376264 | tf_op jit(solution)/shard_map/ppermute | solution.py:441
  273.9 23.8 %collective-permute-start.33 = (f32[2,32,1792]{2,1,0:T(8,128)}, f32[2,32,1792]{2,1,0:T(8,128)S(1)}, u32[]{:S(2)}, u32[]{:S(2)}) collective-permute-start(f32[2,32,1792]{2,1,0:T(8,128)} %get-tuple-element.246), channel_id=1, source_target_pairs={{0,12},{2,14},{4,8},{6,10},{8,4},{10,6},{12,0},{14,2},{16,28},{18,... | collective-permute-start | bytes 1376264 | tf_op jit(solution)/shard_map/ppermute | solution.py:441
  279.6 21.3 %collective-permute-start.30 = (bf16[256,512]{1,0:T(8,128)(2,1)}, bf16[256,512]{1,0:T(8,128)(2,1)S(1)}, u32[]{:S(2)}, u32[]{:S(2)}) collective-permute-start(bf16[256,512]{1,0:T(8,128)(2,1)} %shard_map.118), channel_id=1, source_target_pairs={{0,12},{2,14},{4,8},{6,10},{8,4},{10,6},{12,0},{14,2},{16,28},{18,... | collective-permute-start | bytes 786440 | tf_op jit(solution)/shard_map/ppermute | solution.py:441
  297.7 5.3 %copy-start.1 = (bf16[256,512]{1,0:T(8,128)(2,1)S(1)}, bf16[256,512]{1,0:T(8,128)(2,1)}, u32[]{:S(2)}) copy-start(bf16[256,512]{1,0:T(8,128)(2,1)} %param.13) | copy-start | bytes 786436
